TPU v7x, 256 devices: a whole 4x4x8 slice. The times are simulated.
256 devices in a mesh: gx: 16 (over z_hi, y), yz: 16 (over z_lo, x, core).
Axes of the slice: x: 4, y: 4, z: 8 (z_hi: 4, z_lo: 2; z = z_hi * 2 + z_lo), core: 2. Of those that a mesh axis runs over, the one named last changes fastest.
Arguments:
- solvent_vel: float32 [3, 512, 512, 2, 128], P(None, 'gx', 'yz'), may hold values from -6 to 6
- occupancy: int32 [512, 512, 128], P('gx', 'yz'), may hold values from 0 to 2
- grid_shift: int32 [3], replicated, may hold values from 1 to 3
- axis_index: int32 [128, 128, 64], P('gx', 'yz'), may hold values from 0 to 63
- colloid_pos: float32 [3, 16, 16, 128], P(None, 'gx', 'yz'), may hold values from 0 to 64, as said below
- colloid_vel: float32 [3, 16, 16, 128], P(None, 'gx', 'yz'), may hold values from -6 to 6
- colloid_mass: float32 [16, 16, 128], P('gx', 'yz'), may hold values from 2 to 20
- colloid_count: int32 [16, 16], P('gx', 'yz'), may hold values from 21 to 128, as said below
Outputs:
- solvent_out: float32 [3, 512, 512, 2, 128], P(None, 'gx', 'yz')
- colloid_pos_out: float32 [3, 16, 16, 128], P(None, 'gx', 'yz')
- colloid_vel_out: float32 [3, 16, 16, 128], P(None, 'gx', 'yz')
Inputs may be any that keep to these rules, and one draw needn't show every extreme that they name: `colloid_pos`: component 0 lies in [0, 8), component 1 in [0, 8), component 2 in [0, 64). `colloid_count`: some device holds 128 live colloids in every draw.
All inputs are finite; a program needn't handle non-finite values.
Results may differ from a plain program's by a relative error of at most 0.0003.
Values sent between devices are 32-bit elements; how exact they have to be, the bound alone decides.
No kernel may reach another device: no remote copies, remote signals or barrier semaphores. Data moves between devices by JAX's collectives and lax.ppermute only.
A program may use at most 320 MiB of HBM per device.

v0:
```python
import math

import jax
import jax.numpy as jnp
from jax import lax
from jax.experimental import pallas as pl
from jax.experimental.pallas import tpu as pltpu
from jax.sharding import PartitionSpec as P

CX = 8
CY = 8
CZ = 64
SUB = 4
SUBSTEPS = 4
DIRECTIONS = 64
FX = 32
FY = 32
FZ = 128
KX = CX + 1
JY = CY + 1
JP = 16
ROWS = KX * JP

turn_angle = 130.0 * math.pi / 180.0
cos_angle = math.cos(turn_angle)
sin_angle = math.sin(turn_angle)
golden = math.pi * (3.0 - math.sqrt(5.0))
cutoff = 1.5
stiffness = 20.0
timestep = 0.05
fill_mass = 16.0

SMEM = pltpu.SMEM
VMEM = pltpu.VMEM
HBM = pl.BlockSpec(memory_space=pltpu.HBM)
IN_VMEM = pl.BlockSpec(memory_space=VMEM)
IN_SMEM = pl.BlockSpec(memory_space=SMEM)
DMA = pltpu.SemaphoreType.DMA
NT = (((1,), (1,)), ((), ()))
NN = (((1,), (0,)), ((), ()))
STATE = 2 * ROWS
NUMBERS = STATE + 16
BASE = NUMBERS + ROWS
SMALL_LIMIT = 8 * 1024 * 1024
TURN_LIMIT = 52 * 1024 * 1024


def shifted(value, axis, steps):
    count = lax.axis_size(axis)
    return lax.ppermute(value, axis, [(i, (i + steps) % count) for i in range(count)])


def struct(*shape):
    return jax.ShapeDtypeStruct(shape, jnp.float32)


def exact_dot(left, right, dims):
    right = right.astype(jnp.bfloat16)
    total = None
    for part in range(3):
        piece = left.astype(jnp.bfloat16)
        term = lax.dot_general(piece, right, dims, preferred_element_type=jnp.float32)
        total = term if total is None else total + term
        if part < 2:
            left = left - piece.astype(jnp.float32)
    return total


def colloid_cells(pos, sx, sy, sz):
    cell_x = jnp.clip(jnp.floor(pos[0] * SUB).astype(jnp.int32), 0, FX - 1)
    cell_y = jnp.clip(jnp.floor(pos[1] * SUB).astype(jnp.int32), 0, FY - 1)
    cell_z = jnp.clip(jnp.floor(pos[2] * 2.0).astype(jnp.int32), 0, FZ - 1)
    return ((cell_x + sx) >> 2, (cell_y + sy) >> 2, ((cell_z + sz) & (FZ - 1)) >> 1)


def live_row(count):
    return lax.broadcasted_iota(jnp.int32, (1, FZ), 1) < count


def store_twice(occ, twice, q):
    slots = occ[SUB * q : SUB * q + SUB].reshape(SUB * FY, FZ).astype(jnp.float32)
    base = 2 * SUB * FY * q
    twice[pl.ds(base, SUB * FY, 2), :] = slots
    twice[pl.ds(base + 1, SUB * FY, 2), :] = slots


def sums_kernel(
    shift_at, count_at, v_at, occ_at, axis_at, pos_at, vel_at, mass_at,
    base, up, down,
    shift, count, v, occ, axis, pos, vel, mass, twice, partial, sem, vsem, osem,
):
    small = [
        pltpu.make_async_copy(a, b, sem.at[i])
        for i, (a, b) in enumerate(
            [
                (shift_at, shift),
                (count_at, count),
                (axis_at, axis),
                (pos_at, pos),
                (vel_at, vel),
                (mass_at, mass),
            ]
        )
    ]
    large = []
    for q in range(CX):
        part = pl.ds(SUB * q, SUB)
        large.append(pltpu.make_async_copy(occ_at.at[part], occ.at[part], osem.at[q]))
        large.append(pltpu.make_async_copy(v_at.at[:, part], v.at[:, part], vsem.at[q]))
    for copy in small[:2] + large[:2] + small[2:] + large[2:]:
        copy.start()
    for copy in small[:2]:
        copy.wait()
    sx, sy, sz = shift[0], shift[1], shift[2]
    row = lax.broadcasted_iota(jnp.int32, (2 * FY, FZ), 0)
    slot = (row & 1).astype(jnp.float32)
    low = (row[:8] < 8 - 2 * sy)[None]

    def plane(x, acc):
        live = twice[pl.ds(pl.multiple_of(x * 2 * FY, 2 * FY), 2 * FY), :] > slot
        masked = [jnp.where(live, v[c, x], 0.0) for c in range(3)] + [jnp.where(live, 1.0, 0.0)]
        return tuple(a + m for a, m in zip(acc, masked))

    zero = jnp.zeros((2 * FY, FZ), jnp.float32)
    blank = jnp.zeros((1, 8, FZ), jnp.float32)
    partial[:, :, 8:JP, :] = jnp.zeros((4, KX, JP - 8, FZ), jnp.float32)

    for k in range(KX):
        if k < CX:
            large[2 * k].wait()
            store_twice(occ, twice, k)
            large[2 * k + 1].wait()
        acc = (zero,) * 4
        if k == 0:
            acc = lax.fori_loop(0, SUB - sx, plane, acc)
        elif k == CX:
            acc = lax.fori_loop(FX - sx, FX, plane, acc)
        else:
            for j in range(SUB):
                acc = plane(k * SUB - sx + j, acc)
        for c in range(4):
            parts = acc[c].reshape(CY, 8, FZ)
            picked = jnp.where(
                low, jnp.concatenate([parts, blank]), jnp.concatenate([blank, parts])
            )
            partial[c, k, 0:JY, :] = jnp.sum(picked, axis=1)

    for copy in small[2:]:
        copy.wait()
    kx, jy, lz = colloid_cells(pos, sx, sy, sz)
    alive = live_row(count[0, 0]).astype(jnp.float32)
    weight = mass[0] * alive
    hit = lax.broadcasted_iota(jnp.int32, (ROWS, FZ), 0) == kx * JP + jy
    carried = [jnp.where(hit, vel[c] * weight, 0.0) for c in range(3)]
    carried.append(jnp.where(hit, weight, 0.0))
    target = lax.broadcasted_iota(jnp.int32, (CZ, FZ), 0)
    layer = lax.broadcasted_iota(jnp.int32, (CZ, FZ), 1)
    to_cell = (((layer + sz) & (FZ - 1)) >> 1 == target).astype(jnp.float32)
    to_place = (target == lz).astype(jnp.float32)
    one = jnp.concatenate([to_cell, to_place], axis=1)
    none = jnp.zeros_like(one)
    right = jnp.concatenate(
        [jnp.concatenate([one, none], axis=1), jnp.concatenate([none, one], axis=1)], axis=0
    )
    for p in range(2):
        left = jnp.concatenate(
            [
                partial[2 * p].reshape(ROWS, FZ),
                carried[2 * p],
                partial[2 * p + 1].reshape(ROWS, FZ),
                carried[2 * p + 1],
            ],
            axis=1,
        )
        total = exact_dot(left, right, NT)
        base[p * ROWS : p * ROWS + ROWS] = total
        last = CX * JP
        down[8 * p : 8 * p + 8] = total[0:8]
        down[16 + p : 17 + p] = total[8:9]
        up[8 * p : 8 * p + 8] = total[last : last + 8]
        up[16 + p : 17 + p] = total[last + 8 : last + 9]
    for packet in (up, down):
        for c in range(3):
            packet[18 + c : 19 + c] = pos[c]
        packet[21:22] = alive
        packet[22:24] = jnp.zeros((2, FZ), jnp.float32)
    for c in range(3):
        base[STATE + c : STATE + c + 1] = pos[c]
        base[STATE + 3 + c : STATE + 4 + c] = vel[c]
    base[STATE + 6 : STATE + 7] = mass[0]
    base[STATE + 7 : STATE + 8] = alive
    base[STATE + 8 : STATE + 9] = (kx * JP + jy).astype(jnp.float32)
    base[STATE + 9 : STATE + 10] = lz.astype(jnp.float32)
    base[STATE + 10 : STATE + 16] = jnp.zeros((6, FZ), jnp.float32)
    base[NUMBERS : NUMBERS + ROWS] = jnp.zeros((ROWS, FZ), jnp.float32)
    for k in range(CX):
        number = axis[k].astype(jnp.float32)
        number = jnp.concatenate([number, number], axis=1)
        base[NUMBERS + JP * k : NUMBERS + JP * k + CY] = number
        if k == 0:
            down[24:32] = number


def cell_sums(grid_shift, count, v, occ, axis_index, pos, vel, mass):
    return pl.pallas_call(
        sums_kernel,
        out_shape=(
            struct(BASE, FZ),
            struct(24, FZ),
            struct(32, FZ),
        ),
        in_specs=[HBM] * 8,
        out_specs=(IN_VMEM,) * 3,
        scratch_shapes=[
            SMEM((3,), jnp.int32),
            SMEM((1, 1), jnp.int32),
            VMEM((3, FX, 2 * FY, FZ), jnp.float32),
            VMEM((FX, FY, FZ), jnp.int32),
            VMEM((CX, CY, CZ), jnp.int32),
            VMEM((3, 1, FZ), jnp.float32),
            VMEM((3, 1, FZ), jnp.float32),
            VMEM((1, 1, FZ), jnp.float32),
            VMEM((2 * FX * FY, FZ), jnp.float32),
            VMEM((4, KX, JP, FZ), jnp.float32),
            DMA((6,)),
            DMA((CX,)),
            DMA((CX,)),
        ],
        cost_estimate=pl.CostEstimate(flops=4_000_000, bytes_accessed=3_700_000, transcendentals=0),
        name="cell_sums",
    )(grid_shift, count, v, occ, axis_index, pos, vel, mass)


def prepare_kernel(base, part, state, numbers):
    part[...] = base[0:STATE]
    state[...] = base[STATE:NUMBERS]
    numbers[...] = base[NUMBERS:BASE]


def prepare(base):
    return pl.pallas_call(
        prepare_kernel,
        out_shape=(struct(STATE, FZ), struct(16, FZ), struct(ROWS, FZ)),
        in_specs=[IN_VMEM],
        out_specs=(IN_VMEM,) * 3,
        compiler_params=pltpu.CompilerParams(vmem_limit_bytes=SMALL_LIMIT),
        cost_estimate=pl.CostEstimate(flops=10_000, bytes_accessed=460_000, transcendentals=0),
        name="prepare",
    )(base)


def add_x(part, up, down, full):
    for p in range(2):
        base = p * ROWS
        full[base : base + ROWS] = part[base : base + ROWS]
        full[base : base + 8] += up[8 * p : 8 * p + 8]
        full[base + 8 : base + 9] += up[16 + p : 17 + p]
        last = base + CX * JP
        full[last : last + 8] += down[8 * p : 8 * p + 8]
        full[last + 8 : last + 9] += down[16 + p : 17 + p]


def columns_kernel(part, up1, down1, state, numbers, up, down, full):
    add_x(part, up1, down1, full)
    for p in range(2):
        down[9 * p : 9 * p + 9] = full[pl.ds(p * ROWS, KX, JP), :]
        up[9 * p : 9 * p + 9] = full[pl.ds(p * ROWS + 8, KX, JP), :]
    for packet in (up, down):
        packet[18:22] = up1[18:22]
        packet[22:25] = state[0:3]
        packet[25:26] = state[7:8]
        packet[26:30] = down1[18:22]
    up[30:32] = jnp.zeros((2, FZ), jnp.float32)
    down[30:38] = numbers[pl.ds(0, CX, JP), :]
    down[38:39] = down1[24:25]
    down[39:40] = jnp.zeros((1, FZ), jnp.float32)


def columns(part, up1, down1, state, numbers):
    return pl.pallas_call(
        columns_kernel,
        out_shape=(struct(32, FZ), struct(40, FZ)),
        in_specs=[IN_VMEM] * 5,
        out_specs=(IN_VMEM,) * 2,
        scratch_shapes=[VMEM((2 * ROWS, FZ), jnp.float32)],
        compiler_params=pltpu.CompilerParams(vmem_limit_bytes=SMALL_LIMIT),
        cost_estimate=pl.CostEstimate(flops=100_000, bytes_accessed=500_000, transcendentals=0),
        name="columns",
    )(part, up1, down1, state, numbers)


def pair_force(own, others, rows, terms):
    for i, other in enumerate(others):
        for c in range(4):
            rows[4 * i + c] = jnp.broadcast_to(other[c], (8, FZ))
    column = jnp.concatenate(list(own) + [jnp.zeros((5, FZ), jnp.float32)], axis=0).T
    for t in range(FZ // 16):
        part = column[16 * t : 16 * t + 16]
        mine = [
            jnp.broadcast_to(part[:, c : c + 1], (16, FZ)).reshape(2, 8, FZ) for c in range(3)
        ]
        total = None
        for i in range(len(others)):
            dx = mine[0] - rows[4 * i][None]
            dy = mine[1] - rows[4 * i + 1][None]
            dz = mine[2] - rows[4 * i + 2][None]
            dz = jnp.where(
                dz > 0.5 * CZ, dz - CZ, jnp.where(dz < -0.5 * CZ, dz + CZ, dz)
            )
            reach = jnp.maximum(
                rows[4 * i + 3][None]
                - (dx * dx + dy * dy + dz * dz) * (1.0 / (cutoff * cutoff)),
                0.0,
            )
            weight = reach * reach
            new = (weight * dx, weight * dy, weight * dz)
            total = new if total is None else tuple(a + b for a, b in zip(total, new))
        for c in range(3):
            terms[FZ * c + 16 * t : FZ * c + 16 * t + 16] = total[c].reshape(16, FZ)
    ones = jnp.ones((8, FZ), jnp.bfloat16)
    left = terms[...]
    back = None
    for part in range(3):
        piece = left.astype(jnp.bfloat16)
        term = lax.dot_general(ones, piece, NT, preferred_element_type=jnp.float32)
        back = term if back is None else back + term
        if part < 2:
            left = left - piece.astype(jnp.float32)
    return [stiffness * back[0:1, FZ * c : FZ * c + FZ] for c in range(3)]


PAIR_SCRATCH = [VMEM((36, 8, FZ), jnp.float32), VMEM((3 * FZ, FZ), jnp.float32)]


def around(column, live):
    others = []
    for b in range(3):
        for a in range(3):
            x, y, z = column(b, a)
            limit = jnp.where(live(b, a) > 0.0, 1.0, -1.0)
            others.append((x + (a - 1) * float(CX), y + (b - 1) * float(CY), z, limit))
    return others


def advance(own, velocity, mass, others, rows, terms):
    force = pair_force(own, others, rows, terms)
    velocity = [velocity[c] + timestep * force[c] / mass for c in range(3)]
    return [own[c] + timestep * velocity[c] for c in range(3)], velocity


def fields_kernel(
    part, up1, down1, up2, down2, state, numbers_in,
    field_out, live_out, vel_out, pos_out,
    full, numbers, pair_rows, pair_terms,
):
    add_x(part, up1, down1, full)
    for p in range(2):
        first = pl.ds(p * ROWS, KX, JP)
        full[first, :] = full[first, :] + up2[9 * p : 9 * p + 9]
        last = pl.ds(p * ROWS + 8, KX, JP)
        full[last, :] = full[last, :] + down2[9 * p : 9 * p + 9]
    numbers[...] = numbers_in[...]
    numbers[JP * CX : JP * CX + 8] = down1[24:32]
    numbers[pl.ds(8, KX, JP), :] = down2[30:39]

    lane = lax.broadcasted_iota(jnp.int32, (8, FZ), 1)
    number = (lane & (DIRECTIONS - 1)).astype(jnp.float32)
    height = 1.0 - (2.0 * number + 1.0) / DIRECTIONS
    radius = jnp.sqrt(1.0 - height * height)
    phase = number * golden
    index = numbers[...].astype(jnp.int32)
    n0, n1, n2 = [
        jnp.take_along_axis(jnp.broadcast_to(table[0:1], (ROWS, FZ)), index, axis=1)
        for table in (radius * jnp.cos(phase), radius * jnp.sin(phase), height)
    ]

    lower = lax.broadcasted_iota(jnp.int32, (ROWS, FZ), 1) < CZ
    first, second = full[0:ROWS], full[ROWS : 2 * ROWS]
    heavy = jnp.maximum(jnp.where(lower, pltpu.roll(second, CZ, 1), second), fill_mass)
    mean_xy = first / heavy
    mean_z = second / heavy
    mean_yx = pltpu.roll(mean_xy, CZ, 1)
    mean_z_up = pltpu.roll(mean_z, CZ, 1)
    turn = 1.0 - cos_angle
    t0, t1, t2 = turn * n0, turn * n1, turn * n2
    s0, s1, s2 = sin_angle * n0, sin_angle * n1, sin_angle * n2
    field_out[0] = jnp.where(lower, cos_angle + t0 * n0, t0 * n1 - s2)
    field_out[1] = jnp.where(lower, t0 * n2 + s1, t0 * n1 + s2)
    field_out[2] = jnp.where(lower, cos_angle + t1 * n1, t1 * n2 - s0)
    field_out[3] = jnp.where(lower, t0 * n2 - s1, t1 * n2 + s0)
    field_out[4] = jnp.where(lower, cos_angle + t2 * n2, mean_yx)
    field_out[5] = jnp.where(lower, mean_yx, mean_z_up)

    place = state[8:9].astype(jnp.int32)
    lz = state[9:10].astype(jnp.int32)
    to_place = (lax.broadcasted_iota(jnp.int32, (CZ, FZ), 0) == lz).astype(jnp.float32)
    none = jnp.zeros_like(to_place)
    right = jnp.concatenate(
        [jnp.concatenate([to_place, none], axis=1), jnp.concatenate([none, to_place], axis=1)],
        axis=0,
    )
    hit = lax.broadcasted_iota(jnp.int32, (ROWS, FZ), 0) == place
    picked = []
    for pair in (mean_xy, jnp.where(lower, mean_z, n0), jnp.where(lower, n1, n2)):
        at_z = exact_dot(pair, right, NN)
        for half in (at_z[:, :FZ], at_z[:, FZ:]):
            picked.append(jnp.sum(jnp.where(hit, half, 0.0), axis=0, keepdims=True))
    u, n = picked[:3], picked[3:]
    alive = state[7:8] > 0.0
    old = [state[3 + c : 4 + c] for c in range(3)]
    rel = [old[c] - u[c] for c in range(3)]
    cross = [n[1] * rel[2] - n[2] * rel[1], n[2] * rel[0] - n[0] * rel[2], n[0] * rel[1] - n[1] * rel[0]]
    along = n[0] * rel[0] + n[1] * rel[1] + n[2] * rel[2]
    velocity = [
        jnp.where(
            alive,
            u[c] + cos_angle * rel[c] + sin_angle * cross[c] + turn * along * n[c],
            old[c],
        )
        for c in range(3)
    ]

    own = [state[c : c + 1] for c in range(3)]
    alive_row = state[7:8]

    def rows(b, a):
        if b == 1 and a == 1:
            return own + [alive_row]
        if b == 1:
            source, base = (up1, 18) if a == 0 else (down1, 18)
        else:
            source, base = (up2 if b == 0 else down2), 18 + 4 * a
        return [source[base + c : base + c + 1] for c in range(4)]

    live_out[9:16] = state[0:7]
    for b in range(3):
        for a in range(3):
            live_out[3 * b + a : 3 * b + a + 1] = rows(b, a)[3]
    others = around(lambda b, a: rows(b, a)[:3], lambda b, a: rows(b, a)[3])
    moved, velocity = advance(own, velocity, state[6:7], others, pair_rows, pair_terms)
    for c in range(3):
        vel_out[c : c + 1] = velocity[c]
        pos_out[c : c + 1] = moved[c]
    vel_out[3:4] = jnp.zeros((1, FZ), jnp.float32)
    pos_out[3:4] = jnp.zeros((1, FZ), jnp.float32)


def cell_fields(part, up1, down1, up2, down2, state, numbers):
    return pl.pallas_call(
        fields_kernel,
        out_shape=(struct(6, ROWS, FZ), struct(16, FZ), struct(4, FZ), struct(4, FZ)),
        in_specs=[IN_VMEM] * 7,
        out_specs=(IN_VMEM,) * 4,
        scratch_shapes=[
            VMEM((2 * ROWS, FZ), jnp.float32),
            VMEM((ROWS, FZ), jnp.float32),
            *PAIR_SCRATCH,
        ],
        compiler_params=pltpu.CompilerParams(vmem_limit_bytes=SMALL_LIMIT),
        cost_estimate=pl.CostEstimate(flops=4_000_000, bytes_accessed=1_000_000, transcendentals=0),
        name="cell_fields",
    )(part, up1, down1, up2, down2, state, numbers)


def substep_moves(rest, own, column, up, down, vel, rows, terms):
    mine = [own[c : c + 1] for c in range(3)]
    old = [vel[c : c + 1] for c in range(3)]
    source = (up, column, down)
    others = around(
        lambda b, a: [source[b][4 * a + c : 4 * a + c + 1] for c in range(3)],
        lambda b, a: rest[3 * b + a : 3 * b + a + 1],
    )
    return advance(mine, old, rest[15:16], others, rows, terms)


def substep_kernel(rest, own, column, up, down, vel, vel_out, pos_out, rows, terms):
    moved, velocity = substep_moves(rest, own, column, up, down, vel, rows, terms)
    for c in range(3):
        vel_out[c : c + 1] = velocity[c]
        pos_out[c : c + 1] = moved[c]
    vel_out[3:4] = jnp.zeros((1, FZ), jnp.float32)
    pos_out[3:4] = jnp.zeros((1, FZ), jnp.float32)


def last_kernel(rest, own, column, up, down, vel, vel_out, pos_out, rows, terms):
    moved, velocity = substep_moves(rest, own, column, up, down, vel, rows, terms)
    keep = rest[4:5] > 0.0
    for c in range(3):
        pos_out[c] = jnp.where(keep, moved[c], rest[9 + c : 10 + c])
        vel_out[c] = jnp.where(keep, velocity[c], rest[12 + c : 13 + c])


def substep(kernel, shape, rest, own, column, up, down, vel):
    return pl.pallas_call(
        kernel,
        out_shape=(struct(*shape), struct(*shape)),
        in_specs=[IN_VMEM] * 6,
        out_specs=(IN_VMEM,) * 2,
        scratch_shapes=PAIR_SCRATCH,
        compiler_params=pltpu.CompilerParams(vmem_limit_bytes=SMALL_LIMIT),
        cost_estimate=pl.CostEstimate(flops=4_000_000, bytes_accessed=30_000, transcendentals=0),
        name="substep",
    )(rest, own, column, up, down, vel)


def turn_kernel(shift_at, v_at, occ_at, field, out_at, shift, v, occ, out, twice, wide, sem, vsem, osem, wsem):
    first = pltpu.make_async_copy(shift_at, shift, sem.at[0])
    first.start()
    large = []
    stores = []
    for q in range(CX):
        part = pl.ds(SUB * q, SUB)
        large.append(pltpu.make_async_copy(occ_at.at[part], occ.at[part], osem.at[q]))
        large.append(pltpu.make_async_copy(v_at.at[:, part], v.at[:, part], vsem.at[q]))
        stores.append(pltpu.make_async_copy(out.at[:, part], out_at.at[:, part], wsem.at[q]))
    for copy in large:
        copy.start()
    first.wait()
    sx, sy, sz = shift[0], shift[1], shift[2]
    source = lax.broadcasted_iota(jnp.int32, (CZ, FZ), 0)
    layer = lax.broadcasted_iota(jnp.int32, (CZ, FZ), 1)
    spread = (((layer + sz) & (FZ - 1)) >> 1 == source).astype(jnp.float32)
    none = jnp.zeros_like(spread)
    right = jnp.concatenate(
        [jnp.concatenate([spread, none], axis=1), jnp.concatenate([none, spread], axis=1)],
        axis=0,
    )
    for f in range(6):
        both = exact_dot(field[f], right, NN)
        wide[2 * f] = both[:, :FZ]
        wide[2 * f + 1] = both[:, FZ:]
    row = lax.broadcasted_iota(jnp.int32, (8, FZ), 0)
    slot = (row & 1).astype(jnp.float32)
    low = row < 8 - 2 * sy

    for k in range(KX):
        if k < CX:
            large[2 * k].wait()
            store_twice(occ, twice, k)
            large[2 * k + 1].wait()

        def column(t, carry, k=k):
            f = [
                jnp.where(
                    low, wide[i, pl.ds(k * JP + t, 1), :], wide[i, pl.ds(k * JP + t + 1, 1), :]
                )
                for i in range(12)
            ]
            rows = pl.ds(pl.multiple_of(8 * t, 8), 8)

            def plane(x, carry):
                live = twice[pl.ds(pl.multiple_of(x * 2 * FY + 8 * t, 8), 8), :] > slot
                old = [v[c, x, rows, :] for c in range(3)]
                rel = [old[c] - f[9 + c] for c in range(3)]
                for c in range(3):
                    new = f[9 + c] + (
                        f[3 * c] * rel[0] + f[3 * c + 1] * rel[1] + f[3 * c + 2] * rel[2]
                    )
                    out[c, x, rows, :] = jnp.where(live, new, old[c])
                return carry

            if k == 0:
                lax.fori_loop(0, SUB - sx, plane, 0)
            elif k == CX:
                lax.fori_loop(FX - sx, FX, plane, 0)
            else:
                for j in range(SUB):
                    plane(k * SUB - sx + j, 0)
            return carry

        lax.fori_loop(0, CY, column, 0)
        if k:
            stores[k - 1].start()
    for copy in stores:
        copy.wait()


def turn_solvent(grid_shift, v, occ, field):
    return pl.pallas_call(
        turn_kernel,
        out_shape=struct(*v.shape),
        in_specs=[HBM, HBM, HBM, IN_VMEM],
        out_specs=HBM,
        scratch_shapes=[
            SMEM((3,), jnp.int32),
            VMEM((3, FX, 2 * FY, FZ), jnp.float32),
            VMEM((FX, FY, FZ), jnp.int32),
            VMEM((3, FX, 2 * FY, FZ), jnp.float32),
            VMEM((2 * FX * FY, FZ), jnp.float32),
            VMEM((12, ROWS, FZ), jnp.float32),
            DMA((1,)),
            DMA((CX,)),
            DMA((CX,)),
            DMA((CX,)),
        ],
        compiler_params=pltpu.CompilerParams(vmem_limit_bytes=TURN_LIMIT),
        cost_estimate=pl.CostEstimate(flops=8_000_000, bytes_accessed=7_000_000, transcendentals=0),
        name="turn_solvent",
    )(grid_shift, v, occ, field)


def per_device(
    solvent_vel,
    occupancy,
    grid_shift,
    axis_index,
    colloid_pos,
    colloid_vel,
    colloid_mass,
    colloid_count,
):
    v = solvent_vel.reshape(3, FX, 2 * FY, FZ)
    pos = colloid_pos.reshape(3, 1, FZ)
    vel = colloid_vel.reshape(3, 1, FZ)
    mass = colloid_mass
    count = colloid_count

    base, up, down = cell_sums(grid_shift, count, v, occupancy, axis_index, pos, vel, mass)
    up1, down1 = shifted(up, "gx", 1), shifted(down, "gx", -1)
    part, state, numbers = prepare(base)
    up, down = columns(part, up1, down1, state, numbers)
    up2, down2 = shifted(up, "yz", 1), shifted(down, "yz", -1)
    field, rest, velocity, position = cell_fields(part, up1, down1, up2, down2, state, numbers)
    solvent_out = turn_solvent(grid_shift, v, occupancy, field)
    for step in range(1, SUBSTEPS):
        column = jnp.concatenate([shifted(position, "gx", 1), position, shifted(position, "gx", -1)])
        up, down = shifted(column, "yz", 1), shifted(column, "yz", -1)
        kernel, shape = (
            (substep_kernel, (4, FZ)) if step < SUBSTEPS - 1 else (last_kernel, (3, 1, FZ))
        )
        velocity, position = substep(
            kernel, shape, rest, position, column, up, down, velocity
        )
    return (
        solvent_out.reshape(solvent_vel.shape),
        position[:, None],
        velocity[:, None],
    )


def solution(mesh):
    return jax.shard_map(
        per_device,
        mesh=mesh,
        in_specs=(
            P(None, "gx", "yz", None, None),
            P("gx", "yz", None),
            P(),
            P("gx", "yz", None),
            P(None, "gx", "yz", None),
            P(None, "gx", "yz", None),
            P("gx", "yz", None),
            P("gx", "yz"),
        ),
        out_specs=(
            P(None, "gx", "yz", None, None),
            P(None, "gx", "yz", None),
            P(None, "gx", "yz", None),
        ),
        check_vma=False,
    )
```

profile of v0, /device:TPU:1, one launch (start us, length us, event | category | flops | bytes accessed | tf_op | source)
XLA Modules:
  0.0 73.4 jit_solution(14751589606776815704)
XLA Ops:
  0.6 0.0 copy-start.2
  0.6 0.0 copy-start
  1.4 3.5 %cell_sums.1 = (f32[448,128]{1,0:T(8,128)}, f32[24,128]{1,0:T(8,128)}, f32[32,128]{1,0:T(8,128)}) custom-call(s32[3]{0:T(128)} %shift_at.3, s32[1,1]{1,0:T(1,128)S(6)} %copy.13.count_at, f32[3,32,64,128]{3,2,1,0:T(8,128)} %bitcast.10, s32[32,32,128]{2,1,0:T(8,128)} %occ_at.3, s32[8,8,64]{2,1,0:T(8,128)} %axis_at.1, f32[3,1,128]{2,1,0:T(1,128)} %bitcast.13, ...), custom_call_target="tpu_custom_call" | custom-call | flops 4000000 | bytes 3700000 | tf_op jit(solution)/shard_map/cell_sums/pallas_call | solution.py:205
  4.9 9.4 %collective-permute-start.1 = (f32[32,128]{1,0:T(8,128)}, f32[32,128]{1,0:T(8,128)S(1)}, u32[]{:S(2)}, u32[]{:S(2)}) collective-permute-start(f32[32,128]{1,0:T(8,128)} %get-tuple-element.24), channel_id=1, source_target_pairs={{0,240},{16,0},{32,16},{48,32},{64,48},{80,64},{96,80},{112,96},{1... | collective-permute-start | bytes 49160 | tf_op jit(solution)/shard_map/ppermute | solution.py:50
  14.3 0.0 collective-permute-start
  14.3 0.0 copy-start.1
  14.3 0.9 %copy-done.1 = f32[448,128]{1,0:T(8,128)S(1)} copy-done((f32[448,128]{1,0:T(8,128)S(1)}, f32[448,128]{1,0:T(8,128)}, u32[]{:S(2)}) %copy-start.1) | copy-done | bytes 229400
  15.2 6.0 %collective-permute-done.up1 = f32[24,128]{1,0:T(8,128)S(1)} collective-permute-done((f32[24,128]{1,0:T(8,128)}, f32[24,128]{1,0:T(8,128)S(1)}, u32[]{:S(2)}, u32[]{:S(2)}) %collective-permute-start) | collective-permute-done | bytes 12320 | tf_op jit(solution)/shard_map/ppermute | solution.py:50
  21.2 0.0 collective-permute-done.1.down1
  21.3 2.2 %collective-permute-start.3 = (f32[40,128]{1,0:T(8,128)S(1)}, f32[40,128]{1,0:T(8,128)S(1)}, u32[]{:S(2)}, u32[]{:S(2)}) collective-permute-start(f32[40,128]{1,0:T(8,128)S(1)} %get-tuple-element.28), channel_id=1, source_target_pairs={{0,15},{1,0},{2,1},{3,2},{4,3},{5,4},{6,5},{7,6},{8,7},{9,8},{10,9... | collective-permute-start | bytes 61448 | tf_op jit(solution)/shard_map/ppermute | solution.py:50
  23.5 1.2 %collective-permute-start.2 = (f32[32,128]{1,0:T(8,128)S(1)}, f32[32,128]{1,0:T(8,128)S(1)}, u32[]{:S(2)}, u32[]{:S(2)}) collective-permute-start(f32[32,128]{1,0:T(8,128)S(1)} %get-tuple-element.27), channel_id=1, source_target_pairs={{0,1},{1,2},{2,3},{3,4},{4,5},{5,6},{6,7},{7,8},{8,9},{9,10},{10,1... | collective-permute-start | bytes 49160 | tf_op jit(solution)/shard_map/ppermute | solution.py:50
  24.6 0.9 %collective-permute-done.2.up2 = f32[32,128]{1,0:T(8,128)S(1)} collective-permute-done((f32[32,128]{1,0:T(8,128)S(1)}, f32[32,128]{1,0:T(8,128)S(1)}, u32[]{:S(2)}, u32[]{:S(2)}) %collective-permute-start.2) | collective-permute-done | bytes 16416 | tf_op jit(solution)/shard_map/ppermute | solution.py:50
  25.5 0.5 collective-permute-done.3.down2
  26.0 1.1 %cell_fields.1 = (f32[6,144,128]{2,1,0:T(8,128)S(1)}, f32[16,128]{1,0:T(8,128)S(1)}, f32[4,128]{1,0:T(4,128)S(1)}, f32[4,128]{1,0:T(4,128)S(1)}) custom-call(f32[288,128]{1,0:T(8,128)S(1)} %get-tuple-element.22.part, f32[24,128]{1,0:T(8,128)S(1)} %collective-permute-done.up1, f32[32,128]{1,0:T(8,128)S(1)} %collective-permute-done.1.down1, ...), custom_call_target="tpu_custom_call" | custom-call | flops 4000000 | bytes 1000000 | tf_op jit(solution)/shard_map/cell_fields/pallas_call | solution.py:449
  27.2 0.1 collective-permute-start.5
  27.3 1.5 %collective-permute-start.4 = (f32[4,128]{1,0:T(4,128)S(1)}, f32[4,128]{1,0:T(4,128)S(1)}, u32[]{:S(2)}, u32[]{:S(2)}) collective-permute-start(f32[4,128]{1,0:T(4,128)S(1)} %get-tuple-element.31.own), channel_id=1, source_target_pairs={{0,16},{16,32},{32,48},{48,64},{64,80},{80,96},{96,112},{112,128},... | collective-permute-start | bytes 6152 | tf_op jit(solution)/shard_map/ppermute | solution.py:50
  28.7 1.0 %collective-permute-done.5 = f32[4,128]{1,0:T(4,128)S(1)} collective-permute-done((f32[4,128]{1,0:T(4,128)S(1)}, f32[4,128]{1,0:T(4,128)S(1)}, u32[]{:S(2)}, u32[]{:S(2)}) %collective-permute-start.5) | collective-permute-done | bytes 2080 | tf_op jit(solution)/shard_map/ppermute | solution.py:50
  29.7 4.3 %collective-permute-done.4 = f32[4,128]{1,0:T(4,128)S(1)} collective-permute-done((f32[4,128]{1,0:T(4,128)S(1)}, f32[4,128]{1,0:T(4,128)S(1)}, u32[]{:S(2)}, u32[]{:S(2)}) %collective-permute-start.4) | collective-permute-done | bytes 2080 | tf_op jit(solution)/shard_map/ppermute | solution.py:50
  34.0 5.4 %collective-permute-start.7 = (f32[12,128]{1,0:T(8,128)S(1)}, f32[12,128]{1,0:T(8,128)S(1)}, u32[]{:S(2)}, u32[]{:S(2)}) collective-permute-start(f32[12,128]{1,0:T(8,128)S(1)} %pad_maximum_fusion.column), channel_id=1, source_target_pairs={{0,15},{1,0},{2,1},{3,2},{4,3},{5,4},{6,5},{7,6},{8,7},{9,8},{10,9... | collective-permute-start | bytes 18440 | tf_op jit(solution)/shard_map/ppermute | solution.py:50
  39.4 0.0 collective-permute-start.6
  39.4 0.8 %collective-permute-done.7.down = f32[12,128]{1,0:T(8,128)S(1)} collective-permute-done((f32[12,128]{1,0:T(8,128)S(1)}, f32[12,128]{1,0:T(8,128)S(1)}, u32[]{:S(2)}, u32[]{:S(2)}) %collective-permute-start.7) | collective-permute-done | bytes 6176 | tf_op jit(solution)/shard_map/ppermute | solution.py:50
  40.2 0.3 collective-permute-done.6.up
  40.6 0.8 %substep.3 = (f32[4,128]{1,0:T(4,128)S(1)}, f32[4,128]{1,0:T(4,128)S(1)}) custom-call(f32[16,128]{1,0:T(8,128)S(1)} %get-tuple-element.30.rest, f32[4,128]{1,0:T(4,128)S(1)} %get-tuple-element.31.own, f32[12,128]{1,0:T(8,128)S(1)} %pad_maximum_fusion.column, f32[12,128]{1,0:T(8,128)S(1)} %collective-permute-done.6.up, ...), custom_call_target="tpu_custom_call" | custom-call | flops 4000000 | bytes 30000 | tf_op jit(solution)/shard_map/substep/pallas_call | solution.py:494
  41.4 0.1 collective-permute-start.9
  41.5 1.5 %collective-permute-start.8 = (f32[4,128]{1,0:T(4,128)S(1)}, f32[4,128]{1,0:T(4,128)S(1)}, u32[]{:S(2)}, u32[]{:S(2)}) collective-permute-start(f32[4,128]{1,0:T(4,128)S(1)} %get-tuple-element.33.own), channel_id=1, source_target_pairs={{0,16},{16,32},{32,48},{48,64},{64,80},{80,96},{96,112},{112,128},... | collective-permute-start | bytes 6152 | tf_op jit(solution)/shard_map/ppermute | solution.py:50
  42.9 1.3 %collective-permute-done.9 = f32[4,128]{1,0:T(4,128)S(1)} collective-permute-done((f32[4,128]{1,0:T(4,128)S(1)}, f32[4,128]{1,0:T(4,128)S(1)}, u32[]{:S(2)}, u32[]{:S(2)}) %collective-permute-start.9) | collective-permute-done | bytes 2080 | tf_op jit(solution)/shard_map/ppermute | solution.py:50
  44.2 4.0 %collective-permute-done.8 = f32[4,128]{1,0:T(4,128)S(1)} collective-permute-done((f32[4,128]{1,0:T(4,128)S(1)}, f32[4,128]{1,0:T(4,128)S(1)}, u32[]{:S(2)}, u32[]{:S(2)}) %collective-permute-start.8) | collective-permute-done | bytes 2080 | tf_op jit(solution)/shard_map/ppermute | solution.py:50
  48.2 5.3 %collective-permute-start.11 = (f32[12,128]{1,0:T(8,128)S(1)}, f32[12,128]{1,0:T(8,128)S(1)}, u32[]{:S(2)}, u32[]{:S(2)}) collective-permute-start(f32[12,128]{1,0:T(8,128)S(1)} %pad_maximum_fusion.1.column), channel_id=1, source_target_pairs={{0,15},{1,0},{2,1},{3,2},{4,3},{5,4},{6,5},{7,6},{8,7},{9,8},{10,9... | collective-permute-start | bytes 18440 | tf_op jit(solution)/shard_map/ppermute | solution.py:50
  53.6 0.0 collective-permute-start.10
  53.6 0.8 %collective-permute-done.11.down = f32[12,128]{1,0:T(8,128)S(1)} collective-permute-done((f32[12,128]{1,0:T(8,128)S(1)}, f32[12,128]{1,0:T(8,128)S(1)}, u32[]{:S(2)}, u32[]{:S(2)}) %collective-permute-start.11) | collective-permute-done | bytes 6176 | tf_op jit(solution)/shard_map/ppermute | solution.py:50
  54.4 0.3 collective-permute-done.10.up
  54.7 0.8 %substep.4 = (f32[4,128]{1,0:T(4,128)S(1)}, f32[4,128]{1,0:T(4,128)S(1)}) custom-call(f32[16,128]{1,0:T(8,128)S(1)} %get-tuple-element.30.rest, f32[4,128]{1,0:T(4,128)S(1)} %get-tuple-element.33.own, f32[12,128]{1,0:T(8,128)S(1)} %pad_maximum_fusion.1.column, f32[12,128]{1,0:T(8,128)S(1)} %collective-permute-done.10.up, ...), custom_call_target="tpu_custom_call" | custom-call | flops 4000000 | bytes 30000 | tf_op jit(solution)/shard_map/substep/pallas_call | solution.py:494
  55.6 0.1 collective-permute-start.13
  55.7 1.5 %collective-permute-start.12 = (f32[4,128]{1,0:T(4,128)S(1)}, f32[4,128]{1,0:T(4,128)S(1)}, u32[]{:S(2)}, u32[]{:S(2)}) collective-permute-start(f32[4,128]{1,0:T(4,128)S(1)} %get-tuple-element.35.own), channel_id=1, source_target_pairs={{0,16},{16,32},{32,48},{48,64},{64,80},{80,96},{96,112},{112,128},... | collective-permute-start | bytes 6152 | tf_op jit(solution)/shard_map/ppermute | solution.py:50
  57.1 1.3 %collective-permute-done.13 = f32[4,128]{1,0:T(4,128)S(1)} collective-permute-done((f32[4,128]{1,0:T(4,128)S(1)}, f32[4,128]{1,0:T(4,128)S(1)}, u32[]{:S(2)}, u32[]{:S(2)}) %collective-permute-start.13) | collective-permute-done | bytes 2080 | tf_op jit(solution)/shard_map/ppermute | solution.py:50
  58.4 4.0 %collective-permute-done.12 = f32[4,128]{1,0:T(4,128)S(1)} collective-permute-done((f32[4,128]{1,0:T(4,128)S(1)}, f32[4,128]{1,0:T(4,128)S(1)}, u32[]{:S(2)}, u32[]{:S(2)}) %collective-permute-start.12) | collective-permute-done | bytes 2080 | tf_op jit(solution)/shard_map/ppermute | solution.py:50
  62.4 5.5 %collective-permute-start.15 = (f32[12,128]{1,0:T(8,128)S(1)}, f32[12,128]{1,0:T(8,128)S(1)}, u32[]{:S(2)}, u32[]{:S(2)}) collective-permute-start(f32[12,128]{1,0:T(8,128)S(1)} %pad_maximum_fusion.2.column), channel_id=1, source_target_pairs={{0,15},{1,0},{2,1},{3,2},{4,3},{5,4},{6,5},{7,6},{8,7},{9,8},{10,9... | collective-permute-start | bytes 18440 | tf_op jit(solution)/shard_map/ppermute | solution.py:50
  67.9 0.0 collective-permute-start.14
  67.9 0.0 copy-done.2
  67.9 0.0 copy-done
  67.9 4.0 %turn_solvent.1 = f32[3,32,64,128]{3,2,1,0:T(8,128)} custom-call(s32[3]{0:T(128)S(1)} %copy-done.2, f32[3,32,64,128]{3,2,1,0:T(8,128)} %bitcast.11, s32[32,32,128]{2,1,0:T(8,128)S(1)} %copy-done, f32[6,144,128]{2,1,0:T(8,128)S(1)} %get-tuple-element.29.field), custom_call_target="tpu_custom_call" | custom-call | flops 8000000 | bytes 7000000 | tf_op jit(solution)/shard_map/turn_solvent/pallas_call | solution.py:579
  72.0 0.0 collective-permute-done.15.down
  72.0 0.0 collective-permute-done.14.up
  72.0 1.4 %substep.5 = (f32[3,1,128]{2,1,0:T(1,128)}, f32[3,1,128]{2,1,0:T(1,128)}) custom-call(f32[16,128]{1,0:T(8,128)S(1)} %get-tuple-element.30.rest, f32[4,128]{1,0:T(4,128)S(1)} %get-tuple-element.35.own, f32[12,128]{1,0:T(8,128)S(1)} %pad_maximum_fusion.2.column, f32[12,128]{1,0:T(8,128)S(1)} %collective-permute-done.14.up, ...), custom_call_target="tpu_custom_call" | custom-call | flops 4000000 | bytes 30000 | tf_op jit(solution)/shard_map/substep/pallas_call | solution.py:494
  (5 shorter events, 0.1 us)
Async XLA Ops:
  0.6 67.3 %copy-start.2 = (s32[3]{0:T(128)S(1)}, s32[3]{0:T(128)}, u32[]{:S(2)}) copy-start(s32[3]{0:T(128)} %shift_at.3) | copy-start | bytes 40
  0.6 67.3 %copy-start = (s32[32,32,128]{2,1,0:T(8,128)S(1)}, s32[32,32,128]{2,1,0:T(8,128)}, u32[]{:S(2)}) copy-start(s32[32,32,128]{2,1,0:T(8,128)} %occ_at.3) | copy-start | bytes 1572868
  4.9 16.4 %collective-permute-start.1 = (f32[32,128]{1,0:T(8,128)}, f32[32,128]{1,0:T(8,128)S(1)}, u32[]{:S(2)}, u32[]{:S(2)}) collective-permute-start(f32[32,128]{1,0:T(8,128)} %get-tuple-element.24), channel_id=1, source_target_pairs={{0,240},{16,0},{32,16},{48,32},{64,48},{80,64},{96,80},{112,96},{1... | collective-permute-start | bytes 49160 | tf_op jit(solution)/shard_map/ppermute | solution.py:50
  14.3 7.0 %collective-permute-start = (f32[24,128]{1,0:T(8,128)}, f32[24,128]{1,0:T(8,128)S(1)}, u32[]{:S(2)}, u32[]{:S(2)}) collective-permute-start(f32[24,128]{1,0:T(8,128)} %get-tuple-element.23), channel_id=1, source_target_pairs={{0,16},{16,32},{32,48},{48,64},{64,80},{80,96},{96,112},{112,128},... | collective-permute-start | bytes 36872 | tf_op jit(solution)/shard_map/ppermute | solution.py:50
  14.3 0.9 %copy-start.1 = (f32[448,128]{1,0:T(8,128)S(1)}, f32[448,128]{1,0:T(8,128)}, u32[]{:S(2)}) copy-start(f32[448,128]{1,0:T(8,128)} %get-tuple-element.21.base) | copy-start | bytes 688132
  21.3 4.7 %collective-permute-start.3 = (f32[40,128]{1,0:T(8,128)S(1)}, f32[40,128]{1,0:T(8,128)S(1)}, u32[]{:S(2)}, u32[]{:S(2)}) collective-permute-start(f32[40,128]{1,0:T(8,128)S(1)} %get-tuple-element.28), channel_id=1, source_target_pairs={{0,15},{1,0},{2,1},{3,2},{4,3},{5,4},{6,5},{7,6},{8,7},{9,8},{10,9... | collective-permute-start | bytes 61448 | tf_op jit(solution)/shard_map/ppermute | solution.py:50
  23.5 2.1 %collective-permute-start.2 = (f32[32,128]{1,0:T(8,128)S(1)}, f32[32,128]{1,0:T(8,128)S(1)}, u32[]{:S(2)}, u32[]{:S(2)}) collective-permute-start(f32[32,128]{1,0:T(8,128)S(1)} %get-tuple-element.27), channel_id=1, source_target_pairs={{0,1},{1,2},{2,3},{3,4},{4,5},{5,6},{6,7},{7,8},{8,9},{9,10},{10,1... | collective-permute-start | bytes 49160 | tf_op jit(solution)/shard_map/ppermute | solution.py:50
  27.2 2.5 %collective-permute-start.5 = (f32[4,128]{1,0:T(4,128)S(1)}, f32[4,128]{1,0:T(4,128)S(1)}, u32[]{:S(2)}, u32[]{:S(2)}) collective-permute-start(f32[4,128]{1,0:T(4,128)S(1)} %get-tuple-element.31.own), channel_id=1, source_target_pairs={{0,240},{16,0},{32,16},{48,32},{64,48},{80,64},{96,80},{112,96},{1... | collective-permute-start | bytes 6152 | tf_op jit(solution)/shard_map/ppermute | solution.py:50
  27.3 6.7 %collective-permute-start.4 = (f32[4,128]{1,0:T(4,128)S(1)}, f32[4,128]{1,0:T(4,128)S(1)}, u32[]{:S(2)}, u32[]{:S(2)}) collective-permute-start(f32[4,128]{1,0:T(4,128)S(1)} %get-tuple-element.31.own), channel_id=1, source_target_pairs={{0,16},{16,32},{32,48},{48,64},{64,80},{80,96},{96,112},{112,128},... | collective-permute-start | bytes 6152 | tf_op jit(solution)/shard_map/ppermute | solution.py:50
  34.0 6.2 %collective-permute-start.7 = (f32[12,128]{1,0:T(8,128)S(1)}, f32[12,128]{1,0:T(8,128)S(1)}, u32[]{:S(2)}, u32[]{:S(2)}) collective-permute-start(f32[12,128]{1,0:T(8,128)S(1)} %pad_maximum_fusion.column), channel_id=1, source_target_pairs={{0,15},{1,0},{2,1},{3,2},{4,3},{5,4},{6,5},{7,6},{8,7},{9,8},{10,9... | collective-permute-start | bytes 18440 | tf_op jit(solution)/shard_map/ppermute | solution.py:50
  39.4 1.2 %collective-permute-start.6 = (f32[12,128]{1,0:T(8,128)S(1)}, f32[12,128]{1,0:T(8,128)S(1)}, u32[]{:S(2)}, u32[]{:S(2)}) collective-permute-start(f32[12,128]{1,0:T(8,128)S(1)} %pad_maximum_fusion.column), channel_id=1, source_target_pairs={{0,1},{1,2},{2,3},{3,4},{4,5},{5,6},{6,7},{7,8},{8,9},{9,10},{10,1... | collective-permute-start | bytes 18440 | tf_op jit(solution)/shard_map/ppermute | solution.py:50
  41.4 2.8 %collective-permute-start.9 = (f32[4,128]{1,0:T(4,128)S(1)}, f32[4,128]{1,0:T(4,128)S(1)}, u32[]{:S(2)}, u32[]{:S(2)}) collective-permute-start(f32[4,128]{1,0:T(4,128)S(1)} %get-tuple-element.33.own), channel_id=1, source_target_pairs={{0,240},{16,0},{32,16},{48,32},{64,48},{80,64},{96,80},{112,96},{1... | collective-permute-start | bytes 6152 | tf_op jit(solution)/shard_map/ppermute | solution.py:50
  41.5 6.7 %collective-permute-start.8 = (f32[4,128]{1,0:T(4,128)S(1)}, f32[4,128]{1,0:T(4,128)S(1)}, u32[]{:S(2)}, u32[]{:S(2)}) collective-permute-start(f32[4,128]{1,0:T(4,128)S(1)} %get-tuple-element.33.own), channel_id=1, source_target_pairs={{0,16},{16,32},{32,48},{48,64},{64,80},{80,96},{96,112},{112,128},... | collective-permute-start | bytes 6152 | tf_op jit(solution)/shard_map/ppermute | solution.py:50
  48.2 6.2 %collective-permute-start.11 = (f32[12,128]{1,0:T(8,128)S(1)}, f32[12,128]{1,0:T(8,128)S(1)}, u32[]{:S(2)}, u32[]{:S(2)}) collective-permute-start(f32[12,128]{1,0:T(8,128)S(1)} %pad_maximum_fusion.1.column), channel_id=1, source_target_pairs={{0,15},{1,0},{2,1},{3,2},{4,3},{5,4},{6,5},{7,6},{8,7},{9,8},{10,9... | collective-permute-start | bytes 18440 | tf_op jit(solution)/shard_map/ppermute | solution.py:50
  53.6 1.2 %collective-permute-start.10 = (f32[12,128]{1,0:T(8,128)S(1)}, f32[12,128]{1,0:T(8,128)S(1)}, u32[]{:S(2)}, u32[]{:S(2)}) collective-permute-start(f32[12,128]{1,0:T(8,128)S(1)} %pad_maximum_fusion.1.column), channel_id=1, source_target_pairs={{0,1},{1,2},{2,3},{3,4},{4,5},{5,6},{6,7},{7,8},{8,9},{9,10},{10,1... | collective-permute-start | bytes 18440 | tf_op jit(solution)/shard_map/ppermute | solution.py:50
  55.6 2.8 %collective-permute-start.13 = (f32[4,128]{1,0:T(4,128)S(1)}, f32[4,128]{1,0:T(4,128)S(1)}, u32[]{:S(2)}, u32[]{:S(2)}) collective-permute-start(f32[4,128]{1,0:T(4,128)S(1)} %get-tuple-element.35.own), channel_id=1, source_target_pairs={{0,240},{16,0},{32,16},{48,32},{64,48},{80,64},{96,80},{112,96},{1... | collective-permute-start | bytes 6152 | tf_op jit(solution)/shard_map/ppermute | solution.py:50
  55.7 6.7 %collective-permute-start.12 = (f32[4,128]{1,0:T(4,128)S(1)}, f32[4,128]{1,0:T(4,128)S(1)}, u32[]{:S(2)}, u32[]{:S(2)}) collective-permute-start(f32[4,128]{1,0:T(4,128)S(1)} %get-tuple-element.35.own), channel_id=1, source_target_pairs={{0,16},{16,32},{32,48},{48,64},{64,80},{80,96},{96,112},{112,128},... | collective-permute-start | bytes 6152 | tf_op jit(solution)/shard_map/ppermute | solution.py:50
  62.4 9.6 %collective-permute-start.15 = (f32[12,128]{1,0:T(8,128)S(1)}, f32[12,128]{1,0:T(8,128)S(1)}, u32[]{:S(2)}, u32[]{:S(2)}) collective-permute-start(f32[12,128]{1,0:T(8,128)S(1)} %pad_maximum_fusion.2.column), channel_id=1, source_target_pairs={{0,15},{1,0},{2,1},{3,2},{4,3},{5,4},{6,5},{7,6},{8,7},{9,8},{10,9... | collective-permute-start | bytes 18440 | tf_op jit(solution)/shard_map/ppermute | solution.py:50
  67.9 4.1 %collective-permute-start.14 = (f32[12,128]{1,0:T(8,128)S(1)}, f32[12,128]{1,0:T(8,128)S(1)}, u32[]{:S(2)}, u32[]{:S(2)}) collective-permute-start(f32[12,128]{1,0:T(8,128)S(1)} %pad_maximum_fusion.2.column), channel_id=1, source_target_pairs={{0,1},{1,2},{2,3},{3,4},{4,5},{5,6},{6,7},{7,8},{8,9},{9,10},{10,1... | collective-permute-start | bytes 18440 | tf_op jit(solution)/shard_map/ppermute | solution.py:50
where the time goes:
time: 73.5 us; the launch traced here: 73.4 us
  starting transfers between devices  33.6 us (46%)
  waiting for transfers between devices  25.6 us (35%)
  Pallas kernels  11.8 us (16%)
  between operations  1.46 us (2%)
  local copies, waits for them, and re-layouts  0.95 us (1%)
    ppermute x16, starting transfers between devices, shifted(): lax.ppermute(value, axis, [(i, (i + steps) % count) for i in range(count)])  33.6 us
    ppermute x16, waiting for transfers between devices, shifted(): lax.ppermute(value, axis, [(i, (i + steps) % count) for i in range(count)])  25.6 us
    pallas_call x1, Pallas kernels, turn_solvent(): pl.pallas_call(turn_kernel, out_shape=struct(*v.shape), in_specs=[HBM, HB...  4.05 us
    pallas_call x1, Pallas kernels, cell_sums(): pl.pallas_call(sums_kernel, out_shape=(struct(BASE, FZ), struct(24, FZ),...  3.51 us
    pallas_call x3, Pallas kernels, substep(): pl.pallas_call(kernel, out_shape=(struct(*shape), struct(*shape)), in_spe...  3.05 us
  transfers between devices with their start and end apart: 16, of which 13 were waited for; matrix products, arithmetic and copies ran while one was open for 0% of the time, Pallas kernels for 6%

commit v1 on v0

--- a/solution.py
+++ b/solution.py
@@ -1,3 +1,4 @@
+import functools
 import math
 
 import jax
@@ -41,13 +42,23 @@
 STATE = 2 * ROWS
 NUMBERS = STATE + 16
 BASE = NUMBERS + ROWS
+TURNED = ((1, 2, 3), (4, 5, 6), (7, CX))
+TILE = 32
 SMALL_LIMIT = 8 * 1024 * 1024
-TURN_LIMIT = 52 * 1024 * 1024
-
-
-def shifted(value, axis, steps):
+TURN_LIMIT = 16 * 1024 * 1024
+
+
+def swapped(value, axis, first):
     count = lax.axis_size(axis)
-    return lax.ppermute(value, axis, [(i, (i + steps) % count) for i in range(count)])
+    pairs = []
+    for low in range(first, count + first, 2):
+        a, b = low % count, (low + 1) % count
+        pairs += [(a, b), (b, a)]
+    return lax.ppermute(value, axis, pairs)
+
+
+def swap_both(odd, even, axis):
+    return swapped(odd, axis, 1), swapped(even, axis, 0)
 
 
 def struct(*shape):
@@ -84,9 +95,13 @@
     twice[pl.ds(base + 1, SUB * FY, 2), :] = slots
 
 
+def parity(axis):
+    return lax.axis_index(axis) & 1
+
+
 def sums_kernel(
     shift_at, count_at, v_at, occ_at, axis_at, pos_at, vel_at, mass_at,
-    base, up, down,
+    base, odd, even,
     shift, count, v, occ, axis, pos, vel, mass, twice, partial, sem, vsem, osem,
 ):
     small = [
@@ -174,12 +189,13 @@
         )
         total = exact_dot(left, right, NT)
         base[p * ROWS : p * ROWS + ROWS] = total
-        last = CX * JP
-        down[8 * p : 8 * p + 8] = total[0:8]
-        down[16 + p : 17 + p] = total[8:9]
-        up[8 * p : 8 * p + 8] = total[last : last + 8]
-        up[16 + p : 17 + p] = total[last + 8 : last + 9]
-    for packet in (up, down):
+    turned = parity("gx") * (CX * JP)
+    for p in range(2):
+        for packet, place in ((odd, turned), (even, CX * JP - turned)):
+            start = pl.multiple_of(p * ROWS + place, JP)
+            packet[8 * p : 8 * p + 8] = base[pl.ds(start, 8), :]
+            packet[16 + p : 17 + p] = base[pl.ds(start + 8, 1), :]
+    for packet in (odd, even):
         for c in range(3):
             packet[18 + c : 19 + c] = pos[c]
         packet[21:22] = alive
@@ -198,7 +214,8 @@
         number = jnp.concatenate([number, number], axis=1)
         base[NUMBERS + JP * k : NUMBERS + JP * k + CY] = number
         if k == 0:
-            down[24:32] = number
+            odd[24:32] = number
+            even[24:32] = number
 
 
 def cell_sums(grid_shift, count, v, occ, axis_index, pos, vel, mass):
@@ -206,7 +223,7 @@
         sums_kernel,
         out_shape=(
             struct(BASE, FZ),
-            struct(24, FZ),
+            struct(32, FZ),
             struct(32, FZ),
         ),
         in_specs=[HBM] * 8,
@@ -249,55 +266,62 @@
     )(base)
 
 
-def add_x(part, up, down, full):
+def add_x(part, odd, even, full):
+    full[...] = part[...]
+    turned = parity("gx") * (CX * JP)
     for p in range(2):
-        base = p * ROWS
-        full[base : base + ROWS] = part[base : base + ROWS]
-        full[base : base + 8] += up[8 * p : 8 * p + 8]
-        full[base + 8 : base + 9] += up[16 + p : 17 + p]
-        last = base + CX * JP
-        full[last : last + 8] += down[8 * p : 8 * p + 8]
-        full[last + 8 : last + 9] += down[16 + p : 17 + p]
-
-
-def columns_kernel(part, up1, down1, state, numbers, up, down, full):
-    add_x(part, up1, down1, full)
+        for packet, place in ((odd, turned), (even, CX * JP - turned)):
+            start = pl.multiple_of(p * ROWS + place, JP)
+            full[pl.ds(start, 8), :] += packet[8 * p : 8 * p + 8]
+            full[pl.ds(start + 8, 1), :] += packet[16 + p : 17 + p]
+
+
+def later_x(odd, even, rows):
+    return jnp.where(parity("gx") == 1, odd[rows], even[rows])
+
+
+def columns_kernel(part, odd1, even1, state, numbers, odd, even, full, ends):
+    add_x(part, odd1, even1, full)
     for p in range(2):
-        down[9 * p : 9 * p + 9] = full[pl.ds(p * ROWS, KX, JP), :]
-        up[9 * p : 9 * p + 9] = full[pl.ds(p * ROWS + 8, KX, JP), :]
-    for packet in (up, down):
-        packet[18:22] = up1[18:22]
+        ends[0, 9 * p : 9 * p + 9] = full[pl.ds(p * ROWS, KX, JP), :]
+        ends[1, 9 * p : 9 * p + 9] = full[pl.ds(p * ROWS + 8, KX, JP), :]
+    side = parity("yz")
+    for packet, end in ((odd, side), (even, 1 - side)):
+        packet[0:18] = ends[end, 0:18]
+        packet[18:22] = odd1[18:22]
         packet[22:25] = state[0:3]
         packet[25:26] = state[7:8]
-        packet[26:30] = down1[18:22]
-    up[30:32] = jnp.zeros((2, FZ), jnp.float32)
-    down[30:38] = numbers[pl.ds(0, CX, JP), :]
-    down[38:39] = down1[24:25]
-    down[39:40] = jnp.zeros((1, FZ), jnp.float32)
-
-
-def columns(part, up1, down1, state, numbers):
+        packet[26:30] = even1[18:22]
+        packet[30:38] = numbers[pl.ds(0, CX, JP), :]
+        packet[38:39] = later_x(odd1, even1, slice(24, 25))
+        packet[39:40] = jnp.zeros((1, FZ), jnp.float32)
+
+
+def columns(part, odd1, even1, state, numbers):
     return pl.pallas_call(
         columns_kernel,
-        out_shape=(struct(32, FZ), struct(40, FZ)),
+        out_shape=(struct(40, FZ), struct(40, FZ)),
         in_specs=[IN_VMEM] * 5,
         out_specs=(IN_VMEM,) * 2,
-        scratch_shapes=[VMEM((2 * ROWS, FZ), jnp.float32)],
+        scratch_shapes=[VMEM((2 * ROWS, FZ), jnp.float32), VMEM((2, 24, FZ), jnp.float32)],
         compiler_params=pltpu.CompilerParams(vmem_limit_bytes=SMALL_LIMIT),
         cost_estimate=pl.CostEstimate(flops=100_000, bytes_accessed=500_000, transcendentals=0),
         name="columns",
-    )(part, up1, down1, state, numbers)
-
-
-def pair_force(own, others, rows, terms):
+    )(part, odd1, even1, state, numbers)
+
+
+def pair_force(count, own, others, rows, terms):
     for i, other in enumerate(others):
         for c in range(4):
             rows[4 * i + c] = jnp.broadcast_to(other[c], (8, FZ))
     column = jnp.concatenate(list(own) + [jnp.zeros((5, FZ), jnp.float32)], axis=0).T
-    for t in range(FZ // 16):
-        part = column[16 * t : 16 * t + 16]
+    rows_at = TILE // 8
+
+    def tile(t):
+        part = column[TILE * t : TILE * t + TILE]
         mine = [
-            jnp.broadcast_to(part[:, c : c + 1], (16, FZ)).reshape(2, 8, FZ) for c in range(3)
+            jnp.broadcast_to(part[:, c : c + 1], (TILE, FZ)).reshape(rows_at, 8, FZ)
+            for c in range(3)
         ]
         total = None
         for i in range(len(others)):
@@ -316,9 +340,16 @@
             new = (weight * dx, weight * dy, weight * dz)
             total = new if total is None else tuple(a + b for a, b in zip(total, new))
         for c in range(3):
-            terms[FZ * c + 16 * t : FZ * c + 16 * t + 16] = total[c].reshape(16, FZ)
+            terms[FZ * c + TILE * t : FZ * c + TILE * t + TILE] = total[c].reshape(TILE, FZ)
+
+    for t in range(FZ // TILE):
+        if TILE * t < 21:
+            tile(t)
+        else:
+            pl.when(TILE * t < count)(functools.partial(tile, t))
     ones = jnp.ones((8, FZ), jnp.bfloat16)
-    left = terms[...]
+    slot = lax.broadcasted_iota(jnp.int32, (FZ, FZ), 0) < count
+    left = jnp.where(jnp.concatenate([slot] * 3), terms[...], 0.0)
     back = None
     for part in range(3):
         piece = left.astype(jnp.bfloat16)
@@ -333,35 +364,40 @@
 
 
 def around(column, live):
+    toward_x = ((2 * parity("gx") - 1) * CX).astype(jnp.float32)
+    toward_y = ((2 * parity("yz") - 1) * CY).astype(jnp.float32)
     others = []
     for b in range(3):
         for a in range(3):
             x, y, z = column(b, a)
             limit = jnp.where(live(b, a) > 0.0, 1.0, -1.0)
-            others.append((x + (a - 1) * float(CX), y + (b - 1) * float(CY), z, limit))
+            others.append((x + (1 - a) * toward_x, y + (1 - b) * toward_y, z, limit))
     return others
 
 
-def advance(own, velocity, mass, others, rows, terms):
-    force = pair_force(own, others, rows, terms)
+def advance(count, own, velocity, mass, others, rows, terms):
+    live = live_row(count)
+    force = [jnp.where(live, f, 0.0) for f in pair_force(count, own, others, rows, terms)]
     velocity = [velocity[c] + timestep * force[c] / mass for c in range(3)]
     return [own[c] + timestep * velocity[c] for c in range(3)], velocity
 
 
 def fields_kernel(
-    part, up1, down1, up2, down2, state, numbers_in,
+    count, part, odd1, even1, odd2, even2, state, numbers_in,
     field_out, live_out, vel_out, pos_out,
     full, numbers, pair_rows, pair_terms,
 ):
-    add_x(part, up1, down1, full)
+    add_x(part, odd1, even1, full)
+    forward = parity("yz") == 1
     for p in range(2):
+        rows = slice(9 * p, 9 * p + 9)
         first = pl.ds(p * ROWS, KX, JP)
-        full[first, :] = full[first, :] + up2[9 * p : 9 * p + 9]
+        full[first, :] = full[first, :] + jnp.where(forward, even2[rows], odd2[rows])
         last = pl.ds(p * ROWS + 8, KX, JP)
-        full[last, :] = full[last, :] + down2[9 * p : 9 * p + 9]
+        full[last, :] = full[last, :] + jnp.where(forward, odd2[rows], even2[rows])
     numbers[...] = numbers_in[...]
-    numbers[JP * CX : JP * CX + 8] = down1[24:32]
-    numbers[pl.ds(8, KX, JP), :] = down2[30:39]
+    numbers[JP * CX : JP * CX + 8] = later_x(odd1, even1, slice(24, 32))
+    numbers[pl.ds(8, KX, JP), :] = jnp.where(forward, odd2[30:39], even2[30:39])
 
     lane = lax.broadcasted_iota(jnp.int32, (8, FZ), 1)
     number = (lane & (DIRECTIONS - 1)).astype(jnp.float32)
@@ -427,9 +463,9 @@
         if b == 1 and a == 1:
             return own + [alive_row]
         if b == 1:
-            source, base = (up1, 18) if a == 0 else (down1, 18)
+            source, base = (odd1, 18) if a == 0 else (even1, 18)
         else:
-            source, base = (up2 if b == 0 else down2), 18 + 4 * a
+            source, base = (odd2 if b == 0 else even2), 18 + 4 * a
         return [source[base + c : base + c + 1] for c in range(4)]
 
     live_out[9:16] = state[0:7]
@@ -437,7 +473,9 @@
         for a in range(3):
             live_out[3 * b + a : 3 * b + a + 1] = rows(b, a)[3]
     others = around(lambda b, a: rows(b, a)[:3], lambda b, a: rows(b, a)[3])
-    moved, velocity = advance(own, velocity, state[6:7], others, pair_rows, pair_terms)
+    moved, velocity = advance(
+        count[0, 0], own, velocity, state[6:7], others, pair_rows, pair_terms
+    )
     for c in range(3):
         vel_out[c : c + 1] = velocity[c]
         pos_out[c : c + 1] = moved[c]
@@ -445,11 +483,11 @@
     pos_out[3:4] = jnp.zeros((1, FZ), jnp.float32)
 
 
-def cell_fields(part, up1, down1, up2, down2, state, numbers):
+def cell_fields(count, part, odd1, even1, odd2, even2, state, numbers):
     return pl.pallas_call(
         fields_kernel,
         out_shape=(struct(6, ROWS, FZ), struct(16, FZ), struct(4, FZ), struct(4, FZ)),
-        in_specs=[IN_VMEM] * 7,
+        in_specs=[IN_SMEM] + [IN_VMEM] * 7,
         out_specs=(IN_VMEM,) * 4,
         scratch_shapes=[
             VMEM((2 * ROWS, FZ), jnp.float32),
@@ -459,22 +497,22 @@
         compiler_params=pltpu.CompilerParams(vmem_limit_bytes=SMALL_LIMIT),
         cost_estimate=pl.CostEstimate(flops=4_000_000, bytes_accessed=1_000_000, transcendentals=0),
         name="cell_fields",
-    )(part, up1, down1, up2, down2, state, numbers)
-
-
-def substep_moves(rest, own, column, up, down, vel, rows, terms):
+    )(count, part, odd1, even1, odd2, even2, state, numbers)
+
+
+def substep_moves(count, rest, own, column, odd, even, vel, rows, terms):
     mine = [own[c : c + 1] for c in range(3)]
     old = [vel[c : c + 1] for c in range(3)]
-    source = (up, column, down)
+    source = (odd, column, even)
     others = around(
         lambda b, a: [source[b][4 * a + c : 4 * a + c + 1] for c in range(3)],
         lambda b, a: rest[3 * b + a : 3 * b + a + 1],
     )
-    return advance(mine, old, rest[15:16], others, rows, terms)
-
-
-def substep_kernel(rest, own, column, up, down, vel, vel_out, pos_out, rows, terms):
-    moved, velocity = substep_moves(rest, own, column, up, down, vel, rows, terms)
+    return advance(count[0, 0], mine, old, rest[15:16], others, rows, terms)
+
+
+def substep_kernel(count, rest, own, column, odd, even, vel, vel_out, pos_out, rows, terms):
+    moved, velocity = substep_moves(count, rest, own, column, odd, even, vel, rows, terms)
     for c in range(3):
         vel_out[c : c + 1] = velocity[c]
         pos_out[c : c + 1] = moved[c]
@@ -482,41 +520,52 @@
     pos_out[3:4] = jnp.zeros((1, FZ), jnp.float32)
 
 
-def last_kernel(rest, own, column, up, down, vel, vel_out, pos_out, rows, terms):
-    moved, velocity = substep_moves(rest, own, column, up, down, vel, rows, terms)
+def last_kernel(count, rest, own, column, odd, even, vel, vel_out, pos_out, rows, terms):
+    moved, velocity = substep_moves(count, rest, own, column, odd, even, vel, rows, terms)
     keep = rest[4:5] > 0.0
     for c in range(3):
         pos_out[c] = jnp.where(keep, moved[c], rest[9 + c : 10 + c])
         vel_out[c] = jnp.where(keep, velocity[c], rest[12 + c : 13 + c])
 
 
-def substep(kernel, shape, rest, own, column, up, down, vel):
+def substep(kernel, shape, count, rest, own, column, odd, even, vel):
     return pl.pallas_call(
         kernel,
         out_shape=(struct(*shape), struct(*shape)),
-        in_specs=[IN_VMEM] * 6,
+        in_specs=[IN_SMEM] + [IN_VMEM] * 6,
         out_specs=(IN_VMEM,) * 2,
         scratch_shapes=PAIR_SCRATCH,
         compiler_params=pltpu.CompilerParams(vmem_limit_bytes=SMALL_LIMIT),
         cost_estimate=pl.CostEstimate(flops=4_000_000, bytes_accessed=30_000, transcendentals=0),
         name="substep",
-    )(rest, own, column, up, down, vel)
-
-
-def turn_kernel(shift_at, v_at, occ_at, field, out_at, shift, v, occ, out, twice, wide, sem, vsem, osem, wsem):
-    first = pltpu.make_async_copy(shift_at, shift, sem.at[0])
-    first.start()
-    large = []
+    )(count, rest, own, column, odd, even, vel)
+
+
+def turn_kernel(ks, shift, v, occ, field, *refs):
+    out_at, out, twice, wide, wsem = refs[-5:]
+    sx, sy, sz = shift[0], shift[1], shift[2]
+    places = []
     stores = []
-    for q in range(CX):
-        part = pl.ds(SUB * q, SUB)
-        large.append(pltpu.make_async_copy(occ_at.at[part], occ.at[part], osem.at[q]))
-        large.append(pltpu.make_async_copy(v_at.at[:, part], v.at[:, part], vsem.at[q]))
-        stores.append(pltpu.make_async_copy(out.at[:, part], out_at.at[:, part], wsem.at[q]))
-    for copy in large:
-        copy.start()
-    first.wait()
-    sx, sy, sz = shift[0], shift[1], shift[2]
+    for i, k in enumerate(ks):
+        if k < CX:
+            places += [k * SUB - sx + j for j in range(SUB)]
+            here, there = pl.ds(SUB * i, SUB), pl.ds(SUB * k - sx, SUB)
+            stores.append(
+                [pltpu.make_async_copy(out.at[:, here], out_at.at[:, there], wsem.at[SUB * i])]
+            )
+        else:
+            around_end = [(FX - sx + j) & (FX - 1) for j in range(SUB)]
+            places += around_end
+            stores.append(
+                [
+                    pltpu.make_async_copy(
+                        out.at[:, pl.ds(SUB * i + j, 1)],
+                        out_at.at[:, pl.ds(x, 1)],
+                        wsem.at[SUB * i + j],
+                    )
+                    for j, x in enumerate(around_end)
+                ]
+            )
     source = lax.broadcasted_iota(jnp.int32, (CZ, FZ), 0)
     layer = lax.broadcasted_iota(jnp.int32, (CZ, FZ), 1)
     spread = (((layer + sz) & (FZ - 1)) >> 1 == source).astype(jnp.float32)
@@ -525,78 +574,89 @@
         [jnp.concatenate([spread, none], axis=1), jnp.concatenate([none, spread], axis=1)],
         axis=0,
     )
+    layers = list(ks) + ([0] if CX in ks else [])
     for f in range(6):
-        both = exact_dot(field[f], right, NN)
+        left = jnp.concatenate([field[f, JP * k : JP * k + JP] for k in layers])
+        both = exact_dot(left, right, NN)
         wide[2 * f] = both[:, :FZ]
         wide[2 * f + 1] = both[:, FZ:]
     row = lax.broadcasted_iota(jnp.int32, (8, FZ), 0)
     slot = (row & 1).astype(jnp.float32)
     low = row < 8 - 2 * sy
 
-    for k in range(KX):
-        if k < CX:
-            large[2 * k].wait()
-            store_twice(occ, twice, k)
-            large[2 * k + 1].wait()
-
-        def column(t, carry, k=k):
-            f = [
-                jnp.where(
-                    low, wide[i, pl.ds(k * JP + t, 1), :], wide[i, pl.ds(k * JP + t + 1, 1), :]
+    def turn_layer(at, planes, t):
+        f = [
+            jnp.where(low, wide[i, pl.ds(JP * at + t, 1), :], wide[i, pl.ds(JP * at + t + 1, 1), :])
+            for i in range(12)
+        ]
+        rows = pl.ds(pl.multiple_of(8 * t, 8), 8)
+
+        def plane(n, x):
+            live = twice[pl.ds(pl.multiple_of(n * 2 * FY + 8 * t, 8), 8), :] > slot
+            old = [v[c, x, rows, :] for c in range(3)]
+            rel = [old[c] - f[9 + c] for c in range(3)]
+            for c in range(3):
+                new = f[9 + c] + (
+                    f[3 * c] * rel[0] + f[3 * c + 1] * rel[1] + f[3 * c + 2] * rel[2]
                 )
-                for i in range(12)
-            ]
-            rows = pl.ds(pl.multiple_of(8 * t, 8), 8)
-
-            def plane(x, carry):
-                live = twice[pl.ds(pl.multiple_of(x * 2 * FY + 8 * t, 8), 8), :] > slot
-                old = [v[c, x, rows, :] for c in range(3)]
-                rel = [old[c] - f[9 + c] for c in range(3)]
-                for c in range(3):
-                    new = f[9 + c] + (
-                        f[3 * c] * rel[0] + f[3 * c + 1] * rel[1] + f[3 * c + 2] * rel[2]
-                    )
-                    out[c, x, rows, :] = jnp.where(live, new, old[c])
-                return carry
-
-            if k == 0:
-                lax.fori_loop(0, SUB - sx, plane, 0)
-            elif k == CX:
-                lax.fori_loop(FX - sx, FX, plane, 0)
+                out[c, n, rows, :] = jnp.where(live, new, old[c])
+
+        planes(plane)
+
+    for n, x in enumerate(places):
+        slots = occ[x].astype(jnp.float32)
+        twice[pl.ds(2 * FY * n, FY, 2), :] = slots
+        twice[pl.ds(2 * FY * n + 1, FY, 2), :] = slots
+
+    for i, k in enumerate(ks):
+
+        def column(t, carry, i=i, k=k):
+            def some(first, last):
+                def run(plane):
+                    def step(j, carry):
+                        plane(SUB * i + j, (FX - sx + j) & (FX - 1))
+                        return carry
+
+                    lax.fori_loop(first, last, step, 0)
+
+                return run
+
+            if k < CX:
+                turn_layer(
+                    i, lambda plane: [plane(SUB * i + j, places[SUB * i + j]) for j in range(SUB)], t
+                )
             else:
-                for j in range(SUB):
-                    plane(k * SUB - sx + j, 0)
+                turn_layer(i, some(0, sx), t)
+                turn_layer(i + 1, some(sx, SUB), t)
             return carry
 
         lax.fori_loop(0, CY, column, 0)
-        if k:
-            stores[k - 1].start()
-    for copy in stores:
-        copy.wait()
-
-
-def turn_solvent(grid_shift, v, occ, field):
+        for copy in stores[i]:
+            copy.start()
+    for group in stores:
+        for copy in group:
+            copy.wait()
+
+
+def turn_solvent(ks, grid_shift, v, occ, field, done=None):
+    planes = SUB * len(ks)
+    layers = len(ks) + (CX in ks)
     return pl.pallas_call(
-        turn_kernel,
+        functools.partial(turn_kernel, ks),
         out_shape=struct(*v.shape),
-        in_specs=[HBM, HBM, HBM, IN_VMEM],
+        in_specs=[IN_SMEM, IN_VMEM, IN_VMEM, IN_VMEM] + [HBM] * (done is not None),
         out_specs=HBM,
+        input_output_aliases={} if done is None else {4: 0},
         scratch_shapes=[
-            SMEM((3,), jnp.int32),
-            VMEM((3, FX, 2 * FY, FZ), jnp.float32),
-            VMEM((FX, FY, FZ), jnp.int32),
-            VMEM((3, FX, 2 * FY, FZ), jnp.float32),
-            VMEM((2 * FX * FY, FZ), jnp.float32),
-            VMEM((12, ROWS, FZ), jnp.float32),
-            DMA((1,)),
-            DMA((CX,)),
-            DMA((CX,)),
-            DMA((CX,)),
+            VMEM((3, planes, 2 * FY, FZ), jnp.float32),
+            VMEM((2 * planes * FY, FZ), jnp.float32),
+            VMEM((12, JP * layers, FZ), jnp.float32),
+            DMA((planes,)),
         ],
         compiler_params=pltpu.CompilerParams(vmem_limit_bytes=TURN_LIMIT),
-        cost_estimate=pl.CostEstimate(flops=8_000_000, bytes_accessed=7_000_000, transcendentals=0),
+        cost_estimate=pl.CostEstimate(flops=3_000_000, bytes_accessed=1_300_000, transcendentals=0),
         name="turn_solvent",
-    )(grid_shift, v, occ, field)
+    )(grid_shift, v, occ, field, *([] if done is None else [done]))
 
 
 def per_device(
@@ -615,21 +675,30 @@
     mass = colloid_mass
     count = colloid_count
 
-    base, up, down = cell_sums(grid_shift, count, v, occupancy, axis_index, pos, vel, mass)
-    up1, down1 = shifted(up, "gx", 1), shifted(down, "gx", -1)
+    base, odd, even = cell_sums(grid_shift, count, v, occupancy, axis_index, pos, vel, mass)
+    odd1, even1 = swap_both(odd, even, "gx")
     part, state, numbers = prepare(base)
-    up, down = columns(part, up1, down1, state, numbers)
-    up2, down2 = shifted(up, "yz", 1), shifted(down, "yz", -1)
-    field, rest, velocity, position = cell_fields(part, up1, down1, up2, down2, state, numbers)
-    solvent_out = turn_solvent(grid_shift, v, occupancy, field)
+    odd, even = columns(part, odd1, even1, state, numbers)
+    odd2, even2 = swap_both(odd, even, "yz")
+    field, rest, velocity, position = cell_fields(
+        count, part, odd1, even1, odd2, even2, state, numbers
+    )
+    solvent_out = None
     for step in range(1, SUBSTEPS):
-        column = jnp.concatenate([shifted(position, "gx", 1), position, shifted(position, "gx", -1)])
-        up, down = shifted(column, "yz", 1), shifted(column, "yz", -1)
+        ks = TURNED[step - 1]
+        if step > 1:
+            position, solvent_out = lax.optimization_barrier((position, solvent_out))
+        solvent_out = turn_solvent(ks, grid_shift, v, occupancy, field, solvent_out)
+        odd, even = swap_both(position, position, "gx")
+        odd, solvent_out = lax.optimization_barrier((odd, solvent_out))
+        column = jnp.concatenate([odd, position, even])
+        odd, even = swap_both(column, column, "yz")
+        odd, velocity = lax.optimization_barrier((odd, velocity))
         kernel, shape = (
             (substep_kernel, (4, FZ)) if step < SUBSTEPS - 1 else (last_kernel, (3, 1, FZ))
         )
         velocity, position = substep(
-            kernel, shape, rest, position, column, up, down, velocity
+            kernel, shape, count, rest, position, column, odd, even, velocity
         )
     return (
         solvent_out.reshape(solvent_vel.shape),

time: 73.5 us -> 65.8 us (0.90)
  the two profiles are of different devices: /device:TPU:1 before, /device:TPU:32 now
where the time goes in v1:
time: 65.8 us; the launch traced here: 65.6 us
  waiting for transfers between devices  25.3 us (38%)
  starting transfers between devices  22.6 us (34%)
  Pallas kernels  14.1 us (21%)
  local copies, waits for them, and re-layouts  1.98 us (3%)
  between operations  1.55 us (2%)
    ppermute x16, waiting for transfers between devices, swapped(): return lax.ppermute(value, axis, pairs)  25.3 us
    ppermute x16, starting transfers between devices, swapped(): return lax.ppermute(value, axis, pairs)  22.6 us
    pallas_call x3, Pallas kernels, turn_solvent(): pl.pallas_call(functools.partial(turn_kernel, ks), out_shape=struct(*v.sh...  6.78 us
    pallas_call x1, Pallas kernels, cell_sums(): pl.pallas_call(sums_kernel, out_shape=(struct(BASE, FZ), struct(32, FZ),...  3.66 us
    pallas_call x3, Pallas kernels, substep(): pl.pallas_call(kernel, out_shape=(struct(*shape), struct(*shape)), in_spe...  2.58 us
    unnamed x8, local copies, waits for them, and re-layouts  1.98 us
  transfers between devices with their start and end apart: 16, of which 9 were waited for; matrix products, arithmetic and copies ran while one was open for 0% of the time, Pallas kernels for 10%

profile of v1, /device:TPU:32, one launch (start us, length us, event | category | flops | bytes accessed | tf_op | source)
XLA Modules:
  0.0 65.6 jit_solution(9841404896047863271)
XLA Ops:
  0.6 0.0 copy-start.3
  0.6 0.0 copy-start
  1.4 3.7 %cell_sums.1 = (f32[448,128]{1,0:T(8,128)}, f32[32,128]{1,0:T(8,128)}, f32[32,128]{1,0:T(8,128)}) custom-call(s32[3]{0:T(128)} %shift.5, s32[1,1]{1,0:T(1,128)S(6)} %copy.17.count_at.count, f32[3,32,64,128]{3,2,1,0:T(8,128)} %bitcast.10, s32[32,32,128]{2,1,0:T(8,128)} %occ.5, s32[8,8,64]{2,1,0:T(8,128)} %axis_at.1, f32[3,1,128]{2,1,0:T(1,128)} %bitcast.15, ...), custom_call_target="tpu_custom_call" | custom-call | flops 4000000 | bytes 3700000 | tf_op jit(solution)/shard_map/cell_sums/pallas_call | solution.py:222
  5.1 7.9 %collective-permute-start = (f32[32,128]{1,0:T(8,128)}, f32[32,128]{1,0:T(8,128)S(1)}, u32[]{:S(2)}, u32[]{:S(2)}) collective-permute-start(f32[32,128]{1,0:T(8,128)} %get-tuple-element.39), channel_id=1, source_target_pairs={{16,32},{32,16},{48,64},{64,48},{80,96},{96,80},{112,128},{128,112... | collective-permute-start | bytes 49160 | tf_op jit(solution)/shard_map/ppermute | solution.py:57
  13.1 0.0 collective-permute-start.1
  13.1 0.0 copy-start.2
  13.1 0.9 %copy-done.2 = f32[448,128]{1,0:T(8,128)S(1)} copy-done((f32[448,128]{1,0:T(8,128)S(1)}, f32[448,128]{1,0:T(8,128)}, u32[]{:S(2)}) %copy-start.2) | copy-done | bytes 229400
  14.0 1.0 %collective-permute-done.odd1 = f32[32,128]{1,0:T(8,128)S(1)} collective-permute-done((f32[32,128]{1,0:T(8,128)}, f32[32,128]{1,0:T(8,128)S(1)}, u32[]{:S(2)}, u32[]{:S(2)}) %collective-permute-start) | collective-permute-done | bytes 16416 | tf_op jit(solution)/shard_map/ppermute | solution.py:57
  15.0 2.0 %collective-permute-done.1.even1 = f32[32,128]{1,0:T(8,128)S(1)} collective-permute-done((f32[32,128]{1,0:T(8,128)}, f32[32,128]{1,0:T(8,128)S(1)}, u32[]{:S(2)}, u32[]{:S(2)}) %collective-permute-start.1) | collective-permute-done | bytes 16416 | tf_op jit(solution)/shard_map/ppermute | solution.py:57
  17.0 1.3 %collective-permute-start.2 = (f32[40,128]{1,0:T(8,128)S(1)}, f32[40,128]{1,0:T(8,128)S(1)}, u32[]{:S(2)}, u32[]{:S(2)}) collective-permute-start(f32[40,128]{1,0:T(8,128)S(1)} %get-tuple-element.43), channel_id=1, source_target_pairs={{1,2},{2,1},{3,4},{4,3},{5,6},{6,5},{7,8},{8,7},{9,10},{10,9},{11,... | collective-permute-start | bytes 61448 | tf_op jit(solution)/shard_map/ppermute | solution.py:57
  18.3 0.4 collective-permute-start.3
  18.7 3.7 %collective-permute-done.2.odd2 = f32[40,128]{1,0:T(8,128)S(1)} collective-permute-done((f32[40,128]{1,0:T(8,128)S(1)}, f32[40,128]{1,0:T(8,128)S(1)}, u32[]{:S(2)}, u32[]{:S(2)}) %collective-permute-start.2) | collective-permute-done | bytes 20512 | tf_op jit(solution)/shard_map/ppermute | solution.py:57
  22.4 0.0 collective-permute-done.3.even2
  22.4 1.0 %cell_fields.1 = (f32[6,144,128]{2,1,0:T(8,128)S(1)}, f32[16,128]{1,0:T(8,128)S(1)}, f32[4,128]{1,0:T(4,128)S(1)}, f32[4,128]{1,0:T(4,128)S(1)}) custom-call(s32[1,1]{1,0:T(1,128)S(6)} %copy.17.count_at.count, f32[288,128]{1,0:T(8,128)S(1)} %get-tuple-element.38.part, f32[32,128]{1,0:T(8,128)S(1)} %collective-permute-done.odd1, ...), custom_call_target="tpu_custom_call" | custom-call | flops 4000000 | bytes 1000000 | tf_op jit(solution)/shard_map/cell_fields/pallas_call | solution.py:487
  23.5 4.1 %collective-permute-start.4 = (f32[4,128]{1,0:T(4,128)S(1)}, f32[4,128]{1,0:T(4,128)S(1)}, u32[]{:S(2)}, u32[]{:S(2)}) collective-permute-start(f32[4,128]{1,0:T(4,128)S(1)} %get-tuple-element.46.own), channel_id=1, source_target_pairs={{16,32},{32,16},{48,64},{64,48},{80,96},{96,80},{112,128},{128,112... | collective-permute-start | bytes 6152 | tf_op jit(solution)/shard_map/ppermute | solution.py:57
  27.6 0.0 collective-permute-start.5
  27.6 0.0 copy-done.3
  27.6 0.0 copy-done
  27.6 0.0 copy-start.1
  27.6 1.0 %copy-done.1 = s32[32,32,128]{2,1,0:T(8,128)S(1)} copy-done((s32[32,32,128]{2,1,0:T(8,128)S(1)}, s32[32,32,128]{2,1,0:T(8,128)}, u32[]{:S(2)}) %copy-start.1) | copy-done | bytes 524312
  28.7 2.2 %turn_solvent.3.refs_0_ = f32[3,32,64,128]{3,2,1,0:T(8,128)} custom-call(s32[3]{0:T(128)S(1)} %copy-done.3, f32[3,32,64,128]{3,2,1,0:T(8,128)S(1)} %bitcast.11, s32[32,32,128]{2,1,0:T(8,128)S(1)} %copy-done.1, f32[6,144,128]{2,1,0:T(8,128)S(1)} %get-tuple-element.47.field), custom_call_target="tpu_custom_call" | custom-call | flops 3000000 | bytes 1300000 | tf_op jit(solution)/shard_map/turn_solvent/pallas_call | solution.py:644
  30.9 0.5 collective-permute-done.4
  31.4 0.0 collective-permute-done.5
  31.4 0.8 %collective-permute-start.6 = (f32[12,128]{1,0:T(8,128)S(1)}, f32[12,128]{1,0:T(8,128)S(1)}, u32[]{:S(2)}, u32[]{:S(2)}) collective-permute-start(f32[12,128]{1,0:T(8,128)S(1)} %pad_maximum_fusion.column), channel_id=1, source_target_pairs={{1,2},{2,1},{3,4},{4,3},{5,6},{6,5},{7,8},{8,7},{9,10},{10,9},{11,... | collective-permute-start | bytes 18440 | tf_op jit(solution)/shard_map/ppermute | solution.py:57
  32.2 0.0 collective-permute-start.7
  32.2 4.4 %collective-permute-done.6.odd = f32[12,128]{1,0:T(8,128)S(1)} collective-permute-done((f32[12,128]{1,0:T(8,128)S(1)}, f32[12,128]{1,0:T(8,128)S(1)}, u32[]{:S(2)}, u32[]{:S(2)}) %collective-permute-start.6) | collective-permute-done | bytes 6176 | tf_op jit(solution)/shard_map/ppermute | solution.py:57
  36.7 0.0 collective-permute-done.7.even
  36.7 0.7 %substep.3 = (f32[4,128]{1,0:T(4,128)S(1)}, f32[4,128]{1,0:T(4,128)S(1)}) custom-call(s32[1,1]{1,0:T(1,128)S(6)} %copy.17.count_at.count, f32[16,128]{1,0:T(8,128)S(1)} %get-tuple-element.45.rest, f32[4,128]{1,0:T(4,128)S(1)} %get-tuple-element.46.own, f32[12,128]{1,0:T(8,128)S(1)} %pad_maximum_fusion.column, f32[12,128]{1,0:T(8,128)S(1)} %collective-permute-done.6.odd, ...), custom_call_target="tpu_custom_call" | custom-call | flops 4000000 | bytes 30000 | tf_op jit(solution)/shard_map/substep/pallas_call | solution.py:532
  37.3 3.9 %collective-permute-start.8 = (f32[4,128]{1,0:T(4,128)S(1)}, f32[4,128]{1,0:T(4,128)S(1)}, u32[]{:S(2)}, u32[]{:S(2)}) collective-permute-start(f32[4,128]{1,0:T(4,128)S(1)} %get-tuple-element.54.own), channel_id=1, source_target_pairs={{16,32},{32,16},{48,64},{64,48},{80,96},{96,80},{112,128},{128,112... | collective-permute-start | bytes 6152 | tf_op jit(solution)/shard_map/ppermute | solution.py:57
  41.3 0.0 collective-permute-start.9
  41.3 2.2 %turn_solvent.4.refs_0_ = f32[3,32,64,128]{3,2,1,0:T(8,128)} custom-call(s32[3]{0:T(128)S(1)} %copy-done.3, f32[3,32,64,128]{3,2,1,0:T(8,128)S(1)} %bitcast.12, s32[32,32,128]{2,1,0:T(8,128)S(1)} %copy-done.1, f32[6,144,128]{2,1,0:T(8,128)S(1)} %get-tuple-element.47.field, f32[3,32,64,128]{3,2,1,0:T(8,128)} %turn_solvent.3.refs_0_), custom_call_target="tpu_custom_call", output_to_operand_aliasing={{}: (4, {})} | custom-call | flops 3000000 | bytes 1300000 | tf_op jit(solution)/shard_map/turn_solvent/pallas_call | solution.py:644
  43.5 1.7 %collective-permute-done.8 = f32[4,128]{1,0:T(4,128)S(1)} collective-permute-done((f32[4,128]{1,0:T(4,128)S(1)}, f32[4,128]{1,0:T(4,128)S(1)}, u32[]{:S(2)}, u32[]{:S(2)}) %collective-permute-start.8) | collective-permute-done | bytes 2080 | tf_op jit(solution)/shard_map/ppermute | solution.py:57
  45.2 0.0 collective-permute-done.9
  45.2 0.1 collective-permute-start.10
  45.3 0.1 collective-permute-start.11
  45.4 5.1 %collective-permute-done.10.odd = f32[12,128]{1,0:T(8,128)S(1)} collective-permute-done((f32[12,128]{1,0:T(8,128)S(1)}, f32[12,128]{1,0:T(8,128)S(1)}, u32[]{:S(2)}, u32[]{:S(2)}) %collective-permute-start.10) | collective-permute-done | bytes 6176 | tf_op jit(solution)/shard_map/ppermute | solution.py:57
  50.5 0.0 collective-permute-done.11.even
  50.5 0.7 %substep.4 = (f32[4,128]{1,0:T(4,128)S(1)}, f32[4,128]{1,0:T(4,128)S(1)}) custom-call(s32[1,1]{1,0:T(1,128)S(6)} %copy.17.count_at.count, f32[16,128]{1,0:T(8,128)S(1)} %get-tuple-element.45.rest, f32[4,128]{1,0:T(4,128)S(1)} %get-tuple-element.54.own, f32[12,128]{1,0:T(8,128)S(1)} %pad_maximum_fusion.1.column, f32[12,128]{1,0:T(8,128)S(1)} %collective-permute-done.10.odd, ...), custom_call_target="tpu_custom_call" | custom-call | flops 4000000 | bytes 30000 | tf_op jit(solution)/shard_map/substep/pallas_call | solution.py:532
  51.2 3.7 %collective-permute-start.12 = (f32[4,128]{1,0:T(4,128)S(1)}, f32[4,128]{1,0:T(4,128)S(1)}, u32[]{:S(2)}, u32[]{:S(2)}) collective-permute-start(f32[4,128]{1,0:T(4,128)S(1)} %get-tuple-element.62.own), channel_id=1, source_target_pairs={{16,32},{32,16},{48,64},{64,48},{80,96},{96,80},{112,128},{128,112... | collective-permute-start | bytes 6152 | tf_op jit(solution)/shard_map/ppermute | solution.py:57
  54.9 0.0 collective-permute-start.13
  54.9 2.3 %turn_solvent.5 = f32[3,32,64,128]{3,2,1,0:T(8,128)} custom-call(s32[3]{0:T(128)S(1)} %copy-done.3, f32[3,32,64,128]{3,2,1,0:T(8,128)S(1)} %bitcast.13, s32[32,32,128]{2,1,0:T(8,128)S(1)} %copy-done.1, f32[6,144,128]{2,1,0:T(8,128)S(1)} %get-tuple-element.47.field, f32[3,32,64,128]{3,2,1,0:T(8,128)} %turn_solvent.4.refs_0_), custom_call_target="tpu_custom_call", output_to_operand_aliasing={{}: (4, {})} | custom-call | flops 3000000 | bytes 1300000 | tf_op jit(solution)/shard_map/turn_solvent/pallas_call | solution.py:644
  57.2 1.8 %collective-permute-done.12 = f32[4,128]{1,0:T(4,128)S(1)} collective-permute-done((f32[4,128]{1,0:T(4,128)S(1)}, f32[4,128]{1,0:T(4,128)S(1)}, u32[]{:S(2)}, u32[]{:S(2)}) %collective-permute-start.12) | collective-permute-done | bytes 2080 | tf_op jit(solution)/shard_map/ppermute | solution.py:57
  59.0 0.0 collective-permute-done.13
  59.1 0.1 collective-permute-start.14
  59.2 0.1 collective-permute-start.15
  59.3 5.1 %collective-permute-done.14.odd = f32[12,128]{1,0:T(8,128)S(1)} collective-permute-done((f32[12,128]{1,0:T(8,128)S(1)}, f32[12,128]{1,0:T(8,128)S(1)}, u32[]{:S(2)}, u32[]{:S(2)}) %collective-permute-start.14) | collective-permute-done | bytes 6176 | tf_op jit(solution)/shard_map/ppermute | solution.py:57
  64.3 0.0 collective-permute-done.15.even
  64.3 1.3 %substep.5 = (f32[3,1,128]{2,1,0:T(1,128)}, f32[3,1,128]{2,1,0:T(1,128)}) custom-call(s32[1,1]{1,0:T(1,128)S(6)} %copy.17.count_at.count, f32[16,128]{1,0:T(8,128)S(1)} %get-tuple-element.45.rest, f32[4,128]{1,0:T(4,128)S(1)} %get-tuple-element.62.own, f32[12,128]{1,0:T(8,128)S(1)} %pad_maximum_fusion.2.column, f32[12,128]{1,0:T(8,128)S(1)} %collective-permute-done.14.odd, ...), custom_call_target="tpu_custom_call" | custom-call | flops 4000000 | bytes 30000 | tf_op jit(solution)/shard_map/substep/pallas_call | solution.py:532
  (5 shorter events, 0.1 us)
Async XLA Ops:
  0.6 27.0 %copy-start.3 = (s32[3]{0:T(128)S(1)}, s32[3]{0:T(128)}, u32[]{:S(2)}) copy-start(s32[3]{0:T(128)} %shift.5) | copy-start | bytes 40
  0.6 27.0 %copy-start = (f32[3,32,32,2,128]{4,3,2,1,0:T(2,128)S(1)}, f32[3,32,32,2,128]{4,3,2,1,0:T(2,128)}, u32[]{:S(2)}) copy-start(f32[3,32,32,2,128]{4,3,2,1,0:T(2,128)} %param.8) | copy-start | bytes 9437188
  5.1 9.9 %collective-permute-start = (f32[32,128]{1,0:T(8,128)}, f32[32,128]{1,0:T(8,128)S(1)}, u32[]{:S(2)}, u32[]{:S(2)}) collective-permute-start(f32[32,128]{1,0:T(8,128)} %get-tuple-element.39), channel_id=1, source_target_pairs={{16,32},{32,16},{48,64},{64,48},{80,96},{96,80},{112,128},{128,112... | collective-permute-start | bytes 49160 | tf_op jit(solution)/shard_map/ppermute | solution.py:57
  13.1 3.9 %collective-permute-start.1 = (f32[32,128]{1,0:T(8,128)}, f32[32,128]{1,0:T(8,128)S(1)}, u32[]{:S(2)}, u32[]{:S(2)}) collective-permute-start(f32[32,128]{1,0:T(8,128)} %get-tuple-element.40), channel_id=1, source_target_pairs={{0,16},{16,0},{32,48},{48,32},{64,80},{80,64},{96,112},{112,96},{1... | collective-permute-start | bytes 49160 | tf_op jit(solution)/shard_map/ppermute | solution.py:57
  13.1 0.9 %copy-start.2 = (f32[448,128]{1,0:T(8,128)S(1)}, f32[448,128]{1,0:T(8,128)}, u32[]{:S(2)}) copy-start(f32[448,128]{1,0:T(8,128)} %get-tuple-element.37.base) | copy-start | bytes 688132
  17.0 5.4 %collective-permute-start.2 = (f32[40,128]{1,0:T(8,128)S(1)}, f32[40,128]{1,0:T(8,128)S(1)}, u32[]{:S(2)}, u32[]{:S(2)}) collective-permute-start(f32[40,128]{1,0:T(8,128)S(1)} %get-tuple-element.43), channel_id=1, source_target_pairs={{1,2},{2,1},{3,4},{4,3},{5,6},{6,5},{7,8},{8,7},{9,10},{10,9},{11,... | collective-permute-start | bytes 61448 | tf_op jit(solution)/shard_map/ppermute | solution.py:57
  18.3 4.1 %collective-permute-start.3 = (f32[40,128]{1,0:T(8,128)S(1)}, f32[40,128]{1,0:T(8,128)S(1)}, u32[]{:S(2)}, u32[]{:S(2)}) collective-permute-start(f32[40,128]{1,0:T(8,128)S(1)} %get-tuple-element.44), channel_id=1, source_target_pairs={{0,1},{1,0},{2,3},{3,2},{4,5},{5,4},{6,7},{7,6},{8,9},{9,8},{10,11... | collective-permute-start | bytes 61448 | tf_op jit(solution)/shard_map/ppermute | solution.py:57
  23.5 7.9 %collective-permute-start.4 = (f32[4,128]{1,0:T(4,128)S(1)}, f32[4,128]{1,0:T(4,128)S(1)}, u32[]{:S(2)}, u32[]{:S(2)}) collective-permute-start(f32[4,128]{1,0:T(4,128)S(1)} %get-tuple-element.46.own), channel_id=1, source_target_pairs={{16,32},{32,16},{48,64},{64,48},{80,96},{96,80},{112,128},{128,112... | collective-permute-start | bytes 6152 | tf_op jit(solution)/shard_map/ppermute | solution.py:57
  27.6 3.8 %collective-permute-start.5 = (f32[4,128]{1,0:T(4,128)S(1)}, f32[4,128]{1,0:T(4,128)S(1)}, u32[]{:S(2)}, u32[]{:S(2)}) collective-permute-start(f32[4,128]{1,0:T(4,128)S(1)} %get-tuple-element.46.own), channel_id=1, source_target_pairs={{0,16},{16,0},{32,48},{48,32},{64,80},{80,64},{96,112},{112,96},{1... | collective-permute-start | bytes 6152 | tf_op jit(solution)/shard_map/ppermute | solution.py:57
  27.6 1.0 %copy-start.1 = (s32[32,32,128]{2,1,0:T(8,128)S(1)}, s32[32,32,128]{2,1,0:T(8,128)}, u32[]{:S(2)}) copy-start(s32[32,32,128]{2,1,0:T(8,128)} %occ.5) | copy-start | bytes 1572868
  31.4 5.3 %collective-permute-start.6 = (f32[12,128]{1,0:T(8,128)S(1)}, f32[12,128]{1,0:T(8,128)S(1)}, u32[]{:S(2)}, u32[]{:S(2)}) collective-permute-start(f32[12,128]{1,0:T(8,128)S(1)} %pad_maximum_fusion.column), channel_id=1, source_target_pairs={{1,2},{2,1},{3,4},{4,3},{5,6},{6,5},{7,8},{8,7},{9,10},{10,9},{11,... | collective-permute-start | bytes 18440 | tf_op jit(solution)/shard_map/ppermute | solution.py:57
  32.2 4.4 %collective-permute-start.7 = (f32[12,128]{1,0:T(8,128)S(1)}, f32[12,128]{1,0:T(8,128)S(1)}, u32[]{:S(2)}, u32[]{:S(2)}) collective-permute-start(f32[12,128]{1,0:T(8,128)S(1)} %pad_maximum_fusion.column), channel_id=1, source_target_pairs={{0,1},{1,0},{2,3},{3,2},{4,5},{5,4},{6,7},{7,6},{8,9},{9,8},{10,11... | collective-permute-start | bytes 18440 | tf_op jit(solution)/shard_map/ppermute | solution.py:57
  37.3 7.9 %collective-permute-start.8 = (f32[4,128]{1,0:T(4,128)S(1)}, f32[4,128]{1,0:T(4,128)S(1)}, u32[]{:S(2)}, u32[]{:S(2)}) collective-permute-start(f32[4,128]{1,0:T(4,128)S(1)} %get-tuple-element.54.own), channel_id=1, source_target_pairs={{16,32},{32,16},{48,64},{64,48},{80,96},{96,80},{112,128},{128,112... | collective-permute-start | bytes 6152 | tf_op jit(solution)/shard_map/ppermute | solution.py:57
  41.3 4.0 %collective-permute-start.9 = (f32[4,128]{1,0:T(4,128)S(1)}, f32[4,128]{1,0:T(4,128)S(1)}, u32[]{:S(2)}, u32[]{:S(2)}) collective-permute-start(f32[4,128]{1,0:T(4,128)S(1)} %get-tuple-element.54.own), channel_id=1, source_target_pairs={{0,16},{16,0},{32,48},{48,32},{64,80},{80,64},{96,112},{112,96},{1... | collective-permute-start | bytes 6152 | tf_op jit(solution)/shard_map/ppermute | solution.py:57
  45.2 5.3 %collective-permute-start.10 = (f32[12,128]{1,0:T(8,128)S(1)}, f32[12,128]{1,0:T(8,128)S(1)}, u32[]{:S(2)}, u32[]{:S(2)}) collective-permute-start(f32[12,128]{1,0:T(8,128)S(1)} %pad_maximum_fusion.1.column), channel_id=1, source_target_pairs={{1,2},{2,1},{3,4},{4,3},{5,6},{6,5},{7,8},{8,7},{9,10},{10,9},{11,... | collective-permute-start | bytes 18440 | tf_op jit(solution)/shard_map/ppermute | solution.py:57
  45.3 5.2 %collective-permute-start.11 = (f32[12,128]{1,0:T(8,128)S(1)}, f32[12,128]{1,0:T(8,128)S(1)}, u32[]{:S(2)}, u32[]{:S(2)}) collective-permute-start(f32[12,128]{1,0:T(8,128)S(1)} %pad_maximum_fusion.1.column), channel_id=1, source_target_pairs={{0,1},{1,0},{2,3},{3,2},{4,5},{5,4},{6,7},{7,6},{8,9},{9,8},{10,11... | collective-permute-start | bytes 18440 | tf_op jit(solution)/shard_map/ppermute | solution.py:57
  51.2 7.9 %collective-permute-start.12 = (f32[4,128]{1,0:T(4,128)S(1)}, f32[4,128]{1,0:T(4,128)S(1)}, u32[]{:S(2)}, u32[]{:S(2)}) collective-permute-start(f32[4,128]{1,0:T(4,128)S(1)} %get-tuple-element.62.own), channel_id=1, source_target_pairs={{16,32},{32,16},{48,64},{64,48},{80,96},{96,80},{112,128},{128,112... | collective-permute-start | bytes 6152 | tf_op jit(solution)/shard_map/ppermute | solution.py:57
  54.9 4.1 %collective-permute-start.13 = (f32[4,128]{1,0:T(4,128)S(1)}, f32[4,128]{1,0:T(4,128)S(1)}, u32[]{:S(2)}, u32[]{:S(2)}) collective-permute-start(f32[4,128]{1,0:T(4,128)S(1)} %get-tuple-element.62.own), channel_id=1, source_target_pairs={{0,16},{16,0},{32,48},{48,32},{64,80},{80,64},{96,112},{112,96},{1... | collective-permute-start | bytes 6152 | tf_op jit(solution)/shard_map/ppermute | solution.py:57
  59.1 5.3 %collective-permute-start.14 = (f32[12,128]{1,0:T(8,128)S(1)}, f32[12,128]{1,0:T(8,128)S(1)}, u32[]{:S(2)}, u32[]{:S(2)}) collective-permute-start(f32[12,128]{1,0:T(8,128)S(1)} %pad_maximum_fusion.2.column), channel_id=1, source_target_pairs={{1,2},{2,1},{3,4},{4,3},{5,6},{6,5},{7,8},{8,7},{9,10},{10,9},{11,... | collective-permute-start | bytes 18440 | tf_op jit(solution)/shard_map/ppermute | solution.py:57
  59.2 5.2 %collective-permute-start.15 = (f32[12,128]{1,0:T(8,128)S(1)}, f32[12,128]{1,0:T(8,128)S(1)}, u32[]{:S(2)}, u32[]{:S(2)}) collective-permute-start(f32[12,128]{1,0:T(8,128)S(1)} %pad_maximum_fusion.2.column), channel_id=1, source_target_pairs={{0,1},{1,0},{2,3},{3,2},{4,5},{5,4},{6,7},{7,6},{8,9},{9,8},{10,11... | collective-permute-start | bytes 18440 | tf_op jit(solution)/shard_map/ppermute | solution.py:57

commit v2 on v1

--- a/solution.py
+++ b/solution.py
@@ -310,81 +310,92 @@
     )(part, odd1, even1, state, numbers)
 
 
-def pair_force(count, own, others, rows, terms):
-    for i, other in enumerate(others):
-        for c in range(4):
-            rows[4 * i + c] = jnp.broadcast_to(other[c], (8, FZ))
-    column = jnp.concatenate(list(own) + [jnp.zeros((5, FZ), jnp.float32)], axis=0).T
-    rows_at = TILE // 8
-
-    def tile(t):
-        part = column[TILE * t : TILE * t + TILE]
-        mine = [
-            jnp.broadcast_to(part[:, c : c + 1], (TILE, FZ)).reshape(rows_at, 8, FZ)
-            for c in range(3)
-        ]
-        total = None
-        for i in range(len(others)):
-            dx = mine[0] - rows[4 * i][None]
-            dy = mine[1] - rows[4 * i + 1][None]
-            dz = mine[2] - rows[4 * i + 2][None]
-            dz = jnp.where(
-                dz > 0.5 * CZ, dz - CZ, jnp.where(dz < -0.5 * CZ, dz + CZ, dz)
-            )
-            reach = jnp.maximum(
-                rows[4 * i + 3][None]
-                - (dx * dx + dy * dy + dz * dz) * (1.0 / (cutoff * cutoff)),
-                0.0,
-            )
-            weight = reach * reach
-            new = (weight * dx, weight * dy, weight * dz)
-            total = new if total is None else tuple(a + b for a, b in zip(total, new))
-        for c in range(3):
-            terms[FZ * c + TILE * t : FZ * c + TILE * t + TILE] = total[c].reshape(TILE, FZ)
-
-    for t in range(FZ // TILE):
-        if TILE * t < 21:
-            tile(t)
-        else:
-            pl.when(TILE * t < count)(functools.partial(tile, t))
+def pair_force(devices, rows, terms):
     ones = jnp.ones((8, FZ), jnp.bfloat16)
-    slot = lax.broadcasted_iota(jnp.int32, (FZ, FZ), 0) < count
-    left = jnp.where(jnp.concatenate([slot] * 3), terms[...], 0.0)
-    back = None
-    for part in range(3):
-        piece = left.astype(jnp.bfloat16)
-        term = lax.dot_general(ones, piece, NT, preferred_element_type=jnp.float32)
-        back = term if back is None else back + term
-        if part < 2:
-            left = left - piece.astype(jnp.float32)
-    return [stiffness * back[0:1, FZ * c : FZ * c + FZ] for c in range(3)]
-
-
-PAIR_SCRATCH = [VMEM((36, 8, FZ), jnp.float32), VMEM((3 * FZ, FZ), jnp.float32)]
-
-
-def around(column, live):
-    toward_x = ((2 * parity("gx") - 1) * CX).astype(jnp.float32)
-    toward_y = ((2 * parity("yz") - 1) * CY).astype(jnp.float32)
-    others = []
-    for b in range(3):
-        for a in range(3):
-            x, y, z = column(b, a)
-            limit = jnp.where(live(b, a) > 0.0, 1.0, -1.0)
-            others.append((x + (1 - a) * toward_x, y + (1 - b) * toward_y, z, limit))
-    return others
-
-
-def advance(count, own, velocity, mass, others, rows, terms):
-    live = live_row(count)
-    force = [jnp.where(live, f, 0.0) for f in pair_force(count, own, others, rows, terms)]
-    velocity = [velocity[c] + timestep * force[c] / mass for c in range(3)]
+    slot = lax.broadcasted_iota(jnp.int32, (FZ, FZ), 0)
+    sub = TILE // 8
+
+    for n, (own, live, others) in enumerate(devices):
+        column = jnp.concatenate(list(own) + [jnp.zeros((5, FZ), jnp.float32)], axis=0).T
+
+        def tile(t, n=n, column=column, others=others):
+            part = column[TILE * t : TILE * t + TILE]
+            mine = [
+                jnp.broadcast_to(part[:, c : c + 1], (TILE, FZ)).reshape(sub, 8, FZ)
+                for c in range(3)
+            ]
+            moved = {step: mine[0] - step * float(CX) for step in (-1, 0, 1)}
+            total = None
+            for place, step in others:
+                dx = moved[step] - rows[4 * place][None]
+                dy = mine[1] - rows[4 * place + 1][None]
+                dz = mine[2] - rows[4 * place + 2][None]
+                dz = jnp.where(
+                    dz > 0.5 * CZ, dz - CZ, jnp.where(dz < -0.5 * CZ, dz + CZ, dz)
+                )
+                reach = jnp.maximum(
+                    rows[4 * place + 3][None]
+                    - (dx * dx + dy * dy + dz * dz) * (1.0 / (cutoff * cutoff)),
+                    0.0,
+                )
+                weight = reach * reach
+                new = (weight * dx, weight * dy, weight * dz)
+                total = new if total is None else tuple(a + b for a, b in zip(total, new))
+            for c in range(3):
+                start = FZ * (3 * n + c) + TILE * t
+                terms[start : start + TILE] = total[c].reshape(TILE, FZ)
+
+        for t in range(FZ // TILE):
+            pl.when(TILE * t < live)(functools.partial(tile, t))
+
+    forces = []
+    for n, (own, live, others) in enumerate(devices):
+        left = jnp.where(
+            jnp.concatenate([slot < live] * 3), terms[3 * FZ * n : 3 * FZ * (n + 1)], 0.0
+        )
+        back = None
+        for part in range(3):
+            piece = left.astype(jnp.bfloat16)
+            term = lax.dot_general(ones, piece, NT, preferred_element_type=jnp.float32)
+            back = term if back is None else back + term
+            if part < 2:
+                left = left - piece.astype(jnp.float32)
+        forces.append([stiffness * back[0:1, FZ * c : FZ * c + FZ] for c in range(3)])
+    return forces
+
+
+def pair_scratch(width):
+    return [
+        VMEM((12 * (width + 2), 8, FZ), jnp.float32),
+        VMEM((3 * FZ * width, FZ), jnp.float32),
+    ]
+
+
+def store_rows(rows, place, packet, step_y):
+    x, y, z, alive = packet
+    values = (x, y + step_y, z, jnp.where(alive > 0.0, 1.0, -1.0))
+    for c in range(4):
+        rows[4 * place + c] = jnp.broadcast_to(values[c], (8, FZ))
+
+
+def toward(axis, cells):
+    return ((2 * parity(axis) - 1) * cells).astype(jnp.float32)
+
+
+def live_count(alive):
+    return jnp.sum(alive).astype(jnp.int32)
+
+
+def advance(own, velocity, mass, alive, force):
+    velocity = [
+        velocity[c] + timestep * jnp.where(alive > 0.0, force[c], 0.0) / mass for c in range(3)
+    ]
     return [own[c] + timestep * velocity[c] for c in range(3)], velocity
 
 
 def fields_kernel(
     count, part, odd1, even1, odd2, even2, state, numbers_in,
-    field_out, live_out, vel_out, pos_out,
+    field_out, rest_out, packets,
     full, numbers, pair_rows, pair_terms,
 ):
     add_x(part, odd1, even1, full)
@@ -468,31 +479,34 @@
             source, base = (odd2 if b == 0 else even2), 18 + 4 * a
         return [source[base + c : base + c + 1] for c in range(4)]
 
-    live_out[9:16] = state[0:7]
+    rest_out[0:7] = state[0:7]
+    rest_out[7:8] = alive_row
+    after = parity("gx") == 1
     for b in range(3):
-        for a in range(3):
-            live_out[3 * b + a : 3 * b + a + 1] = rows(b, a)[3]
-    others = around(lambda b, a: rows(b, a)[:3], lambda b, a: rows(b, a)[3])
-    moved, velocity = advance(
-        count[0, 0], own, velocity, state[6:7], others, pair_rows, pair_terms
-    )
-    for c in range(3):
-        vel_out[c : c + 1] = velocity[c]
-        pos_out[c : c + 1] = moved[c]
-    vel_out[3:4] = jnp.zeros((1, FZ), jnp.float32)
-    pos_out[3:4] = jnp.zeros((1, FZ), jnp.float32)
+        step_y = (1 - b) * toward("yz", CY)
+        slots = [rows(b, a) for a in range(3)]
+        first = [jnp.where(after, e, o) for o, e in zip(slots[0], slots[2])]
+        last = [jnp.where(after, o, e) for o, e in zip(slots[0], slots[2])]
+        for a, packet in enumerate((first, slots[1], last)):
+            store_rows(pair_rows, 3 * b + a, packet, step_y)
+    others = [(3 * b + a, a - 1) for b in range(3) for a in range(3)]
+    force = pair_force([(own, count[0, 0], others)], pair_rows, pair_terms)[0]
+    moved, velocity = advance(own, velocity, state[6:7], alive_row, force)
+    packet = jnp.concatenate(moved + [alive_row] + velocity + [state[6:7]], axis=0)
+    for g in range(packets.shape[0]):
+        packets[g] = packet
 
 
 def cell_fields(count, part, odd1, even1, odd2, even2, state, numbers):
     return pl.pallas_call(
         fields_kernel,
-        out_shape=(struct(6, ROWS, FZ), struct(16, FZ), struct(4, FZ), struct(4, FZ)),
+        out_shape=(struct(6, ROWS, FZ), struct(8, FZ), struct(lax.axis_size("gx"), 8, FZ)),
         in_specs=[IN_SMEM] + [IN_VMEM] * 7,
-        out_specs=(IN_VMEM,) * 4,
+        out_specs=(IN_VMEM,) * 3,
         scratch_shapes=[
             VMEM((2 * ROWS, FZ), jnp.float32),
             VMEM((ROWS, FZ), jnp.float32),
-            *PAIR_SCRATCH,
+            *pair_scratch(1),
         ],
         compiler_params=pltpu.CompilerParams(vmem_limit_bytes=SMALL_LIMIT),
         cost_estimate=pl.CostEstimate(flops=4_000_000, bytes_accessed=1_000_000, transcendentals=0),
@@ -500,45 +514,101 @@
     )(count, part, odd1, even1, odd2, even2, state, numbers)
 
 
-def substep_moves(count, rest, own, column, odd, even, vel, rows, terms):
-    mine = [own[c : c + 1] for c in range(3)]
-    old = [vel[c : c + 1] for c in range(3)]
-    source = (odd, column, even)
-    others = around(
-        lambda b, a: [source[b][4 * a + c : 4 * a + c + 1] for c in range(3)],
-        lambda b, a: rest[3 * b + a : 3 * b + a + 1],
-    )
-    return advance(count[0, 0], mine, old, rest[15:16], others, rows, terms)
-
-
-def substep_kernel(count, rest, own, column, odd, even, vel, vel_out, pos_out, rows, terms):
-    moved, velocity = substep_moves(count, rest, own, column, odd, even, vel, rows, terms)
+def padded(rows):
+    return -(-rows // 8) * 8
+
+
+def clear_tail(ref, used):
+    if used < ref.shape[0]:
+        ref[used:] = jnp.zeros((ref.shape[0] - used, FZ), jnp.float32)
+
+
+def pick_kernel(width, packets, row_out, moving_out):
+    count = packets.shape[0]
+    me = lax.axis_index("gx")
+    for a in range(width):
+        source = lax.rem(me + a - width // 2 + 8 * count, count)
+        row_out[4 * a : 4 * a + 4] = packets[source, 0:4]
+        if 0 < a < width - 1:
+            moving_out[4 * a - 4 : 4 * a] = packets[source, 4:8]
+    clear_tail(row_out, 4 * width)
+    clear_tail(moving_out, 4 * (width - 2))
+
+
+def pick(width, packets):
+    return pl.pallas_call(
+        functools.partial(pick_kernel, width),
+        out_shape=(struct(padded(4 * width), FZ), struct(padded(4 * (width - 2)), FZ)),
+        in_specs=[IN_VMEM],
+        out_specs=(IN_VMEM,) * 2,
+        compiler_params=pltpu.CompilerParams(vmem_limit_bytes=SMALL_LIMIT),
+        cost_estimate=pl.CostEstimate(flops=10_000, bytes_accessed=100_000, transcendentals=0),
+        name="pick",
+    )(packets)
+
+
+def substep_moves(width, row, moving, odd, even, rows, terms):
+    span = width + 2
+    for b, source in enumerate((odd, row, even)):
+        step_y = (1 - b) * toward("yz", CY)
+        for a in range(span):
+            packet = [source[4 * a + c : 4 * a + c + 1] for c in range(4)]
+            store_rows(rows, span * b + a, packet, step_y)
+    devices = []
+    for n in range(width):
+        at = 4 * (n + 1)
+        own = [row[at + c : at + c + 1] for c in range(3)]
+        others = [(span * b + n + 1 + step, step) for b in range(3) for step in (-1, 0, 1)]
+        devices.append((own, live_count(row[at + 3 : at + 4]), others))
+    forces = pair_force(devices, rows, terms)
+    results = []
+    for n in range(width):
+        alive = row[4 * n + 7 : 4 * n + 8]
+        velocity = [moving[4 * n + c : 4 * n + c + 1] for c in range(3)]
+        mass = moving[4 * n + 3 : 4 * n + 4]
+        results.append((*advance(devices[n][0], velocity, mass, alive, forces[n]), alive, mass))
+    return results
+
+
+def substep_kernel(width, row, moving, odd, even, row_out, moving_out, rows, terms):
+    results = substep_moves(width, row, moving, odd, even, rows, terms)
+    for n, (moved, velocity, alive, mass) in enumerate(results):
+        row_out[4 * n : 4 * n + 4] = jnp.concatenate(moved + [alive], axis=0)
+        if 0 < n < width - 1:
+            moving_out[4 * n - 4 : 4 * n] = jnp.concatenate(velocity + [mass], axis=0)
+    clear_tail(row_out, 4 * width)
+    clear_tail(moving_out, 4 * (width - 2))
+
+
+def last_kernel(row, moving, odd, even, rest, pos_out, vel_out, rows, terms):
+    ((moved, velocity, alive, mass),) = substep_moves(1, row, moving, odd, even, rows, terms)
+    keep = rest[7:8] > 0.0
     for c in range(3):
-        vel_out[c : c + 1] = velocity[c]
-        pos_out[c : c + 1] = moved[c]
-    vel_out[3:4] = jnp.zeros((1, FZ), jnp.float32)
-    pos_out[3:4] = jnp.zeros((1, FZ), jnp.float32)
-
-
-def last_kernel(count, rest, own, column, odd, even, vel, vel_out, pos_out, rows, terms):
-    moved, velocity = substep_moves(count, rest, own, column, odd, even, vel, rows, terms)
-    keep = rest[4:5] > 0.0
-    for c in range(3):
-        pos_out[c] = jnp.where(keep, moved[c], rest[9 + c : 10 + c])
-        vel_out[c] = jnp.where(keep, velocity[c], rest[12 + c : 13 + c])
-
-
-def substep(kernel, shape, count, rest, own, column, odd, even, vel):
+        pos_out[c] = jnp.where(keep, moved[c], rest[c : c + 1])
+        vel_out[c] = jnp.where(keep, velocity[c], rest[3 + c : 4 + c])
+
+
+def substep(width, row, moving, odd, even, rest):
+    if width > 1:
+        kernel = functools.partial(substep_kernel, width)
+        shapes = (struct(padded(4 * width), FZ), struct(padded(4 * (width - 2)), FZ))
+        operands = (row, moving, odd, even)
+    else:
+        kernel = last_kernel
+        shapes = (struct(3, 1, FZ), struct(3, 1, FZ))
+        operands = (row, moving, odd, even, rest)
     return pl.pallas_call(
         kernel,
-        out_shape=(struct(*shape), struct(*shape)),
-        in_specs=[IN_SMEM] + [IN_VMEM] * 6,
+        out_shape=shapes,
+        in_specs=[IN_VMEM] * len(operands),
         out_specs=(IN_VMEM,) * 2,
-        scratch_shapes=PAIR_SCRATCH,
+        scratch_shapes=pair_scratch(width),
         compiler_params=pltpu.CompilerParams(vmem_limit_bytes=SMALL_LIMIT),
-        cost_estimate=pl.CostEstimate(flops=4_000_000, bytes_accessed=30_000, transcendentals=0),
+        cost_estimate=pl.CostEstimate(
+            flops=4_000_000 * width, bytes_accessed=100_000, transcendentals=0
+        ),
         name="substep",
-    )(count, rest, own, column, odd, even, vel)
+    )(*operands)
 
 
 def turn_kernel(ks, shift, v, occ, field, *refs):
@@ -680,26 +750,22 @@
     part, state, numbers = prepare(base)
     odd, even = columns(part, odd1, even1, state, numbers)
     odd2, even2 = swap_both(odd, even, "yz")
-    field, rest, velocity, position = cell_fields(
-        count, part, odd1, even1, odd2, even2, state, numbers
-    )
+    field, rest, packets = cell_fields(count, part, odd1, even1, odd2, even2, state, numbers)
+    packets = lax.all_to_all(packets, "gx", 0, 0)
+    width = 2 * (SUBSTEPS - 1) + 1
+    row, moving = pick(width, packets)
     solvent_out = None
-    for step in range(1, SUBSTEPS):
-        ks = TURNED[step - 1]
-        if step > 1:
-            position, solvent_out = lax.optimization_barrier((position, solvent_out))
+    for ks in TURNED:
+        width -= 2
+        if solvent_out is None:
+            row, field = lax.optimization_barrier((row, field))
+        else:
+            row, solvent_out = lax.optimization_barrier((row, solvent_out))
         solvent_out = turn_solvent(ks, grid_shift, v, occupancy, field, solvent_out)
-        odd, even = swap_both(position, position, "gx")
+        odd, even = swap_both(row, row, "yz")
         odd, solvent_out = lax.optimization_barrier((odd, solvent_out))
-        column = jnp.concatenate([odd, position, even])
-        odd, even = swap_both(column, column, "yz")
-        odd, velocity = lax.optimization_barrier((odd, velocity))
-        kernel, shape = (
-            (substep_kernel, (4, FZ)) if step < SUBSTEPS - 1 else (last_kernel, (3, 1, FZ))
-        )
-        velocity, position = substep(
-            kernel, shape, count, rest, position, column, odd, even, velocity
-        )
+        row, moving = substep(width, row, moving, odd, even, rest)
+    position, velocity = row, moving
     return (
         solvent_out.reshape(solvent_vel.shape),
         position[:, None],

time: 65.8 us -> 63.2 us (0.960)
  the two profiles are of different devices: /device:TPU:32 before, /device:TPU:1 now
where the time goes in v2:
time: 63.2 us
  starting transfers between devices  24.2 us (38%)
  Pallas kernels  18.1 us (29%)
  blocking collectives  14.1 us (22%)
  waiting for transfers between devices  3.2 us (5%)
  local copies, waits for them, and re-layouts  1.99 us (3%)
  between operations  1.58 us (2%)
    ppermute x10, starting transfers between devices, swapped(): return lax.ppermute(value, axis, pairs)  24.2 us
    all_to_all x1, blocking collectives, per_device(): packets = lax.all_to_all(packets, 'gx', 0, 0)  14.1 us
    pallas_call x3, Pallas kernels, turn_solvent(): pl.pallas_call(functools.partial(turn_kernel, ks), out_shape=struct(*v.sh...  6.77 us
    pallas_call x3, Pallas kernels, substep(): pl.pallas_call(kernel, out_shape=shapes, in_specs=[IN_VMEM] * len(operand...  6.41 us
    pallas_call x1, Pallas kernels, cell_sums(): pl.pallas_call(sums_kernel, out_shape=(struct(BASE, FZ), struct(32, FZ),...  3.66 us
    ppermute x10, waiting for transfers between devices, swapped(): return lax.ppermute(value, axis, pairs)  3.2 us
    unnamed x8, local copies, waits for them, and re-layouts  1.99 us
  transfers between devices with their start and end apart: 10, of which 3 were waited for; matrix products, arithmetic and copies ran while one was open for 0% of the time, Pallas kernels for 11%

profile of v2, /device:TPU:1, one launch (start us, length us, event | category | flops | bytes accessed | tf_op | source)
XLA Modules:
  0.0 63.2 jit_solution(3869349389949714626)
XLA Ops:
  0.6 0.0 copy-start.3
  0.6 0.0 copy-start
  1.4 3.7 %cell_sums.1 = (f32[448,128]{1,0:T(8,128)}, f32[32,128]{1,0:T(8,128)}, f32[32,128]{1,0:T(8,128)}) custom-call(s32[3]{0:T(128)} %shift.5, s32[1,1]{1,0:T(1,128)S(6)} %copy.17.count_at.count, f32[3,32,64,128]{3,2,1,0:T(8,128)} %bitcast.10, s32[32,32,128]{2,1,0:T(8,128)} %occ.5, s32[8,8,64]{2,1,0:T(8,128)} %axis_at.1, f32[3,1,128]{2,1,0:T(1,128)} %bitcast.15, ...), custom_call_target="tpu_custom_call" | custom-call | flops 4000000 | bytes 3700000 | tf_op jit(solution)/shard_map/cell_sums/pallas_call | solution.py:222
  5.1 9.4 %collective-permute-start = (f32[32,128]{1,0:T(8,128)}, f32[32,128]{1,0:T(8,128)S(1)}, u32[]{:S(2)}, u32[]{:S(2)}) collective-permute-start(f32[32,128]{1,0:T(8,128)} %get-tuple-element.36), channel_id=1, source_target_pairs={{16,32},{32,16},{48,64},{64,48},{80,96},{96,80},{112,128},{128,112... | collective-permute-start | bytes 49160 | tf_op jit(solution)/shard_map/ppermute | solution.py:57
  14.5 0.0 collective-permute-start.1
  14.5 0.0 copy-start.2
  14.5 0.9 %copy-done.2 = f32[448,128]{1,0:T(8,128)S(1)} copy-done((f32[448,128]{1,0:T(8,128)S(1)}, f32[448,128]{1,0:T(8,128)}, u32[]{:S(2)}) %copy-start.2) | copy-done | bytes 229400
  15.5 0.4 collective-permute-done.odd1
  15.8 1.5 %collective-permute-done.1.even1 = f32[32,128]{1,0:T(8,128)S(1)} collective-permute-done((f32[32,128]{1,0:T(8,128)}, f32[32,128]{1,0:T(8,128)S(1)}, u32[]{:S(2)}, u32[]{:S(2)}) %collective-permute-start.1) | collective-permute-done | bytes 16416 | tf_op jit(solution)/shard_map/ppermute | solution.py:57
  17.3 3.3 %collective-permute-start.2 = (f32[40,128]{1,0:T(8,128)S(1)}, f32[40,128]{1,0:T(8,128)S(1)}, u32[]{:S(2)}, u32[]{:S(2)}) collective-permute-start(f32[40,128]{1,0:T(8,128)S(1)} %get-tuple-element.40), channel_id=1, source_target_pairs={{1,2},{2,1},{3,4},{4,3},{5,6},{6,5},{7,8},{8,7},{9,10},{10,9},{11,... | collective-permute-start | bytes 61448 | tf_op jit(solution)/shard_map/ppermute | solution.py:57
  20.6 0.1 collective-permute-start.3
  20.8 1.3 %collective-permute-done.2.odd2 = f32[40,128]{1,0:T(8,128)S(1)} collective-permute-done((f32[40,128]{1,0:T(8,128)S(1)}, f32[40,128]{1,0:T(8,128)S(1)}, u32[]{:S(2)}, u32[]{:S(2)}) %collective-permute-start.2) | collective-permute-done | bytes 20512 | tf_op jit(solution)/shard_map/ppermute | solution.py:57
  22.1 0.0 collective-permute-done.3.even2
  22.1 1.2 %cell_fields.1 = (f32[6,144,128]{2,1,0:T(8,128)S(1)}, f32[8,128]{1,0:T(8,128)S(1)}, f32[16,8,128]{2,1,0:T(8,128)S(1)}) custom-call(s32[1,1]{1,0:T(1,128)S(6)} %copy.17.count_at.count, f32[288,128]{1,0:T(8,128)S(1)} %get-tuple-element.35.part, f32[32,128]{1,0:T(8,128)S(1)} %collective-permute-done.odd1, f32[32,128]{1,0:T(8,128)S(1)} %collective-permute-done.1.even1, ...), custom_call_target="tpu_custom_call" | custom-call | flops 4000000 | bytes 1000000 | tf_op jit(solution)/shard_map/cell_fields/pallas_call | solution.py:501
  23.3 14.1 %all_to_all.5.packets = f32[16,8,128]{2,1,0:T(8,128)S(1)} all-to-all(f32[16,8,128]{2,1,0:T(8,128)S(1)} %get-tuple-element.42), channel_id=1, replica_groups=mesh['gx'=16,'yz'=16] {'gx'}, dimensions={0} | all-to-all | bytes 131072 | tf_op jit(solution)/shard_map/all_to_all | solution.py:754
  37.4 3.3 %collective-permute-start.4 = (f32[32,128]{1,0:T(8,128)S(1)}, f32[32,128]{1,0:T(8,128)S(1)}, u32[]{:S(2)}, u32[]{:S(2)}) collective-permute-start(f32[32,128]{1,0:T(8,128)S(1)} %get-tuple-element.45.row), channel_id=1, source_target_pairs={{1,2},{2,1},{3,4},{4,3},{5,6},{6,5},{7,8},{8,7},{9,10},{10,9},{11,... | collective-permute-start | bytes 49160 | tf_op jit(solution)/shard_map/ppermute | solution.py:57
  40.6 1.5 %collective-permute-start.5 = (f32[32,128]{1,0:T(8,128)S(1)}, f32[32,128]{1,0:T(8,128)S(1)}, u32[]{:S(2)}, u32[]{:S(2)}) collective-permute-start(f32[32,128]{1,0:T(8,128)S(1)} %get-tuple-element.45.row), channel_id=1, source_target_pairs={{0,1},{1,0},{2,3},{3,2},{4,5},{5,4},{6,7},{7,6},{8,9},{9,8},{10,11... | collective-permute-start | bytes 49160 | tf_op jit(solution)/shard_map/ppermute | solution.py:57
  42.1 0.0 copy-done.3
  42.1 0.0 copy-done
  42.1 0.0 copy-start.1
  42.1 1.0 %copy-done.1 = s32[32,32,128]{2,1,0:T(8,128)S(1)} copy-done((s32[32,32,128]{2,1,0:T(8,128)S(1)}, s32[32,32,128]{2,1,0:T(8,128)}, u32[]{:S(2)}) %copy-start.1) | copy-done | bytes 524312
  43.2 2.2 %turn_solvent.3.refs_0_ = f32[3,32,64,128]{3,2,1,0:T(8,128)} custom-call(s32[3]{0:T(128)S(1)} %copy-done.3, f32[3,32,64,128]{3,2,1,0:T(8,128)S(1)} %bitcast.11, s32[32,32,128]{2,1,0:T(8,128)S(1)} %copy-done.1, f32[6,144,128]{2,1,0:T(8,128)S(1)} %get-tuple-element.47.field), custom_call_target="tpu_custom_call" | custom-call | flops 3000000 | bytes 1300000 | tf_op jit(solution)/shard_map/turn_solvent/pallas_call | solution.py:714
  45.4 0.0 collective-permute-done.4.odd
  45.4 0.0 collective-permute-done.5.even
  45.4 3.0 %substep.3 = (f32[24,128]{1,0:T(8,128)S(1)}, f32[16,128]{1,0:T(8,128)S(1)}) custom-call(f32[32,128]{1,0:T(8,128)S(1)} %get-tuple-element.45.row, f32[24,128]{1,0:T(8,128)S(1)} %get-tuple-element.46.moving, f32[32,128]{1,0:T(8,128)S(1)} %collective-permute-done.4.odd, f32[32,128]{1,0:T(8,128)S(1)} %collective-permute-done.5.even), custom_call_target="tpu_custom_call" | custom-call | flops 20000000 | bytes 100000 | tf_op jit(solution)/shard_map/substep/pallas_call | solution.py:600
  48.4 0.1 collective-permute-start.6
  48.5 3.5 %collective-permute-start.7 = (f32[24,128]{1,0:T(8,128)S(1)}, f32[24,128]{1,0:T(8,128)S(1)}, u32[]{:S(2)}, u32[]{:S(2)}) collective-permute-start(f32[24,128]{1,0:T(8,128)S(1)} %get-tuple-element.51.row), channel_id=1, source_target_pairs={{0,1},{1,0},{2,3},{3,2},{4,5},{5,4},{6,7},{7,6},{8,9},{9,8},{10,11... | collective-permute-start | bytes 36872 | tf_op jit(solution)/shard_map/ppermute | solution.py:57
  52.1 2.2 %turn_solvent.4.refs_0_ = f32[3,32,64,128]{3,2,1,0:T(8,128)} custom-call(s32[3]{0:T(128)S(1)} %copy-done.3, f32[3,32,64,128]{3,2,1,0:T(8,128)S(1)} %bitcast.12, s32[32,32,128]{2,1,0:T(8,128)S(1)} %copy-done.1, f32[6,144,128]{2,1,0:T(8,128)S(1)} %get-tuple-element.47.field, f32[3,32,64,128]{3,2,1,0:T(8,128)} %turn_solvent.3.refs_0_), custom_call_target="tpu_custom_call", output_to_operand_aliasing={{}: (4, {})} | custom-call | flops 3000000 | bytes 1300000 | tf_op jit(solution)/shard_map/turn_solvent/pallas_call | solution.py:714
  54.3 0.0 collective-permute-done.6.odd
  54.3 0.0 collective-permute-done.7.even
  54.3 2.1 %substep.4 = (f32[16,128]{1,0:T(8,128)S(1)}, f32[8,128]{1,0:T(8,128)S(1)}) custom-call(f32[24,128]{1,0:T(8,128)S(1)} %get-tuple-element.51.row, f32[16,128]{1,0:T(8,128)S(1)} %get-tuple-element.52.moving, f32[24,128]{1,0:T(8,128)S(1)} %collective-permute-done.6.odd, f32[24,128]{1,0:T(8,128)S(1)} %collective-permute-done.7.even), custom_call_target="tpu_custom_call" | custom-call | flops 12000000 | bytes 100000 | tf_op jit(solution)/shard_map/substep/pallas_call | solution.py:600
  56.5 0.1 collective-permute-start.8
  56.6 3.0 %collective-permute-start.9 = (f32[16,128]{1,0:T(8,128)S(1)}, f32[16,128]{1,0:T(8,128)S(1)}, u32[]{:S(2)}, u32[]{:S(2)}) collective-permute-start(f32[16,128]{1,0:T(8,128)S(1)} %get-tuple-element.57.row), channel_id=1, source_target_pairs={{0,1},{1,0},{2,3},{3,2},{4,5},{5,4},{6,7},{7,6},{8,9},{9,8},{10,11... | collective-permute-start | bytes 24584 | tf_op jit(solution)/shard_map/ppermute | solution.py:57
  59.5 2.3 %turn_solvent.5 = f32[3,32,64,128]{3,2,1,0:T(8,128)} custom-call(s32[3]{0:T(128)S(1)} %copy-done.3, f32[3,32,64,128]{3,2,1,0:T(8,128)S(1)} %bitcast.13, s32[32,32,128]{2,1,0:T(8,128)S(1)} %copy-done.1, f32[6,144,128]{2,1,0:T(8,128)S(1)} %get-tuple-element.47.field, f32[3,32,64,128]{3,2,1,0:T(8,128)} %turn_solvent.4.refs_0_), custom_call_target="tpu_custom_call", output_to_operand_aliasing={{}: (4, {})} | custom-call | flops 3000000 | bytes 1300000 | tf_op jit(solution)/shard_map/turn_solvent/pallas_call | solution.py:714
  61.8 0.0 collective-permute-done.8.odd
  61.9 0.0 collective-permute-done.9.even
  61.9 1.3 %substep.5 = (f32[3,1,128]{2,1,0:T(1,128)}, f32[3,1,128]{2,1,0:T(1,128)}) custom-call(f32[16,128]{1,0:T(8,128)S(1)} %get-tuple-element.57.row, f32[8,128]{1,0:T(8,128)S(1)} %get-tuple-element.60.moving, f32[16,128]{1,0:T(8,128)S(1)} %collective-permute-done.8.odd, f32[16,128]{1,0:T(8,128)S(1)} %collective-permute-done.9.even, ...), custom_call_target="tpu_custom_call" | custom-call | flops 4000000 | bytes 100000 | tf_op jit(solution)/shard_map/substep/pallas_call | solution.py:600
  (3 shorter events, 0.1 us)
Async XLA Ops:
  0.6 41.5 %copy-start.3 = (s32[3]{0:T(128)S(1)}, s32[3]{0:T(128)}, u32[]{:S(2)}) copy-start(s32[3]{0:T(128)} %shift.5) | copy-start | bytes 40
  0.6 41.5 %copy-start = (f32[3,32,32,2,128]{4,3,2,1,0:T(2,128)S(1)}, f32[3,32,32,2,128]{4,3,2,1,0:T(2,128)}, u32[]{:S(2)}) copy-start(f32[3,32,32,2,128]{4,3,2,1,0:T(2,128)} %param.8) | copy-start | bytes 9437188
  5.1 10.7 %collective-permute-start = (f32[32,128]{1,0:T(8,128)}, f32[32,128]{1,0:T(8,128)S(1)}, u32[]{:S(2)}, u32[]{:S(2)}) collective-permute-start(f32[32,128]{1,0:T(8,128)} %get-tuple-element.36), channel_id=1, source_target_pairs={{16,32},{32,16},{48,64},{64,48},{80,96},{96,80},{112,128},{128,112... | collective-permute-start | bytes 49160 | tf_op jit(solution)/shard_map/ppermute | solution.py:57
  14.5 2.8 %collective-permute-start.1 = (f32[32,128]{1,0:T(8,128)}, f32[32,128]{1,0:T(8,128)S(1)}, u32[]{:S(2)}, u32[]{:S(2)}) collective-permute-start(f32[32,128]{1,0:T(8,128)} %get-tuple-element.37), channel_id=1, source_target_pairs={{0,16},{16,0},{32,48},{48,32},{64,80},{80,64},{96,112},{112,96},{1... | collective-permute-start | bytes 49160 | tf_op jit(solution)/shard_map/ppermute | solution.py:57
  14.5 0.9 %copy-start.2 = (f32[448,128]{1,0:T(8,128)S(1)}, f32[448,128]{1,0:T(8,128)}, u32[]{:S(2)}) copy-start(f32[448,128]{1,0:T(8,128)} %get-tuple-element.34.base) | copy-start | bytes 688132
  17.3 4.8 %collective-permute-start.2 = (f32[40,128]{1,0:T(8,128)S(1)}, f32[40,128]{1,0:T(8,128)S(1)}, u32[]{:S(2)}, u32[]{:S(2)}) collective-permute-start(f32[40,128]{1,0:T(8,128)S(1)} %get-tuple-element.40), channel_id=1, source_target_pairs={{1,2},{2,1},{3,4},{4,3},{5,6},{6,5},{7,8},{8,7},{9,10},{10,9},{11,... | collective-permute-start | bytes 61448 | tf_op jit(solution)/shard_map/ppermute | solution.py:57
  20.6 1.5 %collective-permute-start.3 = (f32[40,128]{1,0:T(8,128)S(1)}, f32[40,128]{1,0:T(8,128)S(1)}, u32[]{:S(2)}, u32[]{:S(2)}) collective-permute-start(f32[40,128]{1,0:T(8,128)S(1)} %get-tuple-element.41), channel_id=1, source_target_pairs={{0,1},{1,0},{2,3},{3,2},{4,5},{5,4},{6,7},{7,6},{8,9},{9,8},{10,11... | collective-permute-start | bytes 61448 | tf_op jit(solution)/shard_map/ppermute | solution.py:57
  37.4 8.0 %collective-permute-start.4 = (f32[32,128]{1,0:T(8,128)S(1)}, f32[32,128]{1,0:T(8,128)S(1)}, u32[]{:S(2)}, u32[]{:S(2)}) collective-permute-start(f32[32,128]{1,0:T(8,128)S(1)} %get-tuple-element.45.row), channel_id=1, source_target_pairs={{1,2},{2,1},{3,4},{4,3},{5,6},{6,5},{7,8},{8,7},{9,10},{10,9},{11,... | collective-permute-start | bytes 49160 | tf_op jit(solution)/shard_map/ppermute | solution.py:57
  40.6 4.8 %collective-permute-start.5 = (f32[32,128]{1,0:T(8,128)S(1)}, f32[32,128]{1,0:T(8,128)S(1)}, u32[]{:S(2)}, u32[]{:S(2)}) collective-permute-start(f32[32,128]{1,0:T(8,128)S(1)} %get-tuple-element.45.row), channel_id=1, source_target_pairs={{0,1},{1,0},{2,3},{3,2},{4,5},{5,4},{6,7},{7,6},{8,9},{9,8},{10,11... | collective-permute-start | bytes 49160 | tf_op jit(solution)/shard_map/ppermute | solution.py:57
  42.1 1.0 %copy-start.1 = (s32[32,32,128]{2,1,0:T(8,128)S(1)}, s32[32,32,128]{2,1,0:T(8,128)}, u32[]{:S(2)}) copy-start(s32[32,32,128]{2,1,0:T(8,128)} %occ.5) | copy-start | bytes 1572868
  48.4 5.9 %collective-permute-start.6 = (f32[24,128]{1,0:T(8,128)S(1)}, f32[24,128]{1,0:T(8,128)S(1)}, u32[]{:S(2)}, u32[]{:S(2)}) collective-permute-start(f32[24,128]{1,0:T(8,128)S(1)} %get-tuple-element.51.row), channel_id=1, source_target_pairs={{1,2},{2,1},{3,4},{4,3},{5,6},{6,5},{7,8},{8,7},{9,10},{10,9},{11,... | collective-permute-start | bytes 36872 | tf_op jit(solution)/shard_map/ppermute | solution.py:57
  48.5 5.8 %collective-permute-start.7 = (f32[24,128]{1,0:T(8,128)S(1)}, f32[24,128]{1,0:T(8,128)S(1)}, u32[]{:S(2)}, u32[]{:S(2)}) collective-permute-start(f32[24,128]{1,0:T(8,128)S(1)} %get-tuple-element.51.row), channel_id=1, source_target_pairs={{0,1},{1,0},{2,3},{3,2},{4,5},{5,4},{6,7},{7,6},{8,9},{9,8},{10,11... | collective-permute-start | bytes 36872 | tf_op jit(solution)/shard_map/ppermute | solution.py:57
  56.5 5.4 %collective-permute-start.8 = (f32[16,128]{1,0:T(8,128)S(1)}, f32[16,128]{1,0:T(8,128)S(1)}, u32[]{:S(2)}, u32[]{:S(2)}) collective-permute-start(f32[16,128]{1,0:T(8,128)S(1)} %get-tuple-element.57.row), channel_id=1, source_target_pairs={{1,2},{2,1},{3,4},{4,3},{5,6},{6,5},{7,8},{8,7},{9,10},{10,9},{11,... | collective-permute-start | bytes 24584 | tf_op jit(solution)/shard_map/ppermute | solution.py:57
  56.6 5.3 %collective-permute-start.9 = (f32[16,128]{1,0:T(8,128)S(1)}, f32[16,128]{1,0:T(8,128)S(1)}, u32[]{:S(2)}, u32[]{:S(2)}) collective-permute-start(f32[16,128]{1,0:T(8,128)S(1)} %get-tuple-element.57.row), channel_id=1, source_target_pairs={{0,1},{1,0},{2,3},{3,2},{4,5},{5,4},{6,7},{7,6},{8,9},{9,8},{10,11... | collective-permute-start | bytes 24584 | tf_op jit(solution)/shard_map/ppermute | solution.py:57

commit v3 on v2

--- a/solution.py
+++ b/solution.py
@@ -39,7 +39,7 @@
 DMA = pltpu.SemaphoreType.DMA
 NT = (((1,), (1,)), ((), ()))
 NN = (((1,), (0,)), ((), ()))
-STATE = 2 * ROWS
+STATE = 4 * JP
 NUMBERS = STATE + 16
 BASE = NUMBERS + ROWS
 TURNED = ((1, 2, 3), (4, 5, 6), (7, CX))
@@ -88,86 +88,38 @@
     return lax.broadcasted_iota(jnp.int32, (1, FZ), 1) < count
 
 
-def store_twice(occ, twice, q):
-    slots = occ[SUB * q : SUB * q + SUB].reshape(SUB * FY, FZ).astype(jnp.float32)
-    base = 2 * SUB * FY * q
-    twice[pl.ds(base, SUB * FY, 2), :] = slots
-    twice[pl.ds(base + 1, SUB * FY, 2), :] = slots
-
-
 def parity(axis):
     return lax.axis_index(axis) & 1
 
 
-def sums_kernel(
-    shift_at, count_at, v_at, occ_at, axis_at, pos_at, vel_at, mass_at,
-    base, odd, even,
-    shift, count, v, occ, axis, pos, vel, mass, twice, partial, sem, vsem, osem,
-):
-    small = [
-        pltpu.make_async_copy(a, b, sem.at[i])
-        for i, (a, b) in enumerate(
-            [
-                (shift_at, shift),
-                (count_at, count),
-                (axis_at, axis),
-                (pos_at, pos),
-                (vel_at, vel),
-                (mass_at, mass),
-            ]
-        )
-    ]
-    large = []
-    for q in range(CX):
-        part = pl.ds(SUB * q, SUB)
-        large.append(pltpu.make_async_copy(occ_at.at[part], occ.at[part], osem.at[q]))
-        large.append(pltpu.make_async_copy(v_at.at[:, part], v.at[:, part], vsem.at[q]))
-    for copy in small[:2] + large[:2] + small[2:] + large[2:]:
-        copy.start()
-    for copy in small[:2]:
-        copy.wait()
-    sx, sy, sz = shift[0], shift[1], shift[2]
-    row = lax.broadcasted_iota(jnp.int32, (2 * FY, FZ), 0)
-    slot = (row & 1).astype(jnp.float32)
-    low = (row[:8] < 8 - 2 * sy)[None]
-
-    def plane(x, acc):
-        live = twice[pl.ds(pl.multiple_of(x * 2 * FY, 2 * FY), 2 * FY), :] > slot
-        masked = [jnp.where(live, v[c, x], 0.0) for c in range(3)] + [jnp.where(live, 1.0, 0.0)]
-        return tuple(a + m for a, m in zip(acc, masked))
-
-    zero = jnp.zeros((2 * FY, FZ), jnp.float32)
+def live_planes(occ, places, twice):
+    for n, x in enumerate(places):
+        slots = occ[x].astype(jnp.float32)
+        twice[pl.ds(2 * FY * n, FY, 2), :] = slots
+        twice[pl.ds(2 * FY * n + 1, FY, 2), :] = slots
+
+
+def add_plane(v, twice, slot, n, x, acc):
+    live = twice[pl.ds(pl.multiple_of(n * 2 * FY, 2 * FY), 2 * FY), :] > slot
+    masked = [jnp.where(live, v[c, x], 0.0) for c in range(3)] + [jnp.where(live, 1.0, 0.0)]
+    return tuple(a + m for a, m in zip(acc, masked))
+
+
+def store_cells(acc, sy, partial, at):
+    row = lax.broadcasted_iota(jnp.int32, (8, FZ), 0)
+    low = (row < 8 - 2 * sy)[None]
     blank = jnp.zeros((1, 8, FZ), jnp.float32)
-    partial[:, :, 8:JP, :] = jnp.zeros((4, KX, JP - 8, FZ), jnp.float32)
-
-    for k in range(KX):
-        if k < CX:
-            large[2 * k].wait()
-            store_twice(occ, twice, k)
-            large[2 * k + 1].wait()
-        acc = (zero,) * 4
-        if k == 0:
-            acc = lax.fori_loop(0, SUB - sx, plane, acc)
-        elif k == CX:
-            acc = lax.fori_loop(FX - sx, FX, plane, acc)
-        else:
-            for j in range(SUB):
-                acc = plane(k * SUB - sx + j, acc)
-        for c in range(4):
-            parts = acc[c].reshape(CY, 8, FZ)
-            picked = jnp.where(
-                low, jnp.concatenate([parts, blank]), jnp.concatenate([blank, parts])
-            )
-            partial[c, k, 0:JY, :] = jnp.sum(picked, axis=1)
-
-    for copy in small[2:]:
-        copy.wait()
-    kx, jy, lz = colloid_cells(pos, sx, sy, sz)
-    alive = live_row(count[0, 0]).astype(jnp.float32)
-    weight = mass[0] * alive
-    hit = lax.broadcasted_iota(jnp.int32, (ROWS, FZ), 0) == kx * JP + jy
-    carried = [jnp.where(hit, vel[c] * weight, 0.0) for c in range(3)]
-    carried.append(jnp.where(hit, weight, 0.0))
+    for c in range(4):
+        parts = acc[c].reshape(CY, 8, FZ)
+        picked = jnp.where(low, jnp.concatenate([parts, blank]), jnp.concatenate([blank, parts]))
+        partial[c, at, 0:JY, :] = jnp.sum(picked, axis=1)
+
+
+def slot_rows():
+    return (lax.broadcasted_iota(jnp.int32, (2 * FY, FZ), 0) & 1).astype(jnp.float32)
+
+
+def along_z(partial, carried, sz, lz, p):
     target = lax.broadcasted_iota(jnp.int32, (CZ, FZ), 0)
     layer = lax.broadcasted_iota(jnp.int32, (CZ, FZ), 1)
     to_cell = (((layer + sz) & (FZ - 1)) >> 1 == target).astype(jnp.float32)
@@ -177,29 +129,76 @@
     right = jnp.concatenate(
         [jnp.concatenate([one, none], axis=1), jnp.concatenate([none, one], axis=1)], axis=0
     )
+    size = carried[0].shape[0]
+    left = jnp.concatenate(
+        [
+            partial[2 * p].reshape(size, FZ),
+            carried[2 * p],
+            partial[2 * p + 1].reshape(size, FZ),
+            carried[2 * p + 1],
+        ],
+        axis=1,
+    )
+    return exact_dot(left, right, NT)
+
+
+def border_kernel(
+    shift_at, count_at, v_at, occ_at, axis_at, pos_at, vel_at, mass_at,
+    base, odd, even,
+    shift, count, v, occ, axis, pos, vel, mass, twice, partial, sem,
+):
+    ends = ((pl.ds(0, SUB - 1), pl.ds(0, SUB - 1)), (pl.ds(FX - SUB + 1, SUB - 1), pl.ds(SUB - 1, SUB - 1)))
+    pairs = [(shift_at, shift)]
+    pairs += [(occ_at.at[there], occ.at[here]) for there, here in ends]
+    pairs += [(v_at.at[:, there], v.at[:, here]) for there, here in ends]
+    pairs += [(count_at, count), (pos_at, pos), (vel_at, vel), (mass_at, mass), (axis_at, axis)]
+    copies = [pltpu.make_async_copy(a, b, sem.at[i]) for i, (a, b) in enumerate(pairs)]
+    for copy in copies:
+        copy.start()
+    partial[:, :, 8:JP, :] = jnp.zeros((4, 2, JP - 8, FZ), jnp.float32)
+    slot = slot_rows()
+    zero = jnp.zeros((2 * FY, FZ), jnp.float32)
+    for copy in copies[:3]:
+        copy.wait()
+    sx, sy, sz = shift[0], shift[1], shift[2]
+    planes = 2 * (SUB - 1)
+    live_planes(occ, range(planes), twice)
+    for copy in copies[3:]:
+        copy.wait()
+
+    def plane(x, acc):
+        return add_plane(v, twice, slot, x, x, acc)
+
+    store_cells(lax.fori_loop(0, SUB - sx, plane, (zero,) * 4), sy, partial, 0)
+    store_cells(lax.fori_loop(planes - sx, planes, plane, (zero,) * 4), sy, partial, 1)
+
+    kx, jy, lz = colloid_cells(pos, sx, sy, sz)
+    alive = live_row(count[0, 0]).astype(jnp.float32)
+    weight = mass[0] * alive
+    place = jnp.where(kx == 0, jy, jnp.where(kx == CX, JP + jy, 2 * JP))
+    hit = lax.broadcasted_iota(jnp.int32, (2 * JP, FZ), 0) == place
+    carried = [jnp.where(hit, vel[c] * weight, 0.0) for c in range(3)]
+    carried.append(jnp.where(hit, weight, 0.0))
     for p in range(2):
-        left = jnp.concatenate(
-            [
-                partial[2 * p].reshape(ROWS, FZ),
-                carried[2 * p],
-                partial[2 * p + 1].reshape(ROWS, FZ),
-                carried[2 * p + 1],
-            ],
-            axis=1,
-        )
-        total = exact_dot(left, right, NT)
-        base[p * ROWS : p * ROWS + ROWS] = total
-    turned = parity("gx") * (CX * JP)
-    for p in range(2):
-        for packet, place in ((odd, turned), (even, CX * JP - turned)):
-            start = pl.multiple_of(p * ROWS + place, JP)
+        base[2 * JP * p : 2 * JP * (p + 1)] = along_z(partial, carried, sz, lz, p)
+    side = parity("gx")
+    number = None
+    base[NUMBERS : NUMBERS + ROWS] = jnp.zeros((ROWS, FZ), jnp.float32)
+    for k in range(CX):
+        row = axis[k].astype(jnp.float32)
+        row = jnp.concatenate([row, row], axis=1)
+        base[NUMBERS + JP * k : NUMBERS + JP * k + CY] = row
+        number = row if k == 0 else number
+    for packet, end in ((odd, side), (even, 1 - side)):
+        for p in range(2):
+            start = pl.multiple_of(2 * JP * p + JP * end, JP)
             packet[8 * p : 8 * p + 8] = base[pl.ds(start, 8), :]
             packet[16 + p : 17 + p] = base[pl.ds(start + 8, 1), :]
-    for packet in (odd, even):
         for c in range(3):
             packet[18 + c : 19 + c] = pos[c]
         packet[21:22] = alive
         packet[22:24] = jnp.zeros((2, FZ), jnp.float32)
+        packet[24:32] = number
     for c in range(3):
         base[STATE + c : STATE + c + 1] = pos[c]
         base[STATE + 3 + c : STATE + 4 + c] = vel[c]
@@ -208,62 +207,76 @@
     base[STATE + 8 : STATE + 9] = (kx * JP + jy).astype(jnp.float32)
     base[STATE + 9 : STATE + 10] = lz.astype(jnp.float32)
     base[STATE + 10 : STATE + 16] = jnp.zeros((6, FZ), jnp.float32)
-    base[NUMBERS : NUMBERS + ROWS] = jnp.zeros((ROWS, FZ), jnp.float32)
-    for k in range(CX):
-        number = axis[k].astype(jnp.float32)
-        number = jnp.concatenate([number, number], axis=1)
-        base[NUMBERS + JP * k : NUMBERS + JP * k + CY] = number
-        if k == 0:
-            odd[24:32] = number
-            even[24:32] = number
-
-
-def cell_sums(grid_shift, count, v, occ, axis_index, pos, vel, mass):
+
+
+def border_sums(grid_shift, count, v, occ, axis_index, pos, vel, mass):
+    planes = 2 * (SUB - 1)
     return pl.pallas_call(
-        sums_kernel,
-        out_shape=(
-            struct(BASE, FZ),
-            struct(32, FZ),
-            struct(32, FZ),
-        ),
+        border_kernel,
+        out_shape=(struct(BASE, FZ), struct(32, FZ), struct(32, FZ)),
         in_specs=[HBM] * 8,
         out_specs=(IN_VMEM,) * 3,
         scratch_shapes=[
             SMEM((3,), jnp.int32),
             SMEM((1, 1), jnp.int32),
-            VMEM((3, FX, 2 * FY, FZ), jnp.float32),
-            VMEM((FX, FY, FZ), jnp.int32),
+            VMEM((3, planes, 2 * FY, FZ), jnp.float32),
+            VMEM((planes, FY, FZ), jnp.int32),
             VMEM((CX, CY, CZ), jnp.int32),
             VMEM((3, 1, FZ), jnp.float32),
             VMEM((3, 1, FZ), jnp.float32),
             VMEM((1, 1, FZ), jnp.float32),
-            VMEM((2 * FX * FY, FZ), jnp.float32),
-            VMEM((4, KX, JP, FZ), jnp.float32),
-            DMA((6,)),
-            DMA((CX,)),
-            DMA((CX,)),
+            VMEM((2 * planes * FY, FZ), jnp.float32),
+            VMEM((4, 2, JP, FZ), jnp.float32),
+            DMA((10,)),
         ],
-        cost_estimate=pl.CostEstimate(flops=4_000_000, bytes_accessed=3_700_000, transcendentals=0),
-        name="cell_sums",
+        cost_estimate=pl.CostEstimate(flops=1_000_000, bytes_accessed=800_000, transcendentals=0),
+        name="border_sums",
     )(grid_shift, count, v, occ, axis_index, pos, vel, mass)
 
 
-def prepare_kernel(base, part, state, numbers):
-    part[...] = base[0:STATE]
+def inner_kernel(shift, v, occ, base, part, state, numbers, twice, partial):
+    sx, sy, sz = shift[0], shift[1], shift[2]
     state[...] = base[STATE:NUMBERS]
     numbers[...] = base[NUMBERS:BASE]
-
-
-def prepare(base):
+    partial[:, :, 8:JP, :] = jnp.zeros((4, CX - 1, JP - 8, FZ), jnp.float32)
+    slot = slot_rows()
+    zero = jnp.zeros((2 * FY, FZ), jnp.float32)
+    live_planes(occ, [SUB - sx + n for n in range(SUB * (CX - 1))], twice)
+    for k in range(1, CX):
+        acc = (zero,) * 4
+        for j in range(SUB):
+            acc = add_plane(v, twice, slot, SUB * (k - 1) + j, k * SUB - sx + j, acc)
+        store_cells(acc, sy, partial, k - 1)
+    weight = base[STATE + 6 : STATE + 7] * base[STATE + 7 : STATE + 8]
+    place = base[STATE + 8 : STATE + 9].astype(jnp.int32) - JP
+    lz = base[STATE + 9 : STATE + 10].astype(jnp.int32)
+    inner = JP * (CX - 1)
+    hit = lax.broadcasted_iota(jnp.int32, (inner, FZ), 0) == place
+    carried = [
+        jnp.where(hit, base[STATE + 3 + c : STATE + 4 + c] * weight, 0.0) for c in range(3)
+    ]
+    carried.append(jnp.where(hit, weight, 0.0))
+    for p in range(2):
+        first = p * ROWS
+        part[first : first + JP] = base[2 * JP * p : 2 * JP * p + JP]
+        part[first + JP : first + JP + inner] = along_z(partial, carried, sz, lz, p)
+        part[first + CX * JP : first + ROWS] = base[2 * JP * p + JP : 2 * JP * (p + 1)]
+
+
+def inner_sums(grid_shift, v, occ, base):
     return pl.pallas_call(
-        prepare_kernel,
-        out_shape=(struct(STATE, FZ), struct(16, FZ), struct(ROWS, FZ)),
-        in_specs=[IN_VMEM],
+        inner_kernel,
+        out_shape=(struct(2 * ROWS, FZ), struct(16, FZ), struct(ROWS, FZ)),
+        in_specs=[IN_SMEM] + [IN_VMEM] * 3,
         out_specs=(IN_VMEM,) * 3,
-        compiler_params=pltpu.CompilerParams(vmem_limit_bytes=SMALL_LIMIT),
-        cost_estimate=pl.CostEstimate(flops=10_000, bytes_accessed=460_000, transcendentals=0),
-        name="prepare",
-    )(base)
+        scratch_shapes=[
+            VMEM((2 * SUB * (CX - 1) * FY, FZ), jnp.float32),
+            VMEM((4, CX - 1, JP, FZ), jnp.float32),
+        ],
+        compiler_params=pltpu.CompilerParams(vmem_limit_bytes=TURN_LIMIT),
+        cost_estimate=pl.CostEstimate(flops=4_000_000, bytes_accessed=3_700_000, transcendentals=0),
+        name="inner_sums",
+    )(grid_shift, v, occ, base)
 
 
 def add_x(part, odd, even, full):
@@ -673,11 +686,7 @@
 
         planes(plane)
 
-    for n, x in enumerate(places):
-        slots = occ[x].astype(jnp.float32)
-        twice[pl.ds(2 * FY * n, FY, 2), :] = slots
-        twice[pl.ds(2 * FY * n + 1, FY, 2), :] = slots
-
+    live_planes(occ, places, twice)
     for i, k in enumerate(ks):
 
         def column(t, carry, i=i, k=k):
@@ -745,9 +754,9 @@
     mass = colloid_mass
     count = colloid_count
 
-    base, odd, even = cell_sums(grid_shift, count, v, occupancy, axis_index, pos, vel, mass)
+    base, odd, even = border_sums(grid_shift, count, v, occupancy, axis_index, pos, vel, mass)
     odd1, even1 = swap_both(odd, even, "gx")
-    part, state, numbers = prepare(base)
+    part, state, numbers = inner_sums(grid_shift, v, occupancy, base)
     odd, even = columns(part, odd1, even1, state, numbers)
     odd2, even2 = swap_both(odd, even, "yz")
     field, rest, packets = cell_fields(count, part, odd1, even1, odd2, even2, state, numbers)

time: 63.2 us -> 60.8 us (0.962)
  waiting for transfers between devices: 3.2 us -> 0.86 us
    ppermute x10, waiting for transfers between devices: 3.2 us -> 0.86 us  [swapped(): return lax.ppermute(value, axis, pairs)]
  transfers between devices with their start and end apart: 10 -> 10, of which waited for: 3 -> 2; matrix products, arithmetic and copies ran while one was open for 0% -> 0% of each run, Pallas kernels for 11% -> 14%
where the time goes in v3:
time: 60.8 us; the launch traced here: 60.6 us
  starting transfers between devices  24.3 us (40%)
  Pallas kernels  18.1 us (30%)
  blocking collectives  13.8 us (23%)
  local copies, waits for them, and re-layouts  1.94 us (3%)
  between operations  1.6 us (3%)
  waiting for transfers between devices  0.86 us (1%)
    ppermute x10, starting transfers between devices, swapped(): return lax.ppermute(value, axis, pairs)  24.3 us
    all_to_all x1, blocking collectives, per_device(): packets = lax.all_to_all(packets, 'gx', 0, 0)  13.8 us
    pallas_call x3, Pallas kernels, turn_solvent(): pl.pallas_call(functools.partial(turn_kernel, ks), out_shape=struct(*v.sh...  6.77 us
    pallas_call x3, Pallas kernels, substep(): pl.pallas_call(kernel, out_shape=shapes, in_specs=[IN_VMEM] * len(operand...  6.04 us
    pallas_call x1, Pallas kernels, border_sums(): pl.pallas_call(border_kernel, out_shape=(struct(BASE, FZ), struct(32, FZ)...  2.47 us
    unnamed x8, local copies, waits for them, and re-layouts  1.94 us
    pallas_call x1, Pallas kernels, inner_sums(): pl.pallas_call(inner_kernel, out_shape=(struct(2 * ROWS, FZ), struct(16,...  1.6 us
  transfers between devices with their start and end apart: 10, of which 2 were waited for; matrix products, arithmetic and copies ran while one was open for 0% of the time, Pallas kernels for 14%

profile of v3, /device:TPU:1, one launch (start us, length us, event | category | flops | bytes accessed | tf_op | source)
XLA Modules:
  0.0 60.6 jit_solution(4854966162395080456)
XLA Ops:
  0.6 0.0 copy-start.3
  0.6 0.0 copy-start
  1.4 2.5 %border_sums.1 = (f32[224,128]{1,0:T(8,128)}, f32[32,128]{1,0:T(8,128)}, f32[32,128]{1,0:T(8,128)}) custom-call(s32[3]{0:T(128)} %shift.7, s32[1,1]{1,0:T(1,128)S(6)} %copy.17.count_at.count, f32[3,32,64,128]{3,2,1,0:T(8,128)} %bitcast.10, s32[32,32,128]{2,1,0:T(8,128)} %occ.7, s32[8,8,64]{2,1,0:T(8,128)} %axis_at.1, f32[3,1,128]{2,1,0:T(1,128)} %bitcast.16, ...), custom_call_target="tpu_custom_call" | custom-call | flops 1000000 | bytes 800000 | tf_op jit(solution)/shard_map/border_sums/pallas_call | solution.py:214
  3.9 9.4 %collective-permute-start = (f32[32,128]{1,0:T(8,128)}, f32[32,128]{1,0:T(8,128)S(1)}, u32[]{:S(2)}, u32[]{:S(2)}) collective-permute-start(f32[32,128]{1,0:T(8,128)} %get-tuple-element.36), channel_id=1, source_target_pairs={{16,32},{32,16},{48,64},{64,48},{80,96},{96,80},{112,128},{128,112... | collective-permute-start | bytes 49160 | tf_op jit(solution)/shard_map/ppermute | solution.py:57
  13.3 0.0 collective-permute-start.1
  13.3 0.0 copy-done.3
  13.3 0.0 copy-done
  13.3 0.0 copy-start.1
  13.3 1.0 %copy-done.1 = s32[32,32,128]{2,1,0:T(8,128)S(1)} copy-done((s32[32,32,128]{2,1,0:T(8,128)S(1)}, s32[32,32,128]{2,1,0:T(8,128)}, u32[]{:S(2)}) %copy-start.1) | copy-done | bytes 524312
  14.4 0.0 copy-start.2
  14.4 0.9 %copy-done.2 = f32[224,128]{1,0:T(8,128)S(1)} copy-done((f32[224,128]{1,0:T(8,128)S(1)}, f32[224,128]{1,0:T(8,128)}, u32[]{:S(2)}) %copy-start.2) | copy-done | bytes 114712
  15.3 1.6 %inner_sums.1 = (f32[288,128]{1,0:T(8,128)S(1)}, f32[16,128]{1,0:T(8,128)S(1)}, f32[144,128]{1,0:T(8,128)S(1)}) custom-call(s32[3]{0:T(128)S(1)} %copy-done.3, f32[3,32,64,128]{3,2,1,0:T(8,128)S(1)} %bitcast.11, s32[32,32,128]{2,1,0:T(8,128)S(1)} %copy-done.1, f32[224,128]{1,0:T(8,128)S(1)} %copy-done.2), custom_call_target="tpu_custom_call" | custom-call | flops 4000000 | bytes 3700000 | tf_op jit(solution)/shard_map/inner_sums/pallas_call | solution.py:267
  16.9 0.0 collective-permute-done.odd1
  16.9 0.0 collective-permute-done.1.even1
  16.9 2.5 %collective-permute-start.2 = (f32[40,128]{1,0:T(8,128)S(1)}, f32[40,128]{1,0:T(8,128)S(1)}, u32[]{:S(2)}, u32[]{:S(2)}) collective-permute-start(f32[40,128]{1,0:T(8,128)S(1)} %get-tuple-element.40), channel_id=1, source_target_pairs={{1,2},{2,1},{3,4},{4,3},{5,6},{6,5},{7,8},{8,7},{9,10},{10,9},{11,... | collective-permute-start | bytes 61448 | tf_op jit(solution)/shard_map/ppermute | solution.py:57
  19.4 0.9 %collective-permute-start.3 = (f32[40,128]{1,0:T(8,128)S(1)}, f32[40,128]{1,0:T(8,128)S(1)}, u32[]{:S(2)}, u32[]{:S(2)}) collective-permute-start(f32[40,128]{1,0:T(8,128)S(1)} %get-tuple-element.41), channel_id=1, source_target_pairs={{0,1},{1,0},{2,3},{3,2},{4,5},{5,4},{6,7},{7,6},{8,9},{9,8},{10,11... | collective-permute-start | bytes 61448 | tf_op jit(solution)/shard_map/ppermute | solution.py:57
  20.4 0.5 collective-permute-done.2.odd2
  20.9 0.3 collective-permute-done.3.even2
  21.2 1.2 %cell_fields.1 = (f32[6,144,128]{2,1,0:T(8,128)S(1)}, f32[8,128]{1,0:T(8,128)S(1)}, f32[16,8,128]{2,1,0:T(8,128)S(1)}) custom-call(s32[1,1]{1,0:T(1,128)S(6)} %copy.17.count_at.count, f32[288,128]{1,0:T(8,128)S(1)} %get-tuple-element.35.part, f32[32,128]{1,0:T(8,128)S(1)} %collective-permute-done.odd1, f32[32,128]{1,0:T(8,128)S(1)} %collective-permute-done.1.even1, ...), custom_call_target="tpu_custom_call" | custom-call | flops 4000000 | bytes 1000000 | tf_op jit(solution)/shard_map/cell_fields/pallas_call | solution.py:514
  22.4 13.8 %all_to_all.5.packets = f32[16,8,128]{2,1,0:T(8,128)S(1)} all-to-all(f32[16,8,128]{2,1,0:T(8,128)S(1)} %get-tuple-element.42), channel_id=1, replica_groups=mesh['gx'=16,'yz'=16] {'gx'}, dimensions={0} | all-to-all | bytes 131072 | tf_op jit(solution)/shard_map/all_to_all | solution.py:763
  36.2 3.3 %collective-permute-start.4 = (f32[32,128]{1,0:T(8,128)S(1)}, f32[32,128]{1,0:T(8,128)S(1)}, u32[]{:S(2)}, u32[]{:S(2)}) collective-permute-start(f32[32,128]{1,0:T(8,128)S(1)} %get-tuple-element.45.row), channel_id=1, source_target_pairs={{1,2},{2,1},{3,4},{4,3},{5,6},{6,5},{7,8},{8,7},{9,10},{10,9},{11,... | collective-permute-start | bytes 49160 | tf_op jit(solution)/shard_map/ppermute | solution.py:57
  39.5 1.5 %collective-permute-start.5 = (f32[32,128]{1,0:T(8,128)S(1)}, f32[32,128]{1,0:T(8,128)S(1)}, u32[]{:S(2)}, u32[]{:S(2)}) collective-permute-start(f32[32,128]{1,0:T(8,128)S(1)} %get-tuple-element.45.row), channel_id=1, source_target_pairs={{0,1},{1,0},{2,3},{3,2},{4,5},{5,4},{6,7},{7,6},{8,9},{9,8},{10,11... | collective-permute-start | bytes 49160 | tf_op jit(solution)/shard_map/ppermute | solution.py:57
  41.0 2.2 %turn_solvent.3.refs_0_ = f32[3,32,64,128]{3,2,1,0:T(8,128)} custom-call(s32[3]{0:T(128)S(1)} %copy-done.3, f32[3,32,64,128]{3,2,1,0:T(8,128)S(1)} %bitcast.12, s32[32,32,128]{2,1,0:T(8,128)S(1)} %copy-done.1, f32[6,144,128]{2,1,0:T(8,128)S(1)} %get-tuple-element.47.field), custom_call_target="tpu_custom_call" | custom-call | flops 3000000 | bytes 1300000 | tf_op jit(solution)/shard_map/turn_solvent/pallas_call | solution.py:723
  43.2 0.0 collective-permute-done.4.odd
  43.2 0.0 collective-permute-done.5.even
  43.2 2.8 %substep.3 = (f32[24,128]{1,0:T(8,128)S(1)}, f32[16,128]{1,0:T(8,128)S(1)}) custom-call(f32[32,128]{1,0:T(8,128)S(1)} %get-tuple-element.45.row, f32[24,128]{1,0:T(8,128)S(1)} %get-tuple-element.46.moving, f32[32,128]{1,0:T(8,128)S(1)} %collective-permute-done.4.odd, f32[32,128]{1,0:T(8,128)S(1)} %collective-permute-done.5.even), custom_call_target="tpu_custom_call" | custom-call | flops 20000000 | bytes 100000 | tf_op jit(solution)/shard_map/substep/pallas_call | solution.py:613
  46.0 0.4 collective-permute-start.6
  46.4 3.3 %collective-permute-start.7 = (f32[24,128]{1,0:T(8,128)S(1)}, f32[24,128]{1,0:T(8,128)S(1)}, u32[]{:S(2)}, u32[]{:S(2)}) collective-permute-start(f32[24,128]{1,0:T(8,128)S(1)} %get-tuple-element.51.row), channel_id=1, source_target_pairs={{0,1},{1,0},{2,3},{3,2},{4,5},{5,4},{6,7},{7,6},{8,9},{9,8},{10,11... | collective-permute-start | bytes 36872 | tf_op jit(solution)/shard_map/ppermute | solution.py:57
  49.6 2.2 %turn_solvent.4.refs_0_ = f32[3,32,64,128]{3,2,1,0:T(8,128)} custom-call(s32[3]{0:T(128)S(1)} %copy-done.3, f32[3,32,64,128]{3,2,1,0:T(8,128)S(1)} %bitcast.13, s32[32,32,128]{2,1,0:T(8,128)S(1)} %copy-done.1, f32[6,144,128]{2,1,0:T(8,128)S(1)} %get-tuple-element.47.field, f32[3,32,64,128]{3,2,1,0:T(8,128)} %turn_solvent.3.refs_0_), custom_call_target="tpu_custom_call", output_to_operand_aliasing={{}: (4, {})} | custom-call | flops 3000000 | bytes 1300000 | tf_op jit(solution)/shard_map/turn_solvent/pallas_call | solution.py:723
  51.9 0.0 collective-permute-done.6.odd
  51.9 0.0 collective-permute-done.7.even
  51.9 1.9 %substep.4 = (f32[16,128]{1,0:T(8,128)S(1)}, f32[8,128]{1,0:T(8,128)S(1)}) custom-call(f32[24,128]{1,0:T(8,128)S(1)} %get-tuple-element.51.row, f32[16,128]{1,0:T(8,128)S(1)} %get-tuple-element.52.moving, f32[24,128]{1,0:T(8,128)S(1)} %collective-permute-done.6.odd, f32[24,128]{1,0:T(8,128)S(1)} %collective-permute-done.7.even), custom_call_target="tpu_custom_call" | custom-call | flops 12000000 | bytes 100000 | tf_op jit(solution)/shard_map/substep/pallas_call | solution.py:613
  53.8 0.1 collective-permute-start.8
  53.9 3.0 %collective-permute-start.9 = (f32[16,128]{1,0:T(8,128)S(1)}, f32[16,128]{1,0:T(8,128)S(1)}, u32[]{:S(2)}, u32[]{:S(2)}) collective-permute-start(f32[16,128]{1,0:T(8,128)S(1)} %get-tuple-element.57.row), channel_id=1, source_target_pairs={{0,1},{1,0},{2,3},{3,2},{4,5},{5,4},{6,7},{7,6},{8,9},{9,8},{10,11... | collective-permute-start | bytes 24584 | tf_op jit(solution)/shard_map/ppermute | solution.py:57
  57.0 2.3 %turn_solvent.5 = f32[3,32,64,128]{3,2,1,0:T(8,128)} custom-call(s32[3]{0:T(128)S(1)} %copy-done.3, f32[3,32,64,128]{3,2,1,0:T(8,128)S(1)} %bitcast.14, s32[32,32,128]{2,1,0:T(8,128)S(1)} %copy-done.1, f32[6,144,128]{2,1,0:T(8,128)S(1)} %get-tuple-element.47.field, f32[3,32,64,128]{3,2,1,0:T(8,128)} %turn_solvent.4.refs_0_), custom_call_target="tpu_custom_call", output_to_operand_aliasing={{}: (4, {})} | custom-call | flops 3000000 | bytes 1300000 | tf_op jit(solution)/shard_map/turn_solvent/pallas_call | solution.py:723
  59.3 0.0 collective-permute-done.8.odd
  59.3 0.0 collective-permute-done.9.even
  59.3 1.3 %substep.5 = (f32[3,1,128]{2,1,0:T(1,128)}, f32[3,1,128]{2,1,0:T(1,128)}) custom-call(f32[16,128]{1,0:T(8,128)S(1)} %get-tuple-element.57.row, f32[8,128]{1,0:T(8,128)S(1)} %get-tuple-element.60.moving, f32[16,128]{1,0:T(8,128)S(1)} %collective-permute-done.8.odd, f32[16,128]{1,0:T(8,128)S(1)} %collective-permute-done.9.even, ...), custom_call_target="tpu_custom_call" | custom-call | flops 4000000 | bytes 100000 | tf_op jit(solution)/shard_map/substep/pallas_call | solution.py:613
  (2 shorter events, 0.0 us)
Async XLA Ops:
  0.6 12.7 %copy-start.3 = (s32[3]{0:T(128)S(1)}, s32[3]{0:T(128)}, u32[]{:S(2)}) copy-start(s32[3]{0:T(128)} %shift.7) | copy-start | bytes 40
  0.6 12.7 %copy-start = (f32[3,32,32,2,128]{4,3,2,1,0:T(2,128)S(1)}, f32[3,32,32,2,128]{4,3,2,1,0:T(2,128)}, u32[]{:S(2)}) copy-start(f32[3,32,32,2,128]{4,3,2,1,0:T(2,128)} %param.8) | copy-start | bytes 9437188
  3.9 13.0 %collective-permute-start = (f32[32,128]{1,0:T(8,128)}, f32[32,128]{1,0:T(8,128)S(1)}, u32[]{:S(2)}, u32[]{:S(2)}) collective-permute-start(f32[32,128]{1,0:T(8,128)} %get-tuple-element.36), channel_id=1, source_target_pairs={{16,32},{32,16},{48,64},{64,48},{80,96},{96,80},{112,128},{128,112... | collective-permute-start | bytes 49160 | tf_op jit(solution)/shard_map/ppermute | solution.py:57
  13.3 3.6 %collective-permute-start.1 = (f32[32,128]{1,0:T(8,128)}, f32[32,128]{1,0:T(8,128)S(1)}, u32[]{:S(2)}, u32[]{:S(2)}) collective-permute-start(f32[32,128]{1,0:T(8,128)} %get-tuple-element.37), channel_id=1, source_target_pairs={{0,16},{16,0},{32,48},{48,32},{64,80},{80,64},{96,112},{112,96},{1... | collective-permute-start | bytes 49160 | tf_op jit(solution)/shard_map/ppermute | solution.py:57
  13.3 1.0 %copy-start.1 = (s32[32,32,128]{2,1,0:T(8,128)S(1)}, s32[32,32,128]{2,1,0:T(8,128)}, u32[]{:S(2)}) copy-start(s32[32,32,128]{2,1,0:T(8,128)} %occ.7) | copy-start | bytes 1572868
  14.4 0.9 %copy-start.2 = (f32[224,128]{1,0:T(8,128)S(1)}, f32[224,128]{1,0:T(8,128)}, u32[]{:S(2)}) copy-start(f32[224,128]{1,0:T(8,128)} %get-tuple-element.34.base) | copy-start | bytes 344068
  16.9 4.0 %collective-permute-start.2 = (f32[40,128]{1,0:T(8,128)S(1)}, f32[40,128]{1,0:T(8,128)S(1)}, u32[]{:S(2)}, u32[]{:S(2)}) collective-permute-start(f32[40,128]{1,0:T(8,128)S(1)} %get-tuple-element.40), channel_id=1, source_target_pairs={{1,2},{2,1},{3,4},{4,3},{5,6},{6,5},{7,8},{8,7},{9,10},{10,9},{11,... | collective-permute-start | bytes 61448 | tf_op jit(solution)/shard_map/ppermute | solution.py:57
  19.4 1.8 %collective-permute-start.3 = (f32[40,128]{1,0:T(8,128)S(1)}, f32[40,128]{1,0:T(8,128)S(1)}, u32[]{:S(2)}, u32[]{:S(2)}) collective-permute-start(f32[40,128]{1,0:T(8,128)S(1)} %get-tuple-element.41), channel_id=1, source_target_pairs={{0,1},{1,0},{2,3},{3,2},{4,5},{5,4},{6,7},{7,6},{8,9},{9,8},{10,11... | collective-permute-start | bytes 61448 | tf_op jit(solution)/shard_map/ppermute | solution.py:57
  36.2 7.0 %collective-permute-start.4 = (f32[32,128]{1,0:T(8,128)S(1)}, f32[32,128]{1,0:T(8,128)S(1)}, u32[]{:S(2)}, u32[]{:S(2)}) collective-permute-start(f32[32,128]{1,0:T(8,128)S(1)} %get-tuple-element.45.row), channel_id=1, source_target_pairs={{1,2},{2,1},{3,4},{4,3},{5,6},{6,5},{7,8},{8,7},{9,10},{10,9},{11,... | collective-permute-start | bytes 49160 | tf_op jit(solution)/shard_map/ppermute | solution.py:57
  39.5 3.8 %collective-permute-start.5 = (f32[32,128]{1,0:T(8,128)S(1)}, f32[32,128]{1,0:T(8,128)S(1)}, u32[]{:S(2)}, u32[]{:S(2)}) collective-permute-start(f32[32,128]{1,0:T(8,128)S(1)} %get-tuple-element.45.row), channel_id=1, source_target_pairs={{0,1},{1,0},{2,3},{3,2},{4,5},{5,4},{6,7},{7,6},{8,9},{9,8},{10,11... | collective-permute-start | bytes 49160 | tf_op jit(solution)/shard_map/ppermute | solution.py:57
  46.0 5.9 %collective-permute-start.6 = (f32[24,128]{1,0:T(8,128)S(1)}, f32[24,128]{1,0:T(8,128)S(1)}, u32[]{:S(2)}, u32[]{:S(2)}) collective-permute-start(f32[24,128]{1,0:T(8,128)S(1)} %get-tuple-element.51.row), channel_id=1, source_target_pairs={{1,2},{2,1},{3,4},{4,3},{5,6},{6,5},{7,8},{8,7},{9,10},{10,9},{11,... | collective-permute-start | bytes 36872 | tf_op jit(solution)/shard_map/ppermute | solution.py:57
  46.4 5.5 %collective-permute-start.7 = (f32[24,128]{1,0:T(8,128)S(1)}, f32[24,128]{1,0:T(8,128)S(1)}, u32[]{:S(2)}, u32[]{:S(2)}) collective-permute-start(f32[24,128]{1,0:T(8,128)S(1)} %get-tuple-element.51.row), channel_id=1, source_target_pairs={{0,1},{1,0},{2,3},{3,2},{4,5},{5,4},{6,7},{7,6},{8,9},{9,8},{10,11... | collective-permute-start | bytes 36872 | tf_op jit(solution)/shard_map/ppermute | solution.py:57
  53.8 5.4 %collective-permute-start.8 = (f32[16,128]{1,0:T(8,128)S(1)}, f32[16,128]{1,0:T(8,128)S(1)}, u32[]{:S(2)}, u32[]{:S(2)}) collective-permute-start(f32[16,128]{1,0:T(8,128)S(1)} %get-tuple-element.57.row), channel_id=1, source_target_pairs={{1,2},{2,1},{3,4},{4,3},{5,6},{6,5},{7,8},{8,7},{9,10},{10,9},{11,... | collective-permute-start | bytes 24584 | tf_op jit(solution)/shard_map/ppermute | solution.py:57
  53.9 5.3 %collective-permute-start.9 = (f32[16,128]{1,0:T(8,128)S(1)}, f32[16,128]{1,0:T(8,128)S(1)}, u32[]{:S(2)}, u32[]{:S(2)}) collective-permute-start(f32[16,128]{1,0:T(8,128)S(1)} %get-tuple-element.57.row), channel_id=1, source_target_pairs={{0,1},{1,0},{2,3},{3,2},{4,5},{5,4},{6,7},{7,6},{8,9},{9,8},{10,11... | collective-permute-start | bytes 24584 | tf_op jit(solution)/shard_map/ppermute | solution.py:57

commit v4 on v3

--- a/solution.py
+++ b/solution.py
@@ -65,14 +65,14 @@
     return jax.ShapeDtypeStruct(shape, jnp.float32)
 
 
-def exact_dot(left, right, dims):
+def exact_dot(left, right, dims, parts=3):
     right = right.astype(jnp.bfloat16)
     total = None
-    for part in range(3):
+    for part in range(parts):
         piece = left.astype(jnp.bfloat16)
         term = lax.dot_general(piece, right, dims, preferred_element_type=jnp.float32)
         total = term if total is None else total + term
-        if part < 2:
+        if part < parts - 1:
             left = left - piece.astype(jnp.float32)
     return total
 
@@ -323,40 +323,66 @@
     )(part, odd1, even1, state, numbers)
 
 
+def store_around(rows, base, others):
+    wide = [[jnp.broadcast_to(value, (8, FZ)) for value in packet] for packet in others]
+    low = lax.broadcasted_iota(jnp.int32, (8, FZ), 1) < FZ // 2
+    reach = None
+    for c in range(4):
+        rows[base + c] = wide[0][c]
+        for p in range(4):
+            a, b = wide[1 + 2 * p][c], wide[2 + 2 * p][c]
+            rows[base + 4 + 4 * p + c] = jnp.where(low, a, pltpu.roll(b, FZ // 2, 1))
+            late = jnp.where(low, pltpu.roll(a, FZ // 2, 1), b)
+            rows[base + 20 + 4 * p + c] = late
+            if c == 3:
+                reach = late if reach is None else jnp.maximum(reach, late)
+    return jnp.max(reach) > 0.0
+
+
 def pair_force(devices, rows, terms):
     ones = jnp.ones((8, FZ), jnp.bfloat16)
     slot = lax.broadcasted_iota(jnp.int32, (FZ, FZ), 0)
     sub = TILE // 8
 
     for n, (own, live, others) in enumerate(devices):
+        base = 36 * n
+        crowded = store_around(rows, base, others)
         column = jnp.concatenate(list(own) + [jnp.zeros((5, FZ), jnp.float32)], axis=0).T
 
-        def tile(t, n=n, column=column, others=others):
+        def tile(t, n=n, column=column, base=base, crowded=crowded):
             part = column[TILE * t : TILE * t + TILE]
             mine = [
                 jnp.broadcast_to(part[:, c : c + 1], (TILE, FZ)).reshape(sub, 8, FZ)
                 for c in range(3)
             ]
-            moved = {step: mine[0] - step * float(CX) for step in (-1, 0, 1)}
-            total = None
-            for place, step in others:
-                dx = moved[step] - rows[4 * place][None]
-                dy = mine[1] - rows[4 * place + 1][None]
-                dz = mine[2] - rows[4 * place + 2][None]
-                dz = jnp.where(
-                    dz > 0.5 * CZ, dz - CZ, jnp.where(dz < -0.5 * CZ, dz + CZ, dz)
-                )
-                reach = jnp.maximum(
-                    rows[4 * place + 3][None]
-                    - (dx * dx + dy * dy + dz * dz) * (1.0 / (cutoff * cutoff)),
-                    0.0,
-                )
-                weight = reach * reach
-                new = (weight * dx, weight * dy, weight * dz)
-                total = new if total is None else tuple(a + b for a, b in zip(total, new))
-            for c in range(3):
-                start = FZ * (3 * n + c) + TILE * t
-                terms[start : start + TILE] = total[c].reshape(TILE, FZ)
+
+            def force(places):
+                total = None
+                for place in places:
+                    dx = mine[0] - rows[place][None]
+                    dy = mine[1] - rows[place + 1][None]
+                    dz = mine[2] - rows[place + 2][None]
+                    dz = jnp.where(
+                        dz > 0.5 * CZ, dz - CZ, jnp.where(dz < -0.5 * CZ, dz + CZ, dz)
+                    )
+                    reach = jnp.maximum(
+                        rows[place + 3][None]
+                        - (dx * dx + dy * dy + dz * dz) * (1.0 / (cutoff * cutoff)),
+                        0.0,
+                    )
+                    weight = reach * reach
+                    new = (weight * dx, weight * dy, weight * dz)
+                    total = new if total is None else tuple(a + b for a, b in zip(total, new))
+                return total
+
+            at = [pl.ds(FZ * (3 * n + c) + TILE * t, TILE) for c in range(3)]
+            for c, value in enumerate(force(range(base, base + 20, 4))):
+                terms[at[c], :] = value.reshape(TILE, FZ)
+
+            @pl.when(crowded)
+            def _():
+                for c, value in enumerate(force(range(base + 20, base + 36, 4))):
+                    terms[at[c], :] = terms[at[c], :] + value.reshape(TILE, FZ)
 
         for t in range(FZ // TILE):
             pl.when(TILE * t < live)(functools.partial(tile, t))
@@ -367,11 +393,11 @@
             jnp.concatenate([slot < live] * 3), terms[3 * FZ * n : 3 * FZ * (n + 1)], 0.0
         )
         back = None
-        for part in range(3):
+        for part in range(2):
             piece = left.astype(jnp.bfloat16)
             term = lax.dot_general(ones, piece, NT, preferred_element_type=jnp.float32)
             back = term if back is None else back + term
-            if part < 2:
+            if part < 1:
                 left = left - piece.astype(jnp.float32)
         forces.append([stiffness * back[0:1, FZ * c : FZ * c + FZ] for c in range(3)])
     return forces
@@ -379,16 +405,18 @@
 
 def pair_scratch(width):
     return [
-        VMEM((12 * (width + 2), 8, FZ), jnp.float32),
+        VMEM((36 * width, 8, FZ), jnp.float32),
         VMEM((3 * FZ * width, FZ), jnp.float32),
     ]
 
 
-def store_rows(rows, place, packet, step_y):
+def placed(packet, step_x, step_y):
     x, y, z, alive = packet
-    values = (x, y + step_y, z, jnp.where(alive > 0.0, 1.0, -1.0))
-    for c in range(4):
-        rows[4 * place + c] = jnp.broadcast_to(values[c], (8, FZ))
+    return (x + step_x, y + step_y, z, jnp.where(alive > 0.0, 1.0, -1.0))
+
+
+def middle_first(values):
+    return values[4:5] + values[:4] + values[5:]
 
 
 def toward(axis, cells):
@@ -495,15 +523,15 @@
     rest_out[0:7] = state[0:7]
     rest_out[7:8] = alive_row
     after = parity("gx") == 1
+    others = []
     for b in range(3):
         step_y = (1 - b) * toward("yz", CY)
         slots = [rows(b, a) for a in range(3)]
         first = [jnp.where(after, e, o) for o, e in zip(slots[0], slots[2])]
         last = [jnp.where(after, o, e) for o, e in zip(slots[0], slots[2])]
         for a, packet in enumerate((first, slots[1], last)):
-            store_rows(pair_rows, 3 * b + a, packet, step_y)
-    others = [(3 * b + a, a - 1) for b in range(3) for a in range(3)]
-    force = pair_force([(own, count[0, 0], others)], pair_rows, pair_terms)[0]
+            others.append(placed(packet, (a - 1) * float(CX), step_y))
+    force = pair_force([(own, count[0, 0], middle_first(others))], pair_rows, pair_terms)[0]
     moved, velocity = advance(own, velocity, state[6:7], alive_row, force)
     packet = jnp.concatenate(moved + [alive_row] + velocity + [state[6:7]], axis=0)
     for g in range(packets.shape[0]):
@@ -561,18 +589,19 @@
 
 
 def substep_moves(width, row, moving, odd, even, rows, terms):
-    span = width + 2
-    for b, source in enumerate((odd, row, even)):
-        step_y = (1 - b) * toward("yz", CY)
-        for a in range(span):
-            packet = [source[4 * a + c : 4 * a + c + 1] for c in range(4)]
-            store_rows(rows, span * b + a, packet, step_y)
+    sources = (odd, row, even)
     devices = []
     for n in range(width):
         at = 4 * (n + 1)
         own = [row[at + c : at + c + 1] for c in range(3)]
-        others = [(span * b + n + 1 + step, step) for b in range(3) for step in (-1, 0, 1)]
-        devices.append((own, live_count(row[at + 3 : at + 4]), others))
+        others = []
+        for b, source in enumerate(sources):
+            step_y = (1 - b) * toward("yz", CY)
+            for step in (-1, 0, 1):
+                start = at + 4 * step
+                packet = [source[start + c : start + c + 1] for c in range(4)]
+                others.append(placed(packet, step * float(CX), step_y))
+        devices.append((own, live_count(row[at + 3 : at + 4]), middle_first(others)))
     forces = pair_force(devices, rows, terms)
     results = []
     for n in range(width):
@@ -660,7 +689,7 @@
     layers = list(ks) + ([0] if CX in ks else [])
     for f in range(6):
         left = jnp.concatenate([field[f, JP * k : JP * k + JP] for k in layers])
-        both = exact_dot(left, right, NN)
+        both = exact_dot(left, right, NN, parts=2)
         wide[2 * f] = both[:, :FZ]
         wide[2 * f + 1] = both[:, FZ:]
     row = lax.broadcasted_iota(jnp.int32, (8, FZ), 0)

time: 60.8 us -> 60.1 us (0.988)
  no operation moved by 1% of the time
where the time goes in v4:
time: 60.1 us; the launch traced here: 59.9 us
  starting transfers between devices  24.3 us (40%)
  Pallas kernels  17.6 us (29%)
  blocking collectives  13.6 us (23%)
  local copies, waits for them, and re-layouts  1.94 us (3%)
  between operations  1.6 us (3%)
  waiting for transfers between devices  0.86 us (1%)
    ppermute x10, starting transfers between devices, swapped(): return lax.ppermute(value, axis, pairs)  24.3 us
    all_to_all x1, blocking collectives, per_device(): packets = lax.all_to_all(packets, 'gx', 0, 0)  13.6 us
    pallas_call x3, Pallas kernels, turn_solvent(): pl.pallas_call(functools.partial(turn_kernel, ks), out_shape=struct(*v.sh...  6.62 us
    pallas_call x3, Pallas kernels, substep(): pl.pallas_call(kernel, out_shape=shapes, in_specs=[IN_VMEM] * len(operand...  5.82 us
    pallas_call x1, Pallas kernels, border_sums(): pl.pallas_call(border_kernel, out_shape=(struct(BASE, FZ), struct(32, FZ)...  2.47 us
    unnamed x8, local copies, waits for them, and re-layouts  1.94 us
    pallas_call x1, Pallas kernels, inner_sums(): pl.pallas_call(inner_kernel, out_shape=(struct(2 * ROWS, FZ), struct(16,...  1.6 us
  transfers between devices with their start and end apart: 10, of which 2 were waited for; matrix products, arithmetic and copies ran while one was open for 0% of the time, Pallas kernels for 14%

profile of v4, /device:TPU:1, one launch (start us, length us, event | category | flops | bytes accessed | tf_op | source)
XLA Modules:
  0.0 59.9 jit_solution(15637101360163561411)
XLA Ops:
  0.6 0.0 copy-start.3
  0.6 0.0 copy-start
  1.4 2.5 %border_sums.1 = (f32[224,128]{1,0:T(8,128)}, f32[32,128]{1,0:T(8,128)}, f32[32,128]{1,0:T(8,128)}) custom-call(s32[3]{0:T(128)} %shift.7, s32[1,1]{1,0:T(1,128)S(6)} %copy.17.count_at.count, f32[3,32,64,128]{3,2,1,0:T(8,128)} %bitcast.10, s32[32,32,128]{2,1,0:T(8,128)} %occ.7, s32[8,8,64]{2,1,0:T(8,128)} %axis_at.1, f32[3,1,128]{2,1,0:T(1,128)} %bitcast.16, ...), custom_call_target="tpu_custom_call" | custom-call | flops 1000000 | bytes 800000 | tf_op jit(solution)/shard_map/border_sums/pallas_call | solution.py:214
  3.9 9.4 %collective-permute-start = (f32[32,128]{1,0:T(8,128)}, f32[32,128]{1,0:T(8,128)S(1)}, u32[]{:S(2)}, u32[]{:S(2)}) collective-permute-start(f32[32,128]{1,0:T(8,128)} %get-tuple-element.36), channel_id=1, source_target_pairs={{16,32},{32,16},{48,64},{64,48},{80,96},{96,80},{112,128},{128,112... | collective-permute-start | bytes 49160 | tf_op jit(solution)/shard_map/ppermute | solution.py:57
  13.3 0.0 collective-permute-start.1
  13.3 0.0 copy-done.3
  13.3 0.0 copy-done
  13.3 0.0 copy-start.1
  13.3 1.0 %copy-done.1 = s32[32,32,128]{2,1,0:T(8,128)S(1)} copy-done((s32[32,32,128]{2,1,0:T(8,128)S(1)}, s32[32,32,128]{2,1,0:T(8,128)}, u32[]{:S(2)}) %copy-start.1) | copy-done | bytes 524312
  14.4 0.0 copy-start.2
  14.4 0.9 %copy-done.2 = f32[224,128]{1,0:T(8,128)S(1)} copy-done((f32[224,128]{1,0:T(8,128)S(1)}, f32[224,128]{1,0:T(8,128)}, u32[]{:S(2)}) %copy-start.2) | copy-done | bytes 114712
  15.3 1.6 %inner_sums.1 = (f32[288,128]{1,0:T(8,128)S(1)}, f32[16,128]{1,0:T(8,128)S(1)}, f32[144,128]{1,0:T(8,128)S(1)}) custom-call(s32[3]{0:T(128)S(1)} %copy-done.3, f32[3,32,64,128]{3,2,1,0:T(8,128)S(1)} %bitcast.11, s32[32,32,128]{2,1,0:T(8,128)S(1)} %copy-done.1, f32[224,128]{1,0:T(8,128)S(1)} %copy-done.2), custom_call_target="tpu_custom_call" | custom-call | flops 4000000 | bytes 3700000 | tf_op jit(solution)/shard_map/inner_sums/pallas_call | solution.py:267
  16.9 0.0 collective-permute-done.odd1
  16.9 0.0 collective-permute-done.1.even1
  16.9 2.5 %collective-permute-start.2 = (f32[40,128]{1,0:T(8,128)S(1)}, f32[40,128]{1,0:T(8,128)S(1)}, u32[]{:S(2)}, u32[]{:S(2)}) collective-permute-start(f32[40,128]{1,0:T(8,128)S(1)} %get-tuple-element.40), channel_id=1, source_target_pairs={{1,2},{2,1},{3,4},{4,3},{5,6},{6,5},{7,8},{8,7},{9,10},{10,9},{11,... | collective-permute-start | bytes 61448 | tf_op jit(solution)/shard_map/ppermute | solution.py:57
  19.4 0.9 %collective-permute-start.3 = (f32[40,128]{1,0:T(8,128)S(1)}, f32[40,128]{1,0:T(8,128)S(1)}, u32[]{:S(2)}, u32[]{:S(2)}) collective-permute-start(f32[40,128]{1,0:T(8,128)S(1)} %get-tuple-element.41), channel_id=1, source_target_pairs={{0,1},{1,0},{2,3},{3,2},{4,5},{5,4},{6,7},{7,6},{8,9},{9,8},{10,11... | collective-permute-start | bytes 61448 | tf_op jit(solution)/shard_map/ppermute | solution.py:57
  20.4 0.5 collective-permute-done.2.odd2
  20.9 0.3 collective-permute-done.3.even2
  21.2 1.0 %cell_fields.1 = (f32[6,144,128]{2,1,0:T(8,128)S(1)}, f32[8,128]{1,0:T(8,128)S(1)}, f32[16,8,128]{2,1,0:T(8,128)S(1)}) custom-call(s32[1,1]{1,0:T(1,128)S(6)} %copy.17.count_at.count, f32[288,128]{1,0:T(8,128)S(1)} %get-tuple-element.35.part, f32[32,128]{1,0:T(8,128)S(1)} %collective-permute-done.odd1, f32[32,128]{1,0:T(8,128)S(1)} %collective-permute-done.1.even1, ...), custom_call_target="tpu_custom_call" | custom-call | flops 4000000 | bytes 1000000 | tf_op jit(solution)/shard_map/cell_fields/pallas_call | solution.py:542
  22.2 13.6 %all_to_all.5.packets = f32[16,8,128]{2,1,0:T(8,128)S(1)} all-to-all(f32[16,8,128]{2,1,0:T(8,128)S(1)} %get-tuple-element.42), channel_id=1, replica_groups=mesh['gx'=16,'yz'=16] {'gx'}, dimensions={0} | all-to-all | bytes 131072 | tf_op jit(solution)/shard_map/all_to_all | solution.py:792
  35.9 3.4 %collective-permute-start.4 = (f32[32,128]{1,0:T(8,128)S(1)}, f32[32,128]{1,0:T(8,128)S(1)}, u32[]{:S(2)}, u32[]{:S(2)}) collective-permute-start(f32[32,128]{1,0:T(8,128)S(1)} %get-tuple-element.45.row), channel_id=1, source_target_pairs={{1,2},{2,1},{3,4},{4,3},{5,6},{6,5},{7,8},{8,7},{9,10},{10,9},{11,... | collective-permute-start | bytes 49160 | tf_op jit(solution)/shard_map/ppermute | solution.py:57
  39.3 1.3 %collective-permute-start.5 = (f32[32,128]{1,0:T(8,128)S(1)}, f32[32,128]{1,0:T(8,128)S(1)}, u32[]{:S(2)}, u32[]{:S(2)}) collective-permute-start(f32[32,128]{1,0:T(8,128)S(1)} %get-tuple-element.45.row), channel_id=1, source_target_pairs={{0,1},{1,0},{2,3},{3,2},{4,5},{5,4},{6,7},{7,6},{8,9},{9,8},{10,11... | collective-permute-start | bytes 49160 | tf_op jit(solution)/shard_map/ppermute | solution.py:57
  40.6 2.2 %turn_solvent.3.refs_0_ = f32[3,32,64,128]{3,2,1,0:T(8,128)} custom-call(s32[3]{0:T(128)S(1)} %copy-done.3, f32[3,32,64,128]{3,2,1,0:T(8,128)S(1)} %bitcast.12, s32[32,32,128]{2,1,0:T(8,128)S(1)} %copy-done.1, f32[6,144,128]{2,1,0:T(8,128)S(1)} %get-tuple-element.47.field), custom_call_target="tpu_custom_call" | custom-call | flops 3000000 | bytes 1300000 | tf_op jit(solution)/shard_map/turn_solvent/pallas_call | solution.py:752
  42.8 0.0 collective-permute-done.4.odd
  42.8 0.0 collective-permute-done.5.even
  42.8 2.8 %substep.3 = (f32[24,128]{1,0:T(8,128)S(1)}, f32[16,128]{1,0:T(8,128)S(1)}) custom-call(f32[32,128]{1,0:T(8,128)S(1)} %get-tuple-element.45.row, f32[24,128]{1,0:T(8,128)S(1)} %get-tuple-element.46.moving, f32[32,128]{1,0:T(8,128)S(1)} %collective-permute-done.4.odd, f32[32,128]{1,0:T(8,128)S(1)} %collective-permute-done.5.even), custom_call_target="tpu_custom_call" | custom-call | flops 20000000 | bytes 100000 | tf_op jit(solution)/shard_map/substep/pallas_call | solution.py:642
  45.6 0.2 collective-permute-start.6
  45.8 3.3 %collective-permute-start.7 = (f32[24,128]{1,0:T(8,128)S(1)}, f32[24,128]{1,0:T(8,128)S(1)}, u32[]{:S(2)}, u32[]{:S(2)}) collective-permute-start(f32[24,128]{1,0:T(8,128)S(1)} %get-tuple-element.51.row), channel_id=1, source_target_pairs={{0,1},{1,0},{2,3},{3,2},{4,5},{5,4},{6,7},{7,6},{8,9},{9,8},{10,11... | collective-permute-start | bytes 36872 | tf_op jit(solution)/shard_map/ppermute | solution.py:57
  49.1 2.2 %turn_solvent.4.refs_0_ = f32[3,32,64,128]{3,2,1,0:T(8,128)} custom-call(s32[3]{0:T(128)S(1)} %copy-done.3, f32[3,32,64,128]{3,2,1,0:T(8,128)S(1)} %bitcast.13, s32[32,32,128]{2,1,0:T(8,128)S(1)} %copy-done.1, f32[6,144,128]{2,1,0:T(8,128)S(1)} %get-tuple-element.47.field, f32[3,32,64,128]{3,2,1,0:T(8,128)} %turn_solvent.3.refs_0_), custom_call_target="tpu_custom_call", output_to_operand_aliasing={{}: (4, {})} | custom-call | flops 3000000 | bytes 1300000 | tf_op jit(solution)/shard_map/turn_solvent/pallas_call | solution.py:752
  51.3 0.0 collective-permute-done.6.odd
  51.3 0.0 collective-permute-done.7.even
  51.3 1.8 %substep.4 = (f32[16,128]{1,0:T(8,128)S(1)}, f32[8,128]{1,0:T(8,128)S(1)}) custom-call(f32[24,128]{1,0:T(8,128)S(1)} %get-tuple-element.51.row, f32[16,128]{1,0:T(8,128)S(1)} %get-tuple-element.52.moving, f32[24,128]{1,0:T(8,128)S(1)} %collective-permute-done.6.odd, f32[24,128]{1,0:T(8,128)S(1)} %collective-permute-done.7.even), custom_call_target="tpu_custom_call" | custom-call | flops 12000000 | bytes 100000 | tf_op jit(solution)/shard_map/substep/pallas_call | solution.py:642
  53.1 0.1 collective-permute-start.8
  53.2 3.1 %collective-permute-start.9 = (f32[16,128]{1,0:T(8,128)S(1)}, f32[16,128]{1,0:T(8,128)S(1)}, u32[]{:S(2)}, u32[]{:S(2)}) collective-permute-start(f32[16,128]{1,0:T(8,128)S(1)} %get-tuple-element.57.row), channel_id=1, source_target_pairs={{0,1},{1,0},{2,3},{3,2},{4,5},{5,4},{6,7},{7,6},{8,9},{9,8},{10,11... | collective-permute-start | bytes 24584 | tf_op jit(solution)/shard_map/ppermute | solution.py:57
  56.4 2.3 %turn_solvent.5 = f32[3,32,64,128]{3,2,1,0:T(8,128)} custom-call(s32[3]{0:T(128)S(1)} %copy-done.3, f32[3,32,64,128]{3,2,1,0:T(8,128)S(1)} %bitcast.14, s32[32,32,128]{2,1,0:T(8,128)S(1)} %copy-done.1, f32[6,144,128]{2,1,0:T(8,128)S(1)} %get-tuple-element.47.field, f32[3,32,64,128]{3,2,1,0:T(8,128)} %turn_solvent.4.refs_0_), custom_call_target="tpu_custom_call", output_to_operand_aliasing={{}: (4, {})} | custom-call | flops 3000000 | bytes 1300000 | tf_op jit(solution)/shard_map/turn_solvent/pallas_call | solution.py:752
  58.6 0.0 collective-permute-done.8.odd
  58.7 0.0 collective-permute-done.9.even
  58.7 1.2 %substep.5 = (f32[3,1,128]{2,1,0:T(1,128)}, f32[3,1,128]{2,1,0:T(1,128)}) custom-call(f32[16,128]{1,0:T(8,128)S(1)} %get-tuple-element.57.row, f32[8,128]{1,0:T(8,128)S(1)} %get-tuple-element.60.moving, f32[16,128]{1,0:T(8,128)S(1)} %collective-permute-done.8.odd, f32[16,128]{1,0:T(8,128)S(1)} %collective-permute-done.9.even, ...), custom_call_target="tpu_custom_call" | custom-call | flops 4000000 | bytes 100000 | tf_op jit(solution)/shard_map/substep/pallas_call | solution.py:642
  (2 shorter events, 0.0 us)
Async XLA Ops:
  0.6 12.7 %copy-start.3 = (s32[3]{0:T(128)S(1)}, s32[3]{0:T(128)}, u32[]{:S(2)}) copy-start(s32[3]{0:T(128)} %shift.7) | copy-start | bytes 40
  0.6 12.7 %copy-start = (f32[3,32,32,2,128]{4,3,2,1,0:T(2,128)S(1)}, f32[3,32,32,2,128]{4,3,2,1,0:T(2,128)}, u32[]{:S(2)}) copy-start(f32[3,32,32,2,128]{4,3,2,1,0:T(2,128)} %param.8) | copy-start | bytes 9437188
  3.9 13.0 %collective-permute-start = (f32[32,128]{1,0:T(8,128)}, f32[32,128]{1,0:T(8,128)S(1)}, u32[]{:S(2)}, u32[]{:S(2)}) collective-permute-start(f32[32,128]{1,0:T(8,128)} %get-tuple-element.36), channel_id=1, source_target_pairs={{16,32},{32,16},{48,64},{64,48},{80,96},{96,80},{112,128},{128,112... | collective-permute-start | bytes 49160 | tf_op jit(solution)/shard_map/ppermute | solution.py:57
  13.3 3.6 %collective-permute-start.1 = (f32[32,128]{1,0:T(8,128)}, f32[32,128]{1,0:T(8,128)S(1)}, u32[]{:S(2)}, u32[]{:S(2)}) collective-permute-start(f32[32,128]{1,0:T(8,128)} %get-tuple-element.37), channel_id=1, source_target_pairs={{0,16},{16,0},{32,48},{48,32},{64,80},{80,64},{96,112},{112,96},{1... | collective-permute-start | bytes 49160 | tf_op jit(solution)/shard_map/ppermute | solution.py:57
  13.3 1.0 %copy-start.1 = (s32[32,32,128]{2,1,0:T(8,128)S(1)}, s32[32,32,128]{2,1,0:T(8,128)}, u32[]{:S(2)}) copy-start(s32[32,32,128]{2,1,0:T(8,128)} %occ.7) | copy-start | bytes 1572868
  14.4 0.9 %copy-start.2 = (f32[224,128]{1,0:T(8,128)S(1)}, f32[224,128]{1,0:T(8,128)}, u32[]{:S(2)}) copy-start(f32[224,128]{1,0:T(8,128)} %get-tuple-element.34.base) | copy-start | bytes 344068
  16.9 4.0 %collective-permute-start.2 = (f32[40,128]{1,0:T(8,128)S(1)}, f32[40,128]{1,0:T(8,128)S(1)}, u32[]{:S(2)}, u32[]{:S(2)}) collective-permute-start(f32[40,128]{1,0:T(8,128)S(1)} %get-tuple-element.40), channel_id=1, source_target_pairs={{1,2},{2,1},{3,4},{4,3},{5,6},{6,5},{7,8},{8,7},{9,10},{10,9},{11,... | collective-permute-start | bytes 61448 | tf_op jit(solution)/shard_map/ppermute | solution.py:57
  19.4 1.8 %collective-permute-start.3 = (f32[40,128]{1,0:T(8,128)S(1)}, f32[40,128]{1,0:T(8,128)S(1)}, u32[]{:S(2)}, u32[]{:S(2)}) collective-permute-start(f32[40,128]{1,0:T(8,128)S(1)} %get-tuple-element.41), channel_id=1, source_target_pairs={{0,1},{1,0},{2,3},{3,2},{4,5},{5,4},{6,7},{7,6},{8,9},{9,8},{10,11... | collective-permute-start | bytes 61448 | tf_op jit(solution)/shard_map/ppermute | solution.py:57
  35.9 6.9 %collective-permute-start.4 = (f32[32,128]{1,0:T(8,128)S(1)}, f32[32,128]{1,0:T(8,128)S(1)}, u32[]{:S(2)}, u32[]{:S(2)}) collective-permute-start(f32[32,128]{1,0:T(8,128)S(1)} %get-tuple-element.45.row), channel_id=1, source_target_pairs={{1,2},{2,1},{3,4},{4,3},{5,6},{6,5},{7,8},{8,7},{9,10},{10,9},{11,... | collective-permute-start | bytes 49160 | tf_op jit(solution)/shard_map/ppermute | solution.py:57
  39.3 3.5 %collective-permute-start.5 = (f32[32,128]{1,0:T(8,128)S(1)}, f32[32,128]{1,0:T(8,128)S(1)}, u32[]{:S(2)}, u32[]{:S(2)}) collective-permute-start(f32[32,128]{1,0:T(8,128)S(1)} %get-tuple-element.45.row), channel_id=1, source_target_pairs={{0,1},{1,0},{2,3},{3,2},{4,5},{5,4},{6,7},{7,6},{8,9},{9,8},{10,11... | collective-permute-start | bytes 49160 | tf_op jit(solution)/shard_map/ppermute | solution.py:57
  45.6 5.7 %collective-permute-start.6 = (f32[24,128]{1,0:T(8,128)S(1)}, f32[24,128]{1,0:T(8,128)S(1)}, u32[]{:S(2)}, u32[]{:S(2)}) collective-permute-start(f32[24,128]{1,0:T(8,128)S(1)} %get-tuple-element.51.row), channel_id=1, source_target_pairs={{1,2},{2,1},{3,4},{4,3},{5,6},{6,5},{7,8},{8,7},{9,10},{10,9},{11,... | collective-permute-start | bytes 36872 | tf_op jit(solution)/shard_map/ppermute | solution.py:57
  45.8 5.5 %collective-permute-start.7 = (f32[24,128]{1,0:T(8,128)S(1)}, f32[24,128]{1,0:T(8,128)S(1)}, u32[]{:S(2)}, u32[]{:S(2)}) collective-permute-start(f32[24,128]{1,0:T(8,128)S(1)} %get-tuple-element.51.row), channel_id=1, source_target_pairs={{0,1},{1,0},{2,3},{3,2},{4,5},{5,4},{6,7},{7,6},{8,9},{9,8},{10,11... | collective-permute-start | bytes 36872 | tf_op jit(solution)/shard_map/ppermute | solution.py:57
  53.1 5.5 %collective-permute-start.8 = (f32[16,128]{1,0:T(8,128)S(1)}, f32[16,128]{1,0:T(8,128)S(1)}, u32[]{:S(2)}, u32[]{:S(2)}) collective-permute-start(f32[16,128]{1,0:T(8,128)S(1)} %get-tuple-element.57.row), channel_id=1, source_target_pairs={{1,2},{2,1},{3,4},{4,3},{5,6},{6,5},{7,8},{8,7},{9,10},{10,9},{11,... | collective-permute-start | bytes 24584 | tf_op jit(solution)/shard_map/ppermute | solution.py:57
  53.2 5.4 %collective-permute-start.9 = (f32[16,128]{1,0:T(8,128)S(1)}, f32[16,128]{1,0:T(8,128)S(1)}, u32[]{:S(2)}, u32[]{:S(2)}) collective-permute-start(f32[16,128]{1,0:T(8,128)S(1)} %get-tuple-element.57.row), channel_id=1, source_target_pairs={{0,1},{1,0},{2,3},{3,2},{4,5},{5,4},{6,7},{7,6},{8,9},{9,8},{10,11... | collective-permute-start | bytes 24584 | tf_op jit(solution)/shard_map/ppermute | solution.py:57

commit v5 on v4

--- a/solution.py
+++ b/solution.py
@@ -65,7 +65,7 @@
     return jax.ShapeDtypeStruct(shape, jnp.float32)
 
 
-def exact_dot(left, right, dims, parts=3):
+def exact_dot(left, right, dims, parts=2):
     right = right.astype(jnp.bfloat16)
     total = None
     for part in range(parts):

time: 60.1 us -> 60.1 us (level)
  no operation moved by 1% of the time
where the time goes in v5:
time: 60.1 us
  starting transfers between devices  24.2 us (40%)
  Pallas kernels  17.6 us (29%)
  blocking collectives  13.8 us (23%)
  local copies, waits for them, and re-layouts  1.94 us (3%)
  between operations  1.6 us (3%)
  waiting for transfers between devices  0.86 us (1%)
    ppermute x10, starting transfers between devices, swapped(): return lax.ppermute(value, axis, pairs)  24.2 us
    all_to_all x1, blocking collectives, per_device(): packets = lax.all_to_all(packets, 'gx', 0, 0)  13.8 us
    pallas_call x3, Pallas kernels, turn_solvent(): pl.pallas_call(functools.partial(turn_kernel, ks), out_shape=struct(*v.sh...  6.62 us
    pallas_call x3, Pallas kernels, substep(): pl.pallas_call(kernel, out_shape=shapes, in_specs=[IN_VMEM] * len(operand...  6.09 us
    pallas_call x1, Pallas kernels, border_sums(): pl.pallas_call(border_kernel, out_shape=(struct(BASE, FZ), struct(32, FZ)...  2.41 us
    unnamed x8, local copies, waits for them, and re-layouts  1.94 us
    pallas_call x1, Pallas kernels, inner_sums(): pl.pallas_call(inner_kernel, out_shape=(struct(2 * ROWS, FZ), struct(16,...  1.53 us
  transfers between devices with their start and end apart: 10, of which 2 were waited for; matrix products, arithmetic and copies ran while one was open for 0% of the time, Pallas kernels for 14%

profile of v5, /device:TPU:1, one launch (start us, length us, event | category | flops | bytes accessed | tf_op | source)
XLA Modules:
  0.0 60.1 jit_solution(6064960046513595060)
XLA Ops:
  0.6 0.0 copy-start.3
  0.6 0.0 copy-start
  1.4 2.4 %border_sums.1 = (f32[224,128]{1,0:T(8,128)}, f32[32,128]{1,0:T(8,128)}, f32[32,128]{1,0:T(8,128)}) custom-call(s32[3]{0:T(128)} %shift.7, s32[1,1]{1,0:T(1,128)S(6)} %copy.17.count_at.count, f32[3,32,64,128]{3,2,1,0:T(8,128)} %bitcast.10, s32[32,32,128]{2,1,0:T(8,128)} %occ.7, s32[8,8,64]{2,1,0:T(8,128)} %axis_at.1, f32[3,1,128]{2,1,0:T(1,128)} %bitcast.16, ...), custom_call_target="tpu_custom_call" | custom-call | flops 1000000 | bytes 800000 | tf_op jit(solution)/shard_map/border_sums/pallas_call | solution.py:214
  3.9 9.4 %collective-permute-start = (f32[32,128]{1,0:T(8,128)}, f32[32,128]{1,0:T(8,128)S(1)}, u32[]{:S(2)}, u32[]{:S(2)}) collective-permute-start(f32[32,128]{1,0:T(8,128)} %get-tuple-element.36), channel_id=1, source_target_pairs={{16,32},{32,16},{48,64},{64,48},{80,96},{96,80},{112,128},{128,112... | collective-permute-start | bytes 49160 | tf_op jit(solution)/shard_map/ppermute | solution.py:57
  13.3 0.0 collective-permute-start.1
  13.3 0.0 copy-done.3
  13.3 0.0 copy-done
  13.3 0.0 copy-start.1
  13.3 1.0 %copy-done.1 = s32[32,32,128]{2,1,0:T(8,128)S(1)} copy-done((s32[32,32,128]{2,1,0:T(8,128)S(1)}, s32[32,32,128]{2,1,0:T(8,128)}, u32[]{:S(2)}) %copy-start.1) | copy-done | bytes 524312
  14.3 0.0 copy-start.2
  14.3 0.9 %copy-done.2 = f32[224,128]{1,0:T(8,128)S(1)} copy-done((f32[224,128]{1,0:T(8,128)S(1)}, f32[224,128]{1,0:T(8,128)}, u32[]{:S(2)}) %copy-start.2) | copy-done | bytes 114712
  15.2 1.5 %inner_sums.1 = (f32[288,128]{1,0:T(8,128)S(1)}, f32[16,128]{1,0:T(8,128)S(1)}, f32[144,128]{1,0:T(8,128)S(1)}) custom-call(s32[3]{0:T(128)S(1)} %copy-done.3, f32[3,32,64,128]{3,2,1,0:T(8,128)S(1)} %bitcast.11, s32[32,32,128]{2,1,0:T(8,128)S(1)} %copy-done.1, f32[224,128]{1,0:T(8,128)S(1)} %copy-done.2), custom_call_target="tpu_custom_call" | custom-call | flops 4000000 | bytes 3700000 | tf_op jit(solution)/shard_map/inner_sums/pallas_call | solution.py:267
  16.7 0.0 collective-permute-done.odd1
  16.8 0.0 collective-permute-done.1.even1
  16.8 2.6 %collective-permute-start.2 = (f32[40,128]{1,0:T(8,128)S(1)}, f32[40,128]{1,0:T(8,128)S(1)}, u32[]{:S(2)}, u32[]{:S(2)}) collective-permute-start(f32[40,128]{1,0:T(8,128)S(1)} %get-tuple-element.40), channel_id=1, source_target_pairs={{1,2},{2,1},{3,4},{4,3},{5,6},{6,5},{7,8},{8,7},{9,10},{10,9},{11,... | collective-permute-start | bytes 61448 | tf_op jit(solution)/shard_map/ppermute | solution.py:57
  19.4 0.8 %collective-permute-start.3 = (f32[40,128]{1,0:T(8,128)S(1)}, f32[40,128]{1,0:T(8,128)S(1)}, u32[]{:S(2)}, u32[]{:S(2)}) collective-permute-start(f32[40,128]{1,0:T(8,128)S(1)} %get-tuple-element.41), channel_id=1, source_target_pairs={{0,1},{1,0},{2,3},{3,2},{4,5},{5,4},{6,7},{7,6},{8,9},{9,8},{10,11... | collective-permute-start | bytes 61448 | tf_op jit(solution)/shard_map/ppermute | solution.py:57
  20.2 0.6 %collective-permute-done.2.odd2 = f32[40,128]{1,0:T(8,128)S(1)} collective-permute-done((f32[40,128]{1,0:T(8,128)S(1)}, f32[40,128]{1,0:T(8,128)S(1)}, u32[]{:S(2)}, u32[]{:S(2)}) %collective-permute-start.2) | collective-permute-done | bytes 20512 | tf_op jit(solution)/shard_map/ppermute | solution.py:57
  20.8 0.2 collective-permute-done.3.even2
  21.1 1.0 %cell_fields.1 = (f32[6,144,128]{2,1,0:T(8,128)S(1)}, f32[8,128]{1,0:T(8,128)S(1)}, f32[16,8,128]{2,1,0:T(8,128)S(1)}) custom-call(s32[1,1]{1,0:T(1,128)S(6)} %copy.17.count_at.count, f32[288,128]{1,0:T(8,128)S(1)} %get-tuple-element.35.part, f32[32,128]{1,0:T(8,128)S(1)} %collective-permute-done.odd1, f32[32,128]{1,0:T(8,128)S(1)} %collective-permute-done.1.even1, ...), custom_call_target="tpu_custom_call" | custom-call | flops 4000000 | bytes 1000000 | tf_op jit(solution)/shard_map/cell_fields/pallas_call | solution.py:542
  22.0 13.8 %all_to_all.5.packets = f32[16,8,128]{2,1,0:T(8,128)S(1)} all-to-all(f32[16,8,128]{2,1,0:T(8,128)S(1)} %get-tuple-element.42), channel_id=1, replica_groups=mesh['gx'=16,'yz'=16] {'gx'}, dimensions={0} | all-to-all | bytes 131072 | tf_op jit(solution)/shard_map/all_to_all | solution.py:792
  35.9 3.2 %collective-permute-start.4 = (f32[32,128]{1,0:T(8,128)S(1)}, f32[32,128]{1,0:T(8,128)S(1)}, u32[]{:S(2)}, u32[]{:S(2)}) collective-permute-start(f32[32,128]{1,0:T(8,128)S(1)} %get-tuple-element.45.row), channel_id=1, source_target_pairs={{1,2},{2,1},{3,4},{4,3},{5,6},{6,5},{7,8},{8,7},{9,10},{10,9},{11,... | collective-permute-start | bytes 49160 | tf_op jit(solution)/shard_map/ppermute | solution.py:57
  39.1 1.2 %collective-permute-start.5 = (f32[32,128]{1,0:T(8,128)S(1)}, f32[32,128]{1,0:T(8,128)S(1)}, u32[]{:S(2)}, u32[]{:S(2)}) collective-permute-start(f32[32,128]{1,0:T(8,128)S(1)} %get-tuple-element.45.row), channel_id=1, source_target_pairs={{0,1},{1,0},{2,3},{3,2},{4,5},{5,4},{6,7},{7,6},{8,9},{9,8},{10,11... | collective-permute-start | bytes 49160 | tf_op jit(solution)/shard_map/ppermute | solution.py:57
  40.3 2.2 %turn_solvent.3.refs_0_ = f32[3,32,64,128]{3,2,1,0:T(8,128)} custom-call(s32[3]{0:T(128)S(1)} %copy-done.3, f32[3,32,64,128]{3,2,1,0:T(8,128)S(1)} %bitcast.12, s32[32,32,128]{2,1,0:T(8,128)S(1)} %copy-done.1, f32[6,144,128]{2,1,0:T(8,128)S(1)} %get-tuple-element.47.field), custom_call_target="tpu_custom_call" | custom-call | flops 3000000 | bytes 1300000 | tf_op jit(solution)/shard_map/turn_solvent/pallas_call | solution.py:752
  42.4 0.0 collective-permute-done.4.odd
  42.5 0.0 collective-permute-done.5.even
  42.5 2.9 %substep.3 = (f32[24,128]{1,0:T(8,128)S(1)}, f32[16,128]{1,0:T(8,128)S(1)}) custom-call(f32[32,128]{1,0:T(8,128)S(1)} %get-tuple-element.45.row, f32[24,128]{1,0:T(8,128)S(1)} %get-tuple-element.46.moving, f32[32,128]{1,0:T(8,128)S(1)} %collective-permute-done.4.odd, f32[32,128]{1,0:T(8,128)S(1)} %collective-permute-done.5.even), custom_call_target="tpu_custom_call" | custom-call | flops 20000000 | bytes 100000 | tf_op jit(solution)/shard_map/substep/pallas_call | solution.py:642
  45.4 0.8 %collective-permute-start.6 = (f32[24,128]{1,0:T(8,128)S(1)}, f32[24,128]{1,0:T(8,128)S(1)}, u32[]{:S(2)}, u32[]{:S(2)}) collective-permute-start(f32[24,128]{1,0:T(8,128)S(1)} %get-tuple-element.51.row), channel_id=1, source_target_pairs={{1,2},{2,1},{3,4},{4,3},{5,6},{6,5},{7,8},{8,7},{9,10},{10,9},{11,... | collective-permute-start | bytes 36872 | tf_op jit(solution)/shard_map/ppermute | solution.py:57
  46.2 2.9 %collective-permute-start.7 = (f32[24,128]{1,0:T(8,128)S(1)}, f32[24,128]{1,0:T(8,128)S(1)}, u32[]{:S(2)}, u32[]{:S(2)}) collective-permute-start(f32[24,128]{1,0:T(8,128)S(1)} %get-tuple-element.51.row), channel_id=1, source_target_pairs={{0,1},{1,0},{2,3},{3,2},{4,5},{5,4},{6,7},{7,6},{8,9},{9,8},{10,11... | collective-permute-start | bytes 36872 | tf_op jit(solution)/shard_map/ppermute | solution.py:57
  49.1 2.2 %turn_solvent.4.refs_0_ = f32[3,32,64,128]{3,2,1,0:T(8,128)} custom-call(s32[3]{0:T(128)S(1)} %copy-done.3, f32[3,32,64,128]{3,2,1,0:T(8,128)S(1)} %bitcast.13, s32[32,32,128]{2,1,0:T(8,128)S(1)} %copy-done.1, f32[6,144,128]{2,1,0:T(8,128)S(1)} %get-tuple-element.47.field, f32[3,32,64,128]{3,2,1,0:T(8,128)} %turn_solvent.3.refs_0_), custom_call_target="tpu_custom_call", output_to_operand_aliasing={{}: (4, {})} | custom-call | flops 3000000 | bytes 1300000 | tf_op jit(solution)/shard_map/turn_solvent/pallas_call | solution.py:752
  51.3 0.0 collective-permute-done.6.odd
  51.3 0.0 collective-permute-done.7.even
  51.3 2.0 %substep.4 = (f32[16,128]{1,0:T(8,128)S(1)}, f32[8,128]{1,0:T(8,128)S(1)}) custom-call(f32[24,128]{1,0:T(8,128)S(1)} %get-tuple-element.51.row, f32[16,128]{1,0:T(8,128)S(1)} %get-tuple-element.52.moving, f32[24,128]{1,0:T(8,128)S(1)} %collective-permute-done.6.odd, f32[24,128]{1,0:T(8,128)S(1)} %collective-permute-done.7.even), custom_call_target="tpu_custom_call" | custom-call | flops 12000000 | bytes 100000 | tf_op jit(solution)/shard_map/substep/pallas_call | solution.py:642
  53.3 0.1 collective-permute-start.8
  53.4 3.2 %collective-permute-start.9 = (f32[16,128]{1,0:T(8,128)S(1)}, f32[16,128]{1,0:T(8,128)S(1)}, u32[]{:S(2)}, u32[]{:S(2)}) collective-permute-start(f32[16,128]{1,0:T(8,128)S(1)} %get-tuple-element.57.row), channel_id=1, source_target_pairs={{0,1},{1,0},{2,3},{3,2},{4,5},{5,4},{6,7},{7,6},{8,9},{9,8},{10,11... | collective-permute-start | bytes 24584 | tf_op jit(solution)/shard_map/ppermute | solution.py:57
  56.5 2.3 %turn_solvent.5 = f32[3,32,64,128]{3,2,1,0:T(8,128)} custom-call(s32[3]{0:T(128)S(1)} %copy-done.3, f32[3,32,64,128]{3,2,1,0:T(8,128)S(1)} %bitcast.14, s32[32,32,128]{2,1,0:T(8,128)S(1)} %copy-done.1, f32[6,144,128]{2,1,0:T(8,128)S(1)} %get-tuple-element.47.field, f32[3,32,64,128]{3,2,1,0:T(8,128)} %turn_solvent.4.refs_0_), custom_call_target="tpu_custom_call", output_to_operand_aliasing={{}: (4, {})} | custom-call | flops 3000000 | bytes 1300000 | tf_op jit(solution)/shard_map/turn_solvent/pallas_call | solution.py:752
  58.8 0.0 collective-permute-done.8.odd
  58.8 0.0 collective-permute-done.9.even
  58.8 1.2 %substep.5 = (f32[3,1,128]{2,1,0:T(1,128)}, f32[3,1,128]{2,1,0:T(1,128)}) custom-call(f32[16,128]{1,0:T(8,128)S(1)} %get-tuple-element.57.row, f32[8,128]{1,0:T(8,128)S(1)} %get-tuple-element.60.moving, f32[16,128]{1,0:T(8,128)S(1)} %collective-permute-done.8.odd, f32[16,128]{1,0:T(8,128)S(1)} %collective-permute-done.9.even, ...), custom_call_target="tpu_custom_call" | custom-call | flops 4000000 | bytes 100000 | tf_op jit(solution)/shard_map/substep/pallas_call | solution.py:642
  (2 shorter events, 0.0 us)
Async XLA Ops:
  0.6 12.6 %copy-start.3 = (s32[3]{0:T(128)S(1)}, s32[3]{0:T(128)}, u32[]{:S(2)}) copy-start(s32[3]{0:T(128)} %shift.7) | copy-start | bytes 40
  0.6 12.6 %copy-start = (f32[3,32,32,2,128]{4,3,2,1,0:T(2,128)S(1)}, f32[3,32,32,2,128]{4,3,2,1,0:T(2,128)}, u32[]{:S(2)}) copy-start(f32[3,32,32,2,128]{4,3,2,1,0:T(2,128)} %param.8) | copy-start | bytes 9437188
  3.9 12.9 %collective-permute-start = (f32[32,128]{1,0:T(8,128)}, f32[32,128]{1,0:T(8,128)S(1)}, u32[]{:S(2)}, u32[]{:S(2)}) collective-permute-start(f32[32,128]{1,0:T(8,128)} %get-tuple-element.36), channel_id=1, source_target_pairs={{16,32},{32,16},{48,64},{64,48},{80,96},{96,80},{112,128},{128,112... | collective-permute-start | bytes 49160 | tf_op jit(solution)/shard_map/ppermute | solution.py:57
  13.3 3.5 %collective-permute-start.1 = (f32[32,128]{1,0:T(8,128)}, f32[32,128]{1,0:T(8,128)S(1)}, u32[]{:S(2)}, u32[]{:S(2)}) collective-permute-start(f32[32,128]{1,0:T(8,128)} %get-tuple-element.37), channel_id=1, source_target_pairs={{0,16},{16,0},{32,48},{48,32},{64,80},{80,64},{96,112},{112,96},{1... | collective-permute-start | bytes 49160 | tf_op jit(solution)/shard_map/ppermute | solution.py:57
  13.3 1.0 %copy-start.1 = (s32[32,32,128]{2,1,0:T(8,128)S(1)}, s32[32,32,128]{2,1,0:T(8,128)}, u32[]{:S(2)}) copy-start(s32[32,32,128]{2,1,0:T(8,128)} %occ.7) | copy-start | bytes 1572868
  14.3 0.9 %copy-start.2 = (f32[224,128]{1,0:T(8,128)S(1)}, f32[224,128]{1,0:T(8,128)}, u32[]{:S(2)}) copy-start(f32[224,128]{1,0:T(8,128)} %get-tuple-element.34.base) | copy-start | bytes 344068
  16.8 4.0 %collective-permute-start.2 = (f32[40,128]{1,0:T(8,128)S(1)}, f32[40,128]{1,0:T(8,128)S(1)}, u32[]{:S(2)}, u32[]{:S(2)}) collective-permute-start(f32[40,128]{1,0:T(8,128)S(1)} %get-tuple-element.40), channel_id=1, source_target_pairs={{1,2},{2,1},{3,4},{4,3},{5,6},{6,5},{7,8},{8,7},{9,10},{10,9},{11,... | collective-permute-start | bytes 61448 | tf_op jit(solution)/shard_map/ppermute | solution.py:57
  19.4 1.7 %collective-permute-start.3 = (f32[40,128]{1,0:T(8,128)S(1)}, f32[40,128]{1,0:T(8,128)S(1)}, u32[]{:S(2)}, u32[]{:S(2)}) collective-permute-start(f32[40,128]{1,0:T(8,128)S(1)} %get-tuple-element.41), channel_id=1, source_target_pairs={{0,1},{1,0},{2,3},{3,2},{4,5},{5,4},{6,7},{7,6},{8,9},{9,8},{10,11... | collective-permute-start | bytes 61448 | tf_op jit(solution)/shard_map/ppermute | solution.py:57
  35.9 6.6 %collective-permute-start.4 = (f32[32,128]{1,0:T(8,128)S(1)}, f32[32,128]{1,0:T(8,128)S(1)}, u32[]{:S(2)}, u32[]{:S(2)}) collective-permute-start(f32[32,128]{1,0:T(8,128)S(1)} %get-tuple-element.45.row), channel_id=1, source_target_pairs={{1,2},{2,1},{3,4},{4,3},{5,6},{6,5},{7,8},{8,7},{9,10},{10,9},{11,... | collective-permute-start | bytes 49160 | tf_op jit(solution)/shard_map/ppermute | solution.py:57
  39.1 3.4 %collective-permute-start.5 = (f32[32,128]{1,0:T(8,128)S(1)}, f32[32,128]{1,0:T(8,128)S(1)}, u32[]{:S(2)}, u32[]{:S(2)}) collective-permute-start(f32[32,128]{1,0:T(8,128)S(1)} %get-tuple-element.45.row), channel_id=1, source_target_pairs={{0,1},{1,0},{2,3},{3,2},{4,5},{5,4},{6,7},{7,6},{8,9},{9,8},{10,11... | collective-permute-start | bytes 49160 | tf_op jit(solution)/shard_map/ppermute | solution.py:57
  45.4 5.9 %collective-permute-start.6 = (f32[24,128]{1,0:T(8,128)S(1)}, f32[24,128]{1,0:T(8,128)S(1)}, u32[]{:S(2)}, u32[]{:S(2)}) collective-permute-start(f32[24,128]{1,0:T(8,128)S(1)} %get-tuple-element.51.row), channel_id=1, source_target_pairs={{1,2},{2,1},{3,4},{4,3},{5,6},{6,5},{7,8},{8,7},{9,10},{10,9},{11,... | collective-permute-start | bytes 36872 | tf_op jit(solution)/shard_map/ppermute | solution.py:57
  46.2 5.1 %collective-permute-start.7 = (f32[24,128]{1,0:T(8,128)S(1)}, f32[24,128]{1,0:T(8,128)S(1)}, u32[]{:S(2)}, u32[]{:S(2)}) collective-permute-start(f32[24,128]{1,0:T(8,128)S(1)} %get-tuple-element.51.row), channel_id=1, source_target_pairs={{0,1},{1,0},{2,3},{3,2},{4,5},{5,4},{6,7},{7,6},{8,9},{9,8},{10,11... | collective-permute-start | bytes 36872 | tf_op jit(solution)/shard_map/ppermute | solution.py:57
  53.3 5.6 %collective-permute-start.8 = (f32[16,128]{1,0:T(8,128)S(1)}, f32[16,128]{1,0:T(8,128)S(1)}, u32[]{:S(2)}, u32[]{:S(2)}) collective-permute-start(f32[16,128]{1,0:T(8,128)S(1)} %get-tuple-element.57.row), channel_id=1, source_target_pairs={{1,2},{2,1},{3,4},{4,3},{5,6},{6,5},{7,8},{8,7},{9,10},{10,9},{11,... | collective-permute-start | bytes 24584 | tf_op jit(solution)/shard_map/ppermute | solution.py:57
  53.4 5.5 %collective-permute-start.9 = (f32[16,128]{1,0:T(8,128)S(1)}, f32[16,128]{1,0:T(8,128)S(1)}, u32[]{:S(2)}, u32[]{:S(2)}) collective-permute-start(f32[16,128]{1,0:T(8,128)S(1)} %get-tuple-element.57.row), channel_id=1, source_target_pairs={{0,1},{1,0},{2,3},{3,2},{4,5},{5,4},{6,7},{7,6},{8,9},{9,8},{10,11... | collective-permute-start | bytes 24584 | tf_op jit(solution)/shard_map/ppermute | solution.py:57
